TPU v7x, 128 devices: a whole 4x4x4 slice. The times are simulated.
128 devices in a mesh: row: 4 (over z_hi, core), col: 32 (over z_lo, x, y).
Axes of the slice: x: 4, y: 4, z: 4 (z_hi: 2, z_lo: 2; z = z_hi * 2 + z_lo), core: 2. Of those that a mesh axis runs over, the one named last changes fastest.
Arguments:
- tokens: bfloat16 [512, 12288], P('col', 'row'), may hold values from -6 to 6
- cotangent: bfloat16 [512, 12288], P('col', 'row'), may hold values from -6 to 6
- gate_weight: bfloat16 [12288, 24576], P('row', 'col'), may hold values from -0.109375 to 0.109375
- up_weight: bfloat16 [12288, 24576], P('row', 'col'), may hold values from -0.109375 to 0.109375
- down_weight: bfloat16 [24576, 12288], P('col', 'row'), may hold values from -0.078125 to 0.078125
- kept: int32 [3, 96, 192], P(None, 'row', 'col'), may hold values from 0 to 1, as said below
- regrown: int32 [3, 96, 192], P(None, 'row', 'col'), may hold values from 0 to 1, as said below
Outputs:
- output: bfloat16 [512, 12288], P('col', 'row')
- input_grad: bfloat16 [512, 12288], P('col', 'row')
- grad_blocks: bfloat16 [3, 4, 32, 36, 128, 128], P(None, 'row', 'col')
Inputs may be any that keep to these rules, and one draw needn't show every extreme that they name: kept and regrown never both 1. Within each grid row and weight exactly 1152 blocks are active; each tile of 24 x 6 blocks holds between 18 and 72 active blocks, and one tile of every grid row and weight holds exactly 72. `regrown`: same layout as kept.
All inputs are finite; a program needn't handle non-finite values.
Results may differ from a plain program's by a relative error of at most 0.0049.
Values may be sent and summed in bfloat16 or wider, within the bound.
No kernel may reach another device: no remote copies, remote signals or barrier semaphores. Data moves between devices by JAX's collectives and lax.ppermute only.
A program may use at most 128 MiB of HBM per device.

v0:
```python
import jax
import jax.numpy as jnp
from jax import lax
from jax.sharding import PartitionSpec as P

BLOCK = 128


def mask_rows(weight, keep):
    rows, cols = keep.shape
    shaped = weight.reshape(rows, BLOCK, cols, BLOCK) * keep[:, None, :, None]
    return shaped.reshape(weight.shape)


def contract_first(left, right):
    return lax.dot_general(
        left, right, (((0,), (0,)), ((), ())), preferred_element_type=jnp.float32
    )


def contract_last(left, right):
    return lax.dot_general(
        left, right, (((1,), (1,)), ((), ())), preferred_element_type=jnp.float32
    )


def pack_sends(tiles, active, count, offset, ncol, cap):
    flat_active = active.reshape(-1)
    places = jnp.argsort(1 - flat_active, stable=True)
    owners = jnp.arange(ncol, dtype=jnp.int32)[:, None]
    slots = jnp.arange(cap, dtype=jnp.int32)[None, :]
    local = (owners - offset) % ncol + slots * ncol
    valid = local < count
    taken = places[jnp.minimum(local, flat_active.shape[0] - 1)]
    blocks = tiles[taken]
    return jnp.where(valid[:, :, None, None], blocks, jnp.zeros_like(blocks))


def unpack_blocks(received, offsets, place, ncol, cap, own):
    wanted = jnp.arange(own, dtype=jnp.int32) * ncol + place
    source = jnp.sum((offsets[None, :] <= wanted[:, None]).astype(jnp.int32), axis=1) - 1
    start = offsets[source]
    slot = (wanted - start - (place - start) % ncol) // ncol
    flat = received.reshape(received.shape[0] * received.shape[1], BLOCK, BLOCK)
    return flat[source * cap + slot]


def shards(tokens, cotangent, gate_weight, up_weight, down_weight, kept, regrown):
    keep = kept.astype(jnp.bfloat16)
    feat_rows, hid_cols = gate_weight.shape
    brows, bcols = (kept.shape[1], kept.shape[2])
    ncol = lax.axis_size("col")
    place = lax.axis_index("col")
    own = brows * bcols // 4
    cap = (2 * own + ncol - 1) // ncol
    wg = mask_rows(gate_weight, keep[0])
    wu = mask_rows(up_weight, keep[1])
    wd = mask_rows(down_weight, keep[2].T)
    active = kept + regrown
    counts = jnp.sum(active, axis=(1, 2))
    all_counts = lax.all_gather(counts[None, :], "col", axis=0, tiled=True)
    offsets = jnp.cumsum(all_counts, axis=0) - all_counts
    own_offset = lax.dynamic_index_in_dim(offsets, place, 0, keepdims=False)

    def sends_for(grad, which, down):
        if down:
            tiles = grad.reshape(bcols, BLOCK, brows, BLOCK).transpose(2, 0, 1, 3)
        else:
            tiles = grad.reshape(brows, BLOCK, bcols, BLOCK).transpose(0, 2, 1, 3)
        tiles = tiles.reshape(brows * bcols, BLOCK, BLOCK)
        return pack_sends(tiles, active[which], counts[which], own_offset[which], ncol, cap)

    x_all = lax.all_gather(tokens, "col", axis=0, tiled=True)
    both_weights = jnp.concatenate([wg, wu], axis=1)
    sums = lax.psum(jnp.dot(x_all, both_weights, preferred_element_type=jnp.float32), "row")
    gate = sums[:, :hid_cols]
    up = sums[:, hid_cols:]
    sig = jax.nn.sigmoid(gate)
    act = gate * sig
    hidden = (act * up).astype(jnp.bfloat16)
    dy_all = lax.all_gather(cotangent, "col", axis=0, tiled=True)
    factor = float(x_all.shape[0]) ** (-0.5)
    grad_d = (contract_first(hidden, dy_all) * factor).astype(jnp.bfloat16)
    send_down = sends_for(grad_d, 2, True)
    hidden_grad = lax.psum(contract_last(dy_all, wd), "row")
    gate_grad = (hidden_grad * up * sig * (1.0 + gate * (1.0 - sig))).astype(jnp.bfloat16)
    up_grad = (hidden_grad * act).astype(jnp.bfloat16)
    output = lax.psum_scatter(
        jnp.dot(hidden, wd, preferred_element_type=jnp.float32),
        "col",
        scatter_dimension=0,
        tiled=True,
    ).astype(jnp.bfloat16)
    input_grad = lax.psum_scatter(
        contract_last(gate_grad, wg) + contract_last(up_grad, wu),
        "col",
        scatter_dimension=0,
        tiled=True,
    ).astype(jnp.bfloat16)
    grad_g = (contract_first(x_all, gate_grad) * factor).astype(jnp.bfloat16)
    grad_u = (contract_first(x_all, up_grad) * factor).astype(jnp.bfloat16)
    send_gate = sends_for(grad_g, 0, False)
    send_up = sends_for(grad_u, 1, False)
    received = lax.all_to_all(
        jnp.stack([send_gate, send_up, send_down], 0),
        "col",
        split_axis=1,
        concat_axis=1,
        tiled=True,
    )
    placed = []
    for which in range(3):
        placed.append(unpack_blocks(received[which], offsets[:, which], place, ncol, cap, own))
    grad_blocks = jnp.stack(placed, 0)[:, None, None]
    return (output, input_grad, grad_blocks)


def solution(mesh):
    return jax.shard_map(
        shards,
        mesh=mesh,
        in_specs=(
            P("col", "row"),
            P("col", "row"),
            P("row", "col"),
            P("row", "col"),
            P("col", "row"),
            P(None, "row", "col"),
            P(None, "row", "col"),
        ),
        out_specs=(P("col", "row"), P("col", "row"), P(None, "row", "col", None, None, None)),
        check_vma=False,
    )
```

profile of v0, /device:TPU:2, one launch (start us, length us, event | category | flops | bytes accessed | tf_op | source)
XLA Modules:
  0.0 904.5 jit_solution(14224534508136946750)
XLA Ops:
  8.7 6.6 copy.43
  15.3 6.8 copy.42
  25.9 4.4 bitcast_multiply_fusion.1
  30.4 131.5 %all-gather.4.cloned.1.call-done = bf16[512,3072]{1,0:T(8,128)(2,1)} async-done(((bf16[16,3072]{1,0:T(8,128)(2,1)}), bf16[512,3072]{1,0:T(8,128)(2,1)}) %all-gather.4.cloned.1.call-update) | async-done | bytes 3145744 | tf_op jit(solution)/shard_map/all_gather | solution.py:73
  161.8 11.4 %fusion.4 = f32[512,1536]{0,1:T(8,128)} fusion(bf16[512,3072]{1,0:T(8,128)(2,1)} %all-gather.4.cloned.1.call-done, bf16[3072,768]{0,1:T(8,128)(2,1)} %get-tuple-element.44, bf16[3072,768]{0,1:T(8,128)(2,1)} %get-tuple-element.45), kind=kOutput, calls=%fused_computation.25 | convolution fusion | flops 4850712576 | bytes 15728640 | tf_op jit(solution)/shard_map/dot_general | solution.py:75
  173.3 145.8 %all-gather.6.cloned.1.call-done = bf16[512,3072]{1,0:T(8,128)(2,1)} async-done(((bf16[16,3072]{1,0:T(8,128)(2,1)}), bf16[512,3072]{1,0:T(8,128)(2,1)}) %all-gather.6.cloned.1.call-update) | async-done | bytes 3145744 | tf_op jit(solution)/shard_map/all_gather | solution.py:81
  322.0 6.2 convolution_bitcast_fusion
  328.5 107.4 %all-reduce.4.cloned.1.call-done = (f32[512,1536]{0,1:T(8,128)}, f32[512,768]{0,1:T(8,128)}) async-done(((f32[512,1536]{0,1:T(8,128)}, f32[512,768]{0,1:T(8,128)}), (f32[512,1536]{0,1:T(8,128)}, f32[512,768]{0,1:T(8,128)})) %all-reduce.4.cloned.1.call-update) | async-done | bytes 4718608 | tf_op jit(solution)/shard_map/psum | solution.py:75
  439.7 6.9 fusion.11
  448.7 17.3 %all-reduce = s32[96]{0:T(128)S(1)} all-reduce(s32[96]{0:T(128)S(1)} %dynamic-update-slice), channel_id=2, replica_groups=mesh['row'=4,'col'=32] {'col'}, use_global_device_ids=true, to_apply=%add | all-reduce | flops 96 | bytes 768
  486.6 4.6 fusion.35
  491.2 7.2 convolution_add_fusion
  498.5 5.2 fusion.9
  515.0 7.0 copy.49
  522.0 5.0 fusion.7
  530.5 7.0 copy.45
  537.5 5.1 gather_fusion.5
  542.6 5.1 gather_fusion.3
  547.6 5.0 gather_fusion.1
  559.4 7.0 pad_maximum_fusion
  566.4 6.2 all-to-all-start
  575.4 136.0 %all-to-all-done = bf16[3,32,3,128,128]{4,3,2,0,1:T(8,128)(2,1)} async-done(((bf16[3,32,3,128,128]{4,3,2,0,1:T(8,128)(2,1)}), bf16[3,32,3,128,128]{4,3,2,0,1:T(8,128)(2,1)}, u32[]{:S(2)}, u32[]{:S(2)}) %all-to-all-start) | async-done | bytes 9437216 | tf_op jit(solution)/shard_map/all_to_all | solution.py:104
  711.4 7.2 fusion.32
  732.9 163.5 %reduce-scatter.5.cloned.1.call-done = f32[16,3072]{1,0:T(8,128)} async-done(((f32[512,3072]{1,0:T(8,128)}), f32[16,3072]{1,0:T(8,128)}) %reduce-scatter.5.cloned.1.call-update) | async-done | bytes 196624 | tf_op jit(solution)/shard_map/reduce_scatter | solution.py:94
  (124 shorter events, 74.1 us)
Async XLA Ops:
  7.2 154.7 %all-gather.4.cloned.1.call-start = ((), (), s32[]{:S(2)}) async-start(), calls=%async_computation.3 | async-start | bytes 3244032 | tf_op jit(solution)/shard_map/all_gather | solution.py:73
  7.9 311.2 %all-gather.6.cloned.1.call-start = ((), (), s32[]{:S(2)}) async-start(), calls=%async_computation.5 | async-start | bytes 3244032 | tf_op jit(solution)/shard_map/all_gather | solution.py:81
  8.6 427.3 %all-reduce.4.cloned.1.call-start = ((), (), s32[]{:S(2)}) async-start(), calls=%async_computation.7 | async-start | bytes 9437184 | tf_op jit(solution)/shard_map/psum | solution.py:75
  15.3 6.8 copy-start.5
  15.3 6.8 copy-start.6
  15.3 8.3 slice-start
  22.1 2.2 slice-start.1
  23.0 3.0 copy-start
  319.1 2.9 copy-start.8
  319.8 2.2 copy-start.3
  328.3 403.0 %reduce-scatter.3.cloned.1.call-start = ((), (), s32[]{:S(2)}) async-start(), calls=%async_computation.4 | async-start | bytes 6488064 | tf_op jit(solution)/shard_map/reduce_scatter | solution.py:88
  435.9 3.8 copy-start.4
  446.6 0.7 copy-start.9
  446.6 449.8 %reduce-scatter.5.cloned.1.call-start = ((), (), s32[]{:S(2)}) async-start(), calls=%async_computation.6 | async-start | bytes 6488064 | tf_op jit(solution)/shard_map/reduce_scatter | solution.py:94
  498.5 5.2 copy-start.7
  552.7 2.9 copy-start.1
  555.0 2.5 copy-start.2
  566.4 145.0 %all-to-all-start = ((bf16[3,32,3,128,128]{4,3,2,0,1:T(8,128)(2,1)}), bf16[3,32,3,128,128]{4,3,2,0,1:T(8,128)(2,1)}, u32[]{:S(2)}, u32[]{:S(2)}) async-start(bf16[3,32,3,128,128]{4,3,2,0,1:T(8,128)(2,1)} %pad_maximum_fusion), calls=%async_computation.2 | async-start | bytes 18874368 | tf_op jit(solution)/shard_map/all_to_all | solution.py:104
Sparse Core Ops, SparseCore 0:
  9.6 152.1 all-gather.3
  163.5 155.5 all-gather.5
  328.4 107.4 all-reduce.3
  446.7 267.5 reduce-scatter.2
  716.6 179.7 reduce-scatter.4
where the time goes:
time: 914 us; the launch traced here: 905 us
  waiting for transfers between devices  686 us (75%)
  local copies, waits for them, and re-layouts  88.8 us (10%)
  matrix products  49.4 us (5%)
  other arithmetic  41.7 us (5%)
  blocking collectives  17.3 us (2%)
  between operations  14.9 us (2%)
    reduce_scatter x1, waiting for transfers between devices, shards(): lax.psum_scatter(contract_last(gate_grad, wg) + contract_last(up_grad, wu...  164 us
    all_gather x1, waiting for transfers between devices, shards(): dy_all = lax.all_gather(cotangent, 'col', axis=0, tiled=True)  146 us
    all_to_all x1, waiting for transfers between devices, shards(): lax.all_to_all(jnp.stack([send_gate, send_up, send_down], 0), 'col', spli...  136 us
    all_gather x1, waiting for transfers between devices, shards(): x_all = lax.all_gather(tokens, 'col', axis=0, tiled=True)  131 us
    psum x1, waiting for transfers between devices, shards(): lax.psum(jnp.dot(x_all, both_weights, preferred_element_type=jnp.float32)...  107 us
    unnamed x32, local copies, waits for them, and re-layouts  28.4 us
  transfers between devices with their start and end apart: 6, of which 5 were waited for; matrix products, arithmetic and copies ran while one was open for 17% of the time, Pallas kernels for 0%

commit v1 on v0

v1 whole, which is shorter than its diff:
```python
import jax
import jax.numpy as jnp
from jax import lax
from jax.experimental import pallas as pl
from jax.experimental.pallas import tpu as pltpu
from jax.sharding import PartitionSpec as P

BLOCK = 128
MAIN = 7
EXTRA = 2
LANES = 128
BF = jnp.bfloat16
F32 = jnp.float32


def mask_rows(weight, keep):
    rows, cols = keep.shape
    shaped = weight.reshape(rows, BLOCK, cols, BLOCK) * keep[:, None, :, None]
    return shaped.reshape(weight.shape)


def contract_last(left, right):
    return lax.dot_general(left, right, (((1,), (1,)), ((), ())), preferred_element_type=F32)


def gather_rows(part, ncol):
    copies = jnp.broadcast_to(part[None], (ncol,) + part.shape).reshape(ncol * part.shape[0], part.shape[1])
    return lax.all_to_all(copies, "col", 0, 0, tiled=True)


def scatter_sum(partial, ncol):
    rows = partial.shape[0] // ncol
    got = lax.all_to_all(partial.astype(BF), "col", 0, 0, tiled=True)
    return jnp.sum(got.reshape(ncol, rows, -1).astype(F32), axis=0).astype(BF)


def row_sum(value, core):
    half = value.shape[0] // 2
    keep = lax.dynamic_slice_in_dim(value, core * half, half, 0)
    send = lax.dynamic_slice_in_dim(value, (1 - core) * half, half, 0)
    pair = [(0, 1), (1, 0), (2, 3), (3, 2)]
    far = [(0, 2), (1, 3), (2, 0), (3, 1)]
    mine = keep + lax.ppermute(send, "row", pair)
    mine = mine + lax.ppermute(mine.astype(BF), "row", far).astype(F32)
    other = lax.ppermute(mine, "row", pair)
    first = jnp.where(core == 0, mine, other)
    second = jnp.where(core == 0, other, mine)
    return jnp.concatenate([first, second], axis=0)


def dot_rows(left, right):
    return lax.dot_general(left, right, (((0,), (0,)), ((), ())), preferred_element_type=F32)


def pack_kernel(factor, brows, bcols, group, where_ref, x_ref, gg_ref, ug_ref, hid_ref, dy_ref, main_ref, extra_ref):
    cut = main_ref.shape[0]
    wide = group * BLOCK

    def store(which, d, f, block):
        at = where_ref[which * brows * bcols + d * bcols + f]

        @pl.when((at >= 0) & (at < cut))
        def _():
            main_ref[at] = block

        @pl.when(at >= cut)
        def _():
            extra_ref[at - cut] = block

    def step(i, carry):
        lanes = pl.ds(pl.multiple_of(i * wide, wide), wide)
        x = x_ref[:, lanes]
        dy = dy_ref[:, lanes]
        for which, grad_ref in ((0, gg_ref), (1, ug_ref)):
            tile = (dot_rows(x, grad_ref[...]) * factor).astype(BF)
            for u in range(group):
                for f in range(bcols):
                    store(which, i * group + u, f, tile[u * BLOCK:(u + 1) * BLOCK, f * BLOCK:(f + 1) * BLOCK])
        tile = (dot_rows(hid_ref[...], dy) * factor).astype(BF)
        for u in range(group):
            for f in range(bcols):
                store(2, i * group + u, f, tile[f * BLOCK:(f + 1) * BLOCK, u * BLOCK:(u + 1) * BLOCK])
        return carry

    lax.fori_loop(0, brows // group, step, 0)


def pack_grads(where, x_all, gate_grad, up_grad, hidden, dy_all, factor, brows, bcols, ncol):
    import functools

    vmem = pl.BlockSpec(memory_space=pltpu.VMEM)
    tokens = x_all.shape[0]
    feat = brows * BLOCK
    return pl.pallas_call(
        functools.partial(pack_kernel, factor, brows, bcols, 4),
        out_shape=(
            jax.ShapeDtypeStruct((ncol * MAIN, BLOCK, BLOCK), BF),
            jax.ShapeDtypeStruct((ncol * EXTRA, BLOCK, BLOCK), BF),
        ),
        in_specs=[pl.BlockSpec(memory_space=pltpu.SMEM)] + [vmem] * 5,
        out_specs=(vmem, vmem),
        compiler_params=pltpu.CompilerParams(vmem_limit_bytes=48 * 2**20),
        cost_estimate=pl.CostEstimate(flops=6 * tokens * feat * bcols * BLOCK, bytes_accessed=16 * 2**20, transcendentals=0),
    )(where, x_all, gate_grad, up_grad, hidden, dy_all)


def pick_kernel(count, from_ref, got_ref, out_ref):
    def step(i, carry):
        out_ref[i] = got_ref[from_ref[i]]
        return carry

    lax.fori_loop(0, count, step, 0, unroll=4)


def pick_blocks(source, got):
    import functools

    vmem = pl.BlockSpec(memory_space=pltpu.VMEM)
    count = source.shape[0]
    return pl.pallas_call(
        functools.partial(pick_kernel, count),
        out_shape=jax.ShapeDtypeStruct((count, BLOCK, BLOCK), BF),
        in_specs=[pl.BlockSpec(memory_space=pltpu.SMEM), vmem],
        out_specs=vmem,
        compiler_params=pltpu.CompilerParams(vmem_limit_bytes=32 * 2**20),
        cost_estimate=pl.CostEstimate(flops=0, bytes_accessed=12 * 2**20, transcendentals=0),
    )(source, got)


def pair_counts(counts, offsets, ncol):
    owners = jnp.arange(ncol, dtype=jnp.int32)
    first = (owners[None, None, :] - offsets[:, :, None]) % ncol
    return (counts[:, :, None] - first + ncol - 1) // ncol


def send_places(active, counts, offsets, pairs, place, ncol):
    flat = active.reshape(3, -1)
    local = jnp.cumsum(flat, axis=1) - 1
    mine = offsets[:, place][:, None]
    owner = (mine + local) % ncol
    ahead = jnp.cumsum(pairs, axis=0) - pairs
    ahead = ahead[:, place]
    before = jnp.sum(jnp.where(owner[:, :, None] == jnp.arange(ncol)[None, None, :], ahead[:, None, :], 0), axis=2)
    slot = before + local // ncol
    at = jnp.where(slot < MAIN, owner * MAIN + slot, ncol * MAIN + owner * EXTRA + slot - MAIN)
    return jnp.where(flat > 0, at, -1).reshape(-1).astype(jnp.int32)


def pick_places(offsets, pairs, place, own, ncol):
    wanted = jnp.arange(own, dtype=jnp.int32)[None, :] * ncol + place
    source = jnp.sum((offsets[:, None, :] <= wanted[:, :, None]).astype(jnp.int32), axis=2) - 1
    ahead = (jnp.cumsum(pairs, axis=0) - pairs)[:, :, place]
    here = source[:, :, None] == jnp.arange(ncol)[None, None, :]
    start = jnp.sum(jnp.where(here, offsets[:, None, :], 0), axis=2)
    before = jnp.sum(jnp.where(here, ahead[:, None, :], 0), axis=2)
    slot = before + (wanted - start) // ncol
    at = jnp.where(slot < MAIN, source * MAIN + slot, ncol * MAIN + source * EXTRA + slot - MAIN)
    return at.reshape(-1).astype(jnp.int32)


def shards(tokens, cotangent, gate_weight, up_weight, down_weight, kept, regrown):
    keep = kept.astype(BF)
    feat, hid = gate_weight.shape
    brows, bcols = kept.shape[1], kept.shape[2]
    ncol = lax.axis_size("col")
    place = lax.axis_index("col")
    core = lax.axis_index("row") % 2
    own = brows * bcols // 4
    active = kept + regrown
    tally = jnp.sum(active, axis=(1, 2)).astype(BF)
    note = jnp.zeros((tokens.shape[0], LANES), BF).at[0, :3].set(tally)
    x_wide = gather_rows(jnp.concatenate([tokens, note], axis=1), ncol)
    dy_all = gather_rows(cotangent, ncol)
    both = jnp.concatenate([mask_rows(gate_weight, keep[0]), mask_rows(up_weight, keep[1])], axis=1)
    wd = mask_rows(down_weight, keep[2].T)
    x_all = x_wide[:, :feat]
    counts = x_wide.reshape(ncol, -1, feat + LANES)[:, 0, feat:feat + 3].astype(jnp.int32).T
    offsets = jnp.cumsum(counts, axis=1) - counts
    pairs = pair_counts(counts, offsets, ncol)
    need = jnp.max(jnp.sum(pairs, axis=0))
    need = jnp.maximum(need, lax.ppermute(need, "row", [(0, 1), (1, 0), (2, 3), (3, 2)]))
    need = jnp.maximum(need, lax.ppermute(need, "row", [(0, 2), (1, 3), (2, 0), (3, 1)]))
    send_at = send_places(active, counts, offsets, pairs, place, ncol)
    pick_at = pick_places(offsets, pairs, place, own, ncol)

    sums = row_sum(jnp.dot(x_all, both, preferred_element_type=F32), core)
    gate, up = sums[:, :hid], sums[:, hid:]
    sig = jax.nn.sigmoid(gate)
    act = gate * sig
    hidden = (act * up).astype(BF)
    output = scatter_sum(jnp.dot(hidden, wd, preferred_element_type=F32), ncol)
    hidden_grad = row_sum(contract_last(dy_all, wd), core)
    gate_grad = (hidden_grad * up * sig * (1.0 + gate * (1.0 - sig))).astype(BF)
    up_grad = (hidden_grad * act).astype(BF)
    factor = float(x_all.shape[0]) ** (-0.5)
    main, extra = pack_grads(send_at, x_all, gate_grad, up_grad, hidden, dy_all, factor, brows, bcols, ncol)
    got = lax.all_to_all(main, "col", 0, 0, tiled=True)
    input_grad = scatter_sum(contract_last(jnp.concatenate([gate_grad, up_grad], axis=1), both), ncol)

    def with_extra():
        more = lax.all_to_all(extra, "col", 0, 0, tiled=True)
        return pick_blocks(pick_at, jnp.concatenate([got, more], axis=0))

    def without():
        return pick_blocks(pick_at, got)

    grad_blocks = lax.cond(need > MAIN, with_extra, without)
    return (output, input_grad, grad_blocks.reshape(3, 1, 1, own, BLOCK, BLOCK))


def solution(mesh):
    return jax.shard_map(
        shards,
        mesh=mesh,
        in_specs=(
            P("col", "row"),
            P("col", "row"),
            P("row", "col"),
            P("row", "col"),
            P("col", "row"),
            P(None, "row", "col"),
            P(None, "row", "col"),
        ),
        out_specs=(P("col", "row"), P("col", "row"), P(None, "row", "col", None, None, None)),
        check_vma=False,
    )
```

time: 914 us -> 364 us (0.40)
  waiting for transfers between devices: 686 us -> 163 us
  starting transfers between devices: 6.61 us -> 80.9 us
  local copies, waits for them, and re-layouts: 88.8 us -> 36.1 us
  Pallas kernels: 0 us -> 27.5 us
  matrix products: 49.4 us -> 29.6 us
  other arithmetic: 41.7 us -> 23 us
  blocking collectives: 17.3 us -> 0 us
  between operations: 14.9 us -> 2.96 us
    all_gather x2 -> x0, waiting for transfers between devices: 277 us -> none  [the longest x1 146 us: shards(): dy_all = lax.all_gather(cotangent, 'col', axis=0, tiled=True)]
    reduce_scatter x2 -> x0, waiting for transfers between devices: 164 us -> none  [the longest x1 164 us: shards(): lax.psum_scatter(contract_last(gate_grad, wg) + contract_last(up_grad, wu...]
    psum x1 -> x0, waiting for transfers between devices: 107 us -> none  [shards(): lax.psum(jnp.dot(x_all, both_weights, preferred_element_type=jnp.float32)...]
    ppermute x0 -> x8, starting transfers between devices: none -> 47.8 us  [the longest x1 43.1 us: shards(): lax.ppermute(need, 'row', [(0, 2), (1, 3), (2, 0), (3, 1)])]
    gather x15 -> x0, local copies, waits for them, and re-layouts: 30.9 us -> none  [the longest x3 15.2 us: pack_sends(): blocks = tiles[taken]]
    ppermute x0 -> x8, waiting for transfers between devices: none -> 29.4 us  [the longest x2 22.9 us: row_sum(): mine = mine + lax.ppermute(mine.astype(BF), 'row', far).astype(F32)]
    pallas_call x0 -> x2, Pallas kernels: none -> 27.5 us  [the longest x1 24 us: pack_grads(): pl.pallas_call(functools.partial(pack_kernel, factor, brows, bcols, 4), o...]
    all_to_all x1 -> x5, starting transfers between devices: 6.23 us -> 33.1 us  [the longest x2 14.3 us: gather_rows(): return lax.all_to_all(copies, 'col', 0, 0, tiled=True)]
  transfers between devices with their start and end apart: 6 -> 13, of which waited for: 5 -> 10; matrix products, arithmetic and copies ran while one was open for 17% -> 18% of each run, Pallas kernels for 0% -> 7%
where the time goes in v1:
time: 364 us; the launch traced here: 363 us
  waiting for transfers between devices  163 us (45%)
  starting transfers between devices  80.9 us (22%)
  local copies, waits for them, and re-layouts  36.1 us (10%)
  matrix products  29.6 us (8%)
  Pallas kernels  27.5 us (8%)
  other arithmetic  23 us (6%)
    all_to_all x2, waiting for transfers between devices, gather_rows(): return lax.all_to_all(copies, 'col', 0, 0, tiled=True)  49.2 us
    all_to_all x1, waiting for transfers between devices, shards(): got = lax.all_to_all(main, 'col', 0, 0, tiled=True)  44.1 us
    ppermute x1, starting transfers between devices, shards(): lax.ppermute(need, 'row', [(0, 2), (1, 3), (2, 0), (3, 1)])  43.1 us
    all_to_all x2, waiting for transfers between devices, scatter_sum(): got = lax.all_to_all(partial.astype(BF), 'col', 0, 0, tiled=True)  40.4 us
    unnamed x41, local copies, waits for them, and re-layouts  24.4 us
    pallas_call x1, Pallas kernels, pack_grads(): pl.pallas_call(functools.partial(pack_kernel, factor, brows, bcols, 4), o...  24 us
    ppermute x2, waiting for transfers between devices, row_sum(): mine = mine + lax.ppermute(mine.astype(BF), 'row', far).astype(F32)  22.9 us
    dot_general x2, matrix products, contract_last(): lax.dot_general(left, right, (((1,), (1,)), ((), ())), preferred_element_...  16.5 us
  transfers between devices with their start and end apart: 13, of which 10 were waited for; matrix products, arithmetic and copies ran while one was open for 18% of the time, Pallas kernels for 7%

profile of v1, /device:TPU:2, one launch (start us, length us, event | category | flops | bytes accessed | tf_op | source)
XLA Modules:
  0.0 363.2 jit_solution(6043813883550278441)
XLA Ops:
  4.4 9.0 %all-to-all-start.1 = ((bf16[32,16,3200]{2,1,0:T(8,128)(2,1)}), bf16[32,16,3200]{2,1,0:T(8,128)(2,1)S(1)}, u32[]{:S(2)}, u32[]{:S(2)}) async-start(bf16[32,16,3200]{2,1,0:T(8,128)(2,1)} %broadcast_in_dim.34), calls=%async_computation.1 | async-start | bytes 6553600 | tf_op jit(solution)/shard_map/all_to_all | solution.py:28
  13.4 6.6 %copy.50 = bf16[3072,768]{0,1:T(8,128)(2,1)} copy(bf16[3072,768]{1,0:T(8,128)(2,1)} %param.14) | data formatting | bytes 9437184 | tf_op args[3]
  20.0 6.8 %copy.49 = bf16[3072,768]{0,1:T(8,128)(2,1)} copy(bf16[3072,768]{1,0:T(8,128)(2,1)} %param.13) | data formatting | bytes 9437184 | tf_op args[2]
  26.8 29.2 %all-to-all-done.1 = bf16[32,16,3200]{2,1,0:T(8,128)(2,1)S(1)} async-done(((bf16[32,16,3200]{2,1,0:T(8,128)(2,1)}), bf16[32,16,3200]{2,1,0:T(8,128)(2,1)S(1)}, u32[]{:S(2)}, u32[]{:S(2)}) %all-to-all-start.1) | async-done | bytes 3276832 | tf_op jit(solution)/shard_map/all_to_all | solution.py:28
  59.8 5.3 %all-to-all-start.3 = ((bf16[32,16,3072]{2,1,0:T(8,128)(2,1)}), bf16[32,16,3072]{2,1,0:T(8,128)(2,1)}, u32[]{:S(2)}, u32[]{:S(2)}) async-start(bf16[32,16,3072]{2,1,0:T(8,128)(2,1)} %broadcast_in_dim.60), calls=%async_computation.3 | async-start | bytes 6291456 | tf_op jit(solution)/shard_map/all_to_all | solution.py:28
  68.9 4.4 %bitcast_multiply_fusion.1 = (bf16[3072,768]{0,1:T(8,128)(2,1)}, bf16[3072,768]{0,1:T(8,128)(2,1)}) fusion(bf16[3072,768]{0,1:T(8,128)(2,1)S(1)} %bitcast.62, bf16[96,8,24,128]{3,2,1,0:T(8,128)(2,1)S(1)} %bitcast.63, bf16[3072,768]{0,1:T(8,128)(2,1)S(1)} %copy-done.6, bf16[96,8,24,128]{3,2,1,0:T(8,128)(2,1)S(1)} %bitcast.64), kind=kLoop, calls=%fused_computation.5 | loop fusion | flops 4718592 | bytes 28311552 | tf_op jit(solution)/shard_map/mul | solution.py:18
  73.3 8.8 %fusion.1 = f32[512,1536]{1,0:T(8,128)S(1)} fusion(bf16[3072,768]{0,1:T(8,128)(2,1)} %get-tuple-element.73, bf16[3072,768]{0,1:T(8,128)(2,1)} %get-tuple-element.74, bf16[512,3200]{1,0:T(8,128)(2,1)S(1)} %bitcast.66), kind=kOutput, calls=%fused_computation.3 | convolution fusion | flops 4850712576 | bytes 15728640 | tf_op jit(solution)/shard_map/dot_general | solution.py:186
  83.4 20.0 %all-to-all-done.3 = bf16[32,16,3072]{2,1,0:T(8,128)(2,1)} async-done(((bf16[32,16,3072]{2,1,0:T(8,128)(2,1)}), bf16[32,16,3072]{2,1,0:T(8,128)(2,1)}, u32[]{:S(2)}, u32[]{:S(2)}) %all-to-all-start.3) | async-done | bytes 3145760 | tf_op jit(solution)/shard_map/all_to_all | solution.py:28
  104.1 7.6 %fusion.8 = f32[768,512]{0,1:T(8,128)S(1)} fusion(bf16[512,3072]{1,0:T(8,128)(2,1)} %bitcast.9.dy_ref, bf16[768,3072]{1,0:T(8,128)(2,1)} %param.15, bf16[96,8,24,128]{3,2,1,0:T(8,128)(2,1)S(1)} %bitcast.67), kind=kOutput, calls=%fused_computation.24 | convolution fusion | flops 2418278400 | bytes 14155776 | tf_op jit(solution)/shard_map/dot_general | solution.py:23
  113.7 3.7 %collective-permute-start.1 = (bf16[256,1536]{1,0:T(8,128)(2,1)S(1)}, bf16[256,1536]{1,0:T(8,128)(2,1)S(1)}, u32[]{:S(2)}, u32[]{:S(2)}) collective-permute-start(bf16[256,1536]{1,0:T(8,128)(2,1)S(1)} %fusion.9), channel_id=1, source_target_pairs={{0,64},{32,96},{64,0},{96,32},{1,65},{33,97},{65,1},{97,33},{2,66}... | collective-permute-start | bytes 2359304 | tf_op jit(solution)/shard_map/ppermute | solution.py:44
  118.2 17.6 %collective-permute-done.1 = bf16[256,1536]{1,0:T(8,128)(2,1)S(1)} collective-permute-done((bf16[256,1536]{1,0:T(8,128)(2,1)S(1)}, bf16[256,1536]{1,0:T(8,128)(2,1)S(1)}, u32[]{:S(2)}, u32[]{:S(2)}) %collective-permute-start.1) | collective-permute-done | bytes 786464 | tf_op jit(solution)/shard_map/ppermute | solution.py:44
  138.8 5.3 %collective-permute-done.4 = bf16[256,768]{1,0:T(8,128)(2,1)S(1)} collective-permute-done((bf16[256,768]{1,0:T(8,128)(2,1)S(1)}, bf16[256,768]{1,0:T(8,128)(2,1)S(1)}, u32[]{:S(2)}, u32[]{:S(2)}) %collective-permute-start.4) | collective-permute-done | bytes 393248 | tf_op jit(solution)/shard_map/ppermute | solution.py:44
  151.1 4.3 %convolution_convert_fusion = bf16[512,3072]{1,0:T(8,128)(2,1)} fusion(bf16[512,768]{1,0:T(8,128)(2,1)S(1)} %get-tuple-element.59.hid_ref, bf16[768,3072]{1,0:T(8,128)(2,1)S(1)} %bitcast.83, bf16[96,8,24,128]{3,2,1,0:T(8,128)(2,1)S(1)} %bitcast.70), kind=kOutput, calls=%fused_computation.7 | convolution fusion | flops 2419851264 | bytes 13369344 | tf_op jit(solution)/shard_map/dot_general | solution.py:191
  155.4 7.3 %all-to-all-start.2 = ((bf16[32,16,3072]{2,1,0:T(8,128)(2,1)}), bf16[32,16,3072]{2,1,0:T(8,128)(2,1)}, u32[]{:S(2)}, u32[]{:S(2)}) async-start(bf16[32,16,3072]{2,1,0:T(8,128)(2,1)} %bitcast.75), calls=%async_computation.2 | async-start | bytes 6291456 | tf_op jit(solution)/shard_map/all_to_all | solution.py:33
  162.7 8.8 %fusion.2 = bf16[512,3072]{1,0:T(8,128)(2,1)} fusion(bf16[3072,768]{0,1:T(8,128)(2,1)} %get-tuple-element.73, bf16[3072,768]{0,1:T(8,128)(2,1)} %get-tuple-element.74, bf16[512,768]{1,0:T(8,128)(2,1)S(1)} %get-tuple-element.58.ug_ref, bf16[512,768]{1,0:T(8,128)(2,1)S(1)} %get-tuple-element.57.gg_ref), kind=kOutput, calls=%fused_computation.8 | convolution fusion | flops 4855431168 | bytes 14155776 | tf_op jit(solution)/shard_map/dot_general | solution.py:23
  171.5 32.6 %all-to-all-done.2 = bf16[32,16,3072]{2,1,0:T(8,128)(2,1)} async-done(((bf16[32,16,3072]{2,1,0:T(8,128)(2,1)}), bf16[32,16,3072]{2,1,0:T(8,128)(2,1)}, u32[]{:S(2)}, u32[]{:S(2)}) %all-to-all-start.2) | async-done | bytes 3145760 | tf_op jit(solution)/shard_map/all_to_all | solution.py:33
  204.2 6.0 %all-to-all-start.4 = ((bf16[32,16,3072]{2,1,0:T(8,128)(2,1)}), bf16[32,16,3072]{2,1,0:T(8,128)(2,1)}, u32[]{:S(2)}, u32[]{:S(2)}) async-start(bf16[32,16,3072]{2,1,0:T(8,128)(2,1)} %bitcast.74), calls=%async_computation.4 | async-start | bytes 6291456 | tf_op jit(solution)/shard_map/all_to_all | solution.py:33
  219.7 24.0 %shard_map.94 = (bf16[224,128,128]{2,1,0:T(8,128)(2,1)}, bf16[64,128,128]{2,1,0:T(8,128)(2,1)}) custom-call(s32[432]{0:T(512)S(1)} %reshape.134.where_ref, bf16[512,3072]{1,0:T(8,128)(2,1)S(1)} %slice.56.x_ref, bf16[512,768]{1,0:T(8,128)(2,1)S(1)} %copy-done.1, bf16[512,768]{1,0:T(8,128)(2,1)S(1)} %copy-done.3, bf16[512,768]{1,0:T(8,128)(2,1)S(1)} %copy-done.5, ...), custom_call_target="tpu_custom_call" | custom-call | flops 7247757312 | bytes 16777216 | tf_op jit(solution)/shard_map/pallas_call | solution.py:94
  243.7 7.7 %all-to-all-done.4 = bf16[32,16,3072]{2,1,0:T(8,128)(2,1)} async-done(((bf16[32,16,3072]{2,1,0:T(8,128)(2,1)}), bf16[32,16,3072]{2,1,0:T(8,128)(2,1)}, u32[]{:S(2)}, u32[]{:S(2)}) %all-to-all-start.4) | async-done | bytes 3145760 | tf_op jit(solution)/shard_map/all_to_all | solution.py:33
  251.5 5.6 %all-to-all-start.5 = ((bf16[224,128,128]{2,1,0:T(8,128)(2,1)}), bf16[224,128,128]{2,1,0:T(8,128)(2,1)}, u32[]{:S(2)}, u32[]{:S(2)}) async-start(bf16[224,128,128]{2,1,0:T(8,128)(2,1)} %get-tuple-element.36), calls=%async_computation.5 | async-start | bytes 14680064 | tf_op jit(solution)/shard_map/all_to_all | solution.py:197
  260.2 43.1 %collective-permute-start.7 = (s32[]{:T(128)}, s32[]{:T(128)}, u32[]{:S(2)}, u32[]{:S(2)}) collective-permute-start(s32[]{:T(128)} %max.6), channel_id=1, source_target_pairs={{0,64},{32,96},{64,0},{96,32},{1,65},{33,97},{65,1},{97,33},{2,66}... | collective-permute-start | bytes 20 | tf_op jit(solution)/shard_map/ppermute | solution.py:182
  303.3 3.8 %collective-permute-done.7 = s32[]{:T(128)} collective-permute-done((s32[]{:T(128)}, s32[]{:T(128)}, u32[]{:S(2)}, u32[]{:S(2)}) %collective-permute-start.7) | collective-permute-done | bytes 36 | tf_op jit(solution)/shard_map/ppermute | solution.py:182
  313.8 44.1 %all-to-all-done.5 = bf16[224,128,128]{2,1,0:T(8,128)(2,1)} async-done(((bf16[224,128,128]{2,1,0:T(8,128)(2,1)}), bf16[224,128,128]{2,1,0:T(8,128)(2,1)}, u32[]{:S(2)}, u32[]{:S(2)}) %all-to-all-start.5) | async-done | bytes 7340064 | tf_op jit(solution)/shard_map/all_to_all | solution.py:197
  357.9 3.5 conditional.1
  (114 shorter events, 48.5 us)
Async XLA Ops:
  4.4 51.6 %all-to-all-start.1 = ((bf16[32,16,3200]{2,1,0:T(8,128)(2,1)}), bf16[32,16,3200]{2,1,0:T(8,128)(2,1)S(1)}, u32[]{:S(2)}, u32[]{:S(2)}) async-start(bf16[32,16,3200]{2,1,0:T(8,128)(2,1)} %broadcast_in_dim.34), calls=%async_computation.1 | async-start | bytes 6553600 | tf_op jit(solution)/shard_map/all_to_all | solution.py:28
  20.0 37.7 %copy-start.11 = (bf16[16,3072]{1,0:T(8,128)(2,1)S(1)}, bf16[16,3072]{1,0:T(8,128)(2,1)}, u32[]{:S(2)}) copy-start(bf16[16,3072]{1,0:T(8,128)(2,1)} %param.12) | copy-start | bytes 294916
  59.7 6.7 %slice-start = ((s8[4718592]{0:T(1024)(128)(4,1)}), s8[524288]{0:T(1024)(128)(4,1)S(1)}, s32[]{:S(2)}) async-start(s8[4718592]{0:T(1024)(128)(4,1)} %bitcast.61), calls=%async_computation.6 | async-start | bytes 1048576
  59.8 43.7 %all-to-all-start.3 = ((bf16[32,16,3072]{2,1,0:T(8,128)(2,1)}), bf16[32,16,3072]{2,1,0:T(8,128)(2,1)}, u32[]{:S(2)}, u32[]{:S(2)}) async-start(bf16[32,16,3072]{2,1,0:T(8,128)(2,1)} %broadcast_in_dim.60), calls=%async_computation.3 | async-start | bytes 6291456 | tf_op jit(solution)/shard_map/all_to_all | solution.py:28
  65.8 3.1 copy-start.6
  68.9 4.4 %copy-start.8 = (bf16[32,16,3200]{2,1,0:T(8,128)(2,1)S(1)}, bf16[32,16,3200]{2,1,0:T(8,128)(2,1)}, u32[]{:S(2)}) copy-start(bf16[32,16,3200]{2,1,0:T(8,128)(2,1)} %copy-done.7) | copy-start | bytes 9830404
  83.4 28.7 %collective-permute-start = (f32[256,1536]{1,0:T(8,128)}, f32[256,1536]{1,0:T(8,128)}, u32[]{:S(2)}, u32[]{:S(2)}) collective-permute-start(f32[256,1536]{1,0:T(8,128)} %constant_dynamic-slice_fusion.1), channel_id=1, source_target_pairs={{0,32},{32,0},{64,96},{96,64},{1,33},{33,1},{65,97},{97,65},{2,34}... | collective-permute-start | bytes 4718600 | tf_op jit(solution)/shard_map/ppermute | solution.py:43
  104.1 7.7 %copy-start.9 = (bf16[6,128,24,128]{3,2,1,0:T(8,128)(2,1)}, bf16[6,128,24,128]{3,2,1,0:T(8,128)(2,1)S(1)}, u32[]{:S(2)}) copy-start(bf16[6,128,24,128]{3,2,1,0:T(8,128)(2,1)S(1)} %mul.117) | copy-start | bytes 14155780
  111.8 5.6 %collective-permute-start.3 = (f32[256,768]{1,0:T(8,128)S(1)}, f32[256,768]{1,0:T(8,128)S(1)}, u32[]{:S(2)}, u32[]{:S(2)}) collective-permute-start(f32[256,768]{1,0:T(8,128)S(1)} %dynamic-slice_bitcast_fusion), channel_id=1, source_target_pairs={{0,32},{32,0},{64,96},{96,64},{1,33},{33,1},{65,97},{97,65},{2,34}... | collective-permute-start | bytes 2359304 | tf_op jit(solution)/shard_map/ppermute | solution.py:43
  113.7 22.1 %collective-permute-start.1 = (bf16[256,1536]{1,0:T(8,128)(2,1)S(1)}, bf16[256,1536]{1,0:T(8,128)(2,1)S(1)}, u32[]{:S(2)}, u32[]{:S(2)}) collective-permute-start(bf16[256,1536]{1,0:T(8,128)(2,1)S(1)} %fusion.9), channel_id=1, source_target_pairs={{0,64},{32,96},{64,0},{96,32},{1,65},{33,97},{65,1},{97,33},{2,66}... | collective-permute-start | bytes 2359304 | tf_op jit(solution)/shard_map/ppermute | solution.py:44
  117.5 26.5 %collective-permute-start.4 = (bf16[256,768]{1,0:T(8,128)(2,1)S(1)}, bf16[256,768]{1,0:T(8,128)(2,1)S(1)}, u32[]{:S(2)}, u32[]{:S(2)}) collective-permute-start(bf16[256,768]{1,0:T(8,128)(2,1)S(1)} %fusion.10), channel_id=1, source_target_pairs={{0,64},{32,96},{64,0},{96,32},{1,65},{33,97},{65,1},{97,33},{2,66}... | collective-permute-start | bytes 1179656 | tf_op jit(solution)/shard_map/ppermute | solution.py:44
  138.8 7.9 %collective-permute-start.2 = (f32[256,1536]{1,0:T(8,128)}, f32[256,1536]{1,0:T(8,128)S(1)}, u32[]{:S(2)}, u32[]{:S(2)}) collective-permute-start(f32[256,1536]{1,0:T(8,128)} %convert_add_fusion), channel_id=1, source_target_pairs={{0,32},{32,0},{64,96},{96,64},{1,33},{33,1},{65,97},{97,65},{2,34}... | collective-permute-start | bytes 4718600 | tf_op jit(solution)/shard_map/ppermute | solution.py:45
  144.1 2.4 collective-permute-start.5
  146.5 3.9 %slice-start.4 = ((s8[4718592]{0:T(1024)(128)(4,1)}), s8[4194304]{0:T(1024)(128)(4,1)S(1)}, s32[]{:S(2)}) async-start(s8[4718592]{0:T(1024)(128)(4,1)} %bitcast.82), calls=%async_computation.10 | async-start | bytes 8388608
  146.6 4.0 %slice-start.3 = ((s8[4718592]{0:T(1024)(128)(4,1)}), s8[524288]{0:T(1024)(128)(4,1)S(1)}, s32[]{:S(2)}) async-start(s8[4718592]{0:T(1024)(128)(4,1)} %bitcast.68), calls=%async_computation.9 | async-start | bytes 1048576
  146.6 4.5 %slice-start.5 = ((s8[4718592]{0:T(1024)(128)(4,1)}), s8[524288]{0:T(1024)(128)(4,1)S(1)}, s32[]{:S(2)}) async-start(s8[4718592]{0:T(1024)(128)(4,1)} %bitcast.82), calls=%async_computation.11 | async-start | bytes 1048576
  149.5 5.9 %copy-start.4 = (bf16[512,768]{1,0:T(8,128)(2,1)}, bf16[512,768]{1,0:T(8,128)(2,1)S(1)}, u32[]{:S(2)}) copy-start(bf16[512,768]{1,0:T(8,128)(2,1)S(1)} %get-tuple-element.59.hid_ref) | copy-start | bytes 2359300
  149.5 13.1 %copy-start = (bf16[512,768]{1,0:T(8,128)(2,1)}, bf16[512,768]{1,0:T(8,128)(2,1)S(1)}, u32[]{:S(2)}) copy-start(bf16[512,768]{1,0:T(8,128)(2,1)S(1)} %get-tuple-element.57.gg_ref) | copy-start | bytes 2359300
  149.5 13.1 %copy-start.2 = (bf16[512,768]{1,0:T(8,128)(2,1)}, bf16[512,768]{1,0:T(8,128)(2,1)S(1)}, u32[]{:S(2)}) copy-start(bf16[512,768]{1,0:T(8,128)(2,1)S(1)} %get-tuple-element.58.ug_ref) | copy-start | bytes 2359300
  155.4 48.8 %all-to-all-start.2 = ((bf16[32,16,3072]{2,1,0:T(8,128)(2,1)}), bf16[32,16,3072]{2,1,0:T(8,128)(2,1)}, u32[]{:S(2)}, u32[]{:S(2)}) async-start(bf16[32,16,3072]{2,1,0:T(8,128)(2,1)} %bitcast.75), calls=%async_computation.2 | async-start | bytes 6291456 | tf_op jit(solution)/shard_map/all_to_all | solution.py:33
  204.2 47.3 %all-to-all-start.4 = ((bf16[32,16,3072]{2,1,0:T(8,128)(2,1)}), bf16[32,16,3072]{2,1,0:T(8,128)(2,1)}, u32[]{:S(2)}, u32[]{:S(2)}) async-start(bf16[32,16,3072]{2,1,0:T(8,128)(2,1)} %bitcast.74), calls=%async_computation.4 | async-start | bytes 6291456 | tf_op jit(solution)/shard_map/all_to_all | solution.py:33
  251.5 106.4 %all-to-all-start.5 = ((bf16[224,128,128]{2,1,0:T(8,128)(2,1)}), bf16[224,128,128]{2,1,0:T(8,128)(2,1)}, u32[]{:S(2)}, u32[]{:S(2)}) async-start(bf16[224,128,128]{2,1,0:T(8,128)(2,1)} %get-tuple-element.36), calls=%async_computation.5 | async-start | bytes 14680064 | tf_op jit(solution)/shard_map/all_to_all | solution.py:197
  257.7 1.2 collective-permute-start.6
  260.2 46.9 %collective-permute-start.7 = (s32[]{:T(128)}, s32[]{:T(128)}, u32[]{:S(2)}, u32[]{:S(2)}) collective-permute-start(s32[]{:T(128)} %max.6), channel_id=1, source_target_pairs={{0,64},{32,96},{64,0},{96,32},{1,65},{33,97},{65,1},{97,33},{2,66}... | collective-permute-start | bytes 20 | tf_op jit(solution)/shard_map/ppermute | solution.py:182
  (7 other events, 12.1 us)

commit v2 on v1

v2 whole, which is shorter than its diff:
```python
import functools

import jax
import jax.numpy as jnp
from jax import lax
from jax.experimental import pallas as pl
from jax.experimental.pallas import tpu as pltpu
from jax.sharding import PartitionSpec as P

BLOCK = 128
MAIN = 7
EXTRA = 2
LANES = 128
BF = jnp.bfloat16
F32 = jnp.float32


def contract_last(left, right):
    return lax.dot_general(left, right, (((1,), (1,)), ((), ())), preferred_element_type=F32)


def together(go, step, *args):
    shapes = jax.eval_shape(step, *args)
    return lax.cond(go, step, lambda *_: jax.tree.map(lambda v: jnp.zeros(v.shape, v.dtype), shapes), *args)


def plane_groups(ncol):
    return [list(range(ncol // 2)), list(range(ncol // 2, ncol))]


def across(value, ncol):
    return lax.ppermute(value, "col", [(i, (i + ncol // 2) % ncol) for i in range(ncol)])


def gather_rows(part, ncol):
    many = ncol // 2
    copies = jnp.broadcast_to(part[None], (many,) + part.shape).reshape(many * part.shape[0], part.shape[1])
    return plane_exchange(copies, ncol)


def plane_exchange(value, ncol):
    return lax.all_to_all(value, "col", 0, 0, axis_index_groups=plane_groups(ncol), tiled=True)


def add_parts(got, ncol):
    many = ncol // 2
    total = jnp.sum(got.reshape(many, got.shape[0] // many, -1).astype(F32), axis=0)
    rows = total.shape[0] // 2
    return (total[:rows] + across(total[rows:], ncol)).astype(BF)


def tie(*values):
    return lax.optimization_barrier(values)


def row_sum(keep, send):
    pair = [(0, 1), (1, 0), (2, 3), (3, 2)]
    far = [(0, 2), (1, 3), (2, 0), (3, 1)]
    mine = keep + lax.ppermute(send, "row", pair)
    mine = mine + lax.ppermute(mine.astype(BF), "row", far).astype(F32)
    return mine, lax.ppermute(mine, "row", pair)


def mask_kernel(bcols, kept_ref, gate_ref, up_ref, down_ref, both_ref, out_ref):
    i = pl.program_id(0)
    count = pl.num_programs(0) * bcols
    for f in range(bcols):
        cut = slice(f * BLOCK, (f + 1) * BLOCK)
        for which, from_ref in ((0, gate_ref), (1, up_ref)):
            keep = kept_ref[which * count + i * bcols + f] > 0
            value = from_ref[:, cut]
            both_ref[:, (which * bcols + f) * BLOCK:(which * bcols + f + 1) * BLOCK] = jnp.where(keep, value, jnp.zeros_like(value))
        keep = kept_ref[2 * count + i * bcols + f] > 0
        value = down_ref[cut, :]
        out_ref[cut, :] = jnp.where(keep, value, jnp.zeros_like(value))


def mask_weights(kept, gate, up, down):
    feat, hid = gate.shape
    bcols = hid // BLOCK
    side = pl.BlockSpec((BLOCK, hid), lambda i: (i, 0))
    flat = pl.BlockSpec((hid, BLOCK), lambda i: (0, i))
    return pl.pallas_call(
        functools.partial(mask_kernel, bcols),
        grid=(feat // BLOCK,),
        out_shape=(jax.ShapeDtypeStruct((feat, 2 * hid), BF), jax.ShapeDtypeStruct((hid, feat), BF)),
        in_specs=[pl.BlockSpec(memory_space=pltpu.SMEM), side, side, flat],
        out_specs=(pl.BlockSpec((BLOCK, 2 * hid), lambda i: (i, 0)), flat),
        compiler_params=pltpu.CompilerParams(vmem_limit_bytes=16 * 2**20),
    )(kept.reshape(-1), gate, up, down)


def put_halves(first, keep_ref, send_ref, lanes, value):
    half = keep_ref.shape[0]

    @pl.when(first)
    def _():
        keep_ref[:, lanes] = value[:half]
        send_ref[:, lanes] = value[half:]

    @pl.when(jnp.logical_not(first))
    def _():
        keep_ref[:, lanes] = value[half:]
        send_ref[:, lanes] = value[:half]


def shares_kernel(feat, cut, down, core_ref, rows_ref, weight_ref, keep_ref, send_ref):
    first = core_ref[0] == 0

    def step(i, carry):
        at = pl.multiple_of(i * cut, cut)
        lanes = pl.ds(at, cut)
        if down:
            value = contract_last(rows_ref[:, :feat], weight_ref[lanes, :])
        else:
            value = jnp.dot(rows_ref[:, :feat], weight_ref[:, lanes], preferred_element_type=F32)
        put_halves(first, keep_ref, send_ref, lanes, value)
        return carry

    lax.fori_loop(0, keep_ref.shape[1] // cut, step, 0)


def shares(core, rows, weight, down):
    feat, wide = weight.shape[::-1] if down else weight.shape
    vmem = pl.BlockSpec(memory_space=pltpu.VMEM)
    shape = jax.ShapeDtypeStruct((rows.shape[0] // 2, wide), F32)
    return pl.pallas_call(
        functools.partial(shares_kernel, feat, 256, down),
        out_shape=(shape, shape),
        in_specs=[pl.BlockSpec(memory_space=pltpu.SMEM)] + [vmem] * 2,
        out_specs=(vmem, vmem),
        compiler_params=pltpu.CompilerParams(vmem_limit_bytes=40 * 2**20),
    )(core, rows, weight)


def hidden_kernel(core_ref, mine_ref, other_ref, down_ref, hidden_ref, part_ref):
    half, hid = mine_ref.shape[0], hidden_ref.shape[1]
    cut = 512

    def point(sums_ref, at):
        gate, up = sums_ref[:, :hid], sums_ref[:, hid:]
        hidden_ref[pl.ds(at, half), :] = (gate * jax.nn.sigmoid(gate) * up).astype(BF)

    place = pl.multiple_of(core_ref[0] * half, half)
    point(mine_ref, place)
    point(other_ref, pl.multiple_of(half - place, half))

    def step(i, carry):
        lanes = pl.ds(pl.multiple_of(i * cut, cut), cut)
        part_ref[:, lanes] = jnp.dot(hidden_ref[...], down_ref[:, lanes], preferred_element_type=F32).astype(BF)
        return carry

    lax.fori_loop(0, part_ref.shape[1] // cut, step, 0)


def hidden_stage(core, mine, other, wd):
    hid, feat = wd.shape
    rows = 2 * mine.shape[0]
    vmem = pl.BlockSpec(memory_space=pltpu.VMEM)
    return pl.pallas_call(
        hidden_kernel,
        out_shape=(jax.ShapeDtypeStruct((rows, hid), BF), jax.ShapeDtypeStruct((rows, feat), BF)),
        in_specs=[pl.BlockSpec(memory_space=pltpu.SMEM)] + [vmem] * 3,
        out_specs=(vmem, vmem),
        compiler_params=pltpu.CompilerParams(vmem_limit_bytes=40 * 2**20),
    )(core, mine, other, wd)


def grads_kernel(core_ref, mine_ref, other_ref, back_ref, back_other_ref, both_ref, grads_ref, part_ref):
    half, hid = back_ref.shape
    cut = 512

    def point(sums_ref, hidden_grad_ref, at):
        gate, up, hidden_grad = sums_ref[:, :hid], sums_ref[:, hid:], hidden_grad_ref[...]
        sig = jax.nn.sigmoid(gate)
        rows = pl.ds(at, half)
        grads_ref[rows, :hid] = (hidden_grad * up * sig * (1.0 + gate * (1.0 - sig))).astype(BF)
        grads_ref[rows, hid:] = (hidden_grad * (gate * sig)).astype(BF)

    place = pl.multiple_of(core_ref[0] * half, half)
    point(mine_ref, back_ref, place)
    point(other_ref, back_other_ref, pl.multiple_of(half - place, half))

    def step(i, carry):
        lanes = pl.ds(pl.multiple_of(i * cut, cut), cut)
        part_ref[:, lanes] = contract_last(grads_ref[...], both_ref[lanes, :]).astype(BF)
        return carry

    lax.fori_loop(0, part_ref.shape[1] // cut, step, 0)


def grads_stage(core, sums, back, both):
    feat, wide = both.shape
    rows = 2 * back[0].shape[0]
    vmem = pl.BlockSpec(memory_space=pltpu.VMEM)
    return pl.pallas_call(
        grads_kernel,
        out_shape=(jax.ShapeDtypeStruct((rows, wide), BF), jax.ShapeDtypeStruct((rows, feat), BF)),
        in_specs=[pl.BlockSpec(memory_space=pltpu.SMEM)] + [vmem] * 5,
        out_specs=(vmem, vmem),
        compiler_params=pltpu.CompilerParams(vmem_limit_bytes=44 * 2**20),
    )(core, *sums, *back, both)


def dot_rows(left, right):
    return lax.dot_general(left, right, (((0,), (0,)), ((), ())), preferred_element_type=F32)


def pack_kernel(factor, brows, bcols, group, where_ref, x_ref, dy_ref, grads_ref, hidden_ref, main_ref, extra_ref):
    cut = main_ref.shape[0]
    wide = group * BLOCK
    hid = bcols * BLOCK

    def store(which, d, f, block):
        at = where_ref[which * brows * bcols + d * bcols + f]

        @pl.when((at >= 0) & (at < cut))
        def _():
            main_ref[at] = block

        @pl.when(at >= cut)
        def _():
            extra_ref[at - cut] = block

    def step(i, carry):
        lanes = pl.ds(pl.multiple_of(i * wide, wide), wide)
        x = x_ref[:, lanes]
        for which in (0, 1):
            tile = (dot_rows(x, grads_ref[:, which * hid:(which + 1) * hid]) * factor).astype(BF)
            for u in range(group):
                for f in range(bcols):
                    store(which, i * group + u, f, tile[u * BLOCK:(u + 1) * BLOCK, f * BLOCK:(f + 1) * BLOCK])
        tile = (dot_rows(hidden_ref[...], dy_ref[:, lanes]) * factor).astype(BF)
        for u in range(group):
            for f in range(bcols):
                store(2, i * group + u, f, tile[f * BLOCK:(f + 1) * BLOCK, u * BLOCK:(u + 1) * BLOCK])
        return carry

    lax.fori_loop(0, brows // group, step, 0)


def pack_grads(where, x_all, dy_all, grads, hidden, factor, brows, bcols, ncol):
    vmem = pl.BlockSpec(memory_space=pltpu.VMEM)
    return pl.pallas_call(
        functools.partial(pack_kernel, factor, brows, bcols, 4),
        out_shape=(
            jax.ShapeDtypeStruct((ncol * MAIN, BLOCK, BLOCK), BF),
            jax.ShapeDtypeStruct((ncol * EXTRA, BLOCK, BLOCK), BF),
        ),
        in_specs=[pl.BlockSpec(memory_space=pltpu.SMEM)] + [vmem] * 4,
        out_specs=(vmem, vmem),
        compiler_params=pltpu.CompilerParams(vmem_limit_bytes=48 * 2**20),
    )(where, x_all, dy_all, grads, hidden)


def pick_kernel(count, from_ref, got_ref, out_ref):
    def step(i, carry):
        out_ref[i] = got_ref[from_ref[i]]
        return carry

    lax.fori_loop(0, count, step, 0, unroll=4)


def pick_blocks(source, got):
    vmem = pl.BlockSpec(memory_space=pltpu.VMEM)
    count = source.shape[0]
    return pl.pallas_call(
        functools.partial(pick_kernel, count),
        out_shape=jax.ShapeDtypeStruct((count, BLOCK, BLOCK), BF),
        in_specs=[pl.BlockSpec(memory_space=pltpu.SMEM), vmem],
        out_specs=vmem,
        compiler_params=pltpu.CompilerParams(vmem_limit_bytes=32 * 2**20),
    )(source, got)


def pair_counts(counts, offsets, ncol):
    owners = jnp.arange(ncol, dtype=jnp.int32)
    first = (owners[None, None, :] - offsets[:, :, None]) % ncol
    return (counts[:, :, None] - first + ncol - 1) // ncol


def send_places(active, counts, offsets, pairs, place, ncol):
    flat = active.reshape(3, -1)
    local = jnp.cumsum(flat, axis=1) - 1
    mine = offsets[:, place][:, None]
    owner = (mine + local) % ncol
    ahead = jnp.cumsum(pairs, axis=0) - pairs
    ahead = ahead[:, place]
    before = jnp.sum(jnp.where(owner[:, :, None] == jnp.arange(ncol)[None, None, :], ahead[:, None, :], 0), axis=2)
    slot = before + local // ncol
    at = jnp.where(slot < MAIN, owner * MAIN + slot, ncol * MAIN + owner * EXTRA + slot - MAIN)
    return jnp.where(flat > 0, at, -1).reshape(-1).astype(jnp.int32)


def pick_places(offsets, pairs, place, own, ncol):
    wanted = jnp.arange(own, dtype=jnp.int32)[None, :] * ncol + place
    source = jnp.sum((offsets[:, None, :] <= wanted[:, :, None]).astype(jnp.int32), axis=2) - 1
    ahead = (jnp.cumsum(pairs, axis=0) - pairs)[:, :, place]
    here = source[:, :, None] == jnp.arange(ncol)[None, None, :]
    start = jnp.sum(jnp.where(here, offsets[:, None, :], 0), axis=2)
    before = jnp.sum(jnp.where(here, ahead[:, None, :], 0), axis=2)
    slot = before + (wanted - start) // ncol
    at = jnp.where(slot < MAIN, source * MAIN + slot, ncol * MAIN + source * EXTRA + slot - MAIN)
    return at.reshape(-1).astype(jnp.int32)


def shards(tokens, cotangent, gate_weight, up_weight, down_weight, kept, regrown):
    feat, hid = gate_weight.shape
    brows, bcols = kept.shape[1], kept.shape[2]
    ncol = lax.axis_size("col")
    place = lax.axis_index("col")
    core = (lax.axis_index("row") % 2).astype(jnp.int32).reshape(1)
    own = brows * bcols // 4
    rows = tokens.shape[0]
    active = kept + regrown
    tally = jnp.sum(active, axis=(1, 2))
    note = jnp.zeros((rows, LANES), BF).at[0, :3].set(tally.astype(BF))
    go = jnp.sum(tally) >= 0

    mine = jnp.concatenate([tokens, note, cotangent], axis=1)
    joint = jnp.concatenate([mine, across(mine, ncol)], axis=0)
    x_all = gather_rows(joint[:, :feat + LANES], ncol)
    both, wd = mask_weights(kept, gate_weight, up_weight, down_weight)
    x_all, both, wd, late = tie(x_all, both, wd, joint[:, feat + LANES:])
    dy_all = gather_rows(late, ncol)

    near = x_all.reshape(ncol // 2, 2, rows, -1)[:, :, 0, feat:feat + 3].astype(jnp.int32)
    near = jnp.where(place < ncol // 2, near, near[:, ::-1])
    counts = near.transpose(2, 1, 0).reshape(3, ncol)
    offsets = jnp.cumsum(counts, axis=1) - counts
    pairs = pair_counts(counts, offsets, ncol)
    need = jnp.max(jnp.sum(pairs, axis=0))
    send_at = send_places(active, counts, offsets, pairs, place, ncol)
    pick_at = pick_places(offsets, pairs, place, own, ncol)

    def forward(x_all, both, wd):
        sums = row_sum(*shares(core, x_all, both, False))
        return sums + tuple(hidden_stage(core, *sums, wd))

    def backward(dy_all, sums, need, both, wd):
        back = row_sum(*shares(core, dy_all, wd, True))
        need = jnp.maximum(need, lax.ppermute(need, "row", [(0, 1), (1, 0), (2, 3), (3, 2)]))
        need = jnp.maximum(need, lax.ppermute(need, "row", [(0, 2), (1, 3), (2, 0), (3, 1)]))
        return (need,) + tuple(grads_stage(core, sums, back, both))

    gate_up_mine, gate_up_other, hidden, out_part = together(go, forward, x_all, both, wd)
    dy_all, gate_up_mine, gate_up_other, out_part, send_at, pick_at, need = tie(
        dy_all, gate_up_mine, gate_up_other, out_part, send_at, pick_at, need)
    got_out = plane_exchange(out_part, ncol)
    need, grads, in_part = together(go, backward, dy_all, (gate_up_mine, gate_up_other), need, both, wd)
    got_out, in_part, need = tie(got_out, in_part, need)
    got_in = plane_exchange(in_part, ncol)
    output = add_parts(got_out, ncol)
    factor = float(rows * ncol) ** (-0.5)
    main, extra = pack_grads(send_at, x_all, dy_all, grads, hidden, factor, brows, bcols, ncol)
    got_in, main, extra, output = tie(got_in, main, extra, output)
    got = lax.all_to_all(main, "col", 0, 0, tiled=True)
    input_grad = add_parts(got_in, ncol)

    def with_extra():
        more = lax.all_to_all(extra, "col", 0, 0, tiled=True)
        return pick_blocks(pick_at, jnp.concatenate([got, more], axis=0))

    def without():
        return pick_blocks(pick_at, got)

    grad_blocks = lax.cond(need > MAIN, with_extra, without)
    return (output, input_grad, grad_blocks.reshape(3, 1, 1, own, BLOCK, BLOCK))


def solution(mesh):
    return jax.shard_map(
        shards,
        mesh=mesh,
        in_specs=(
            P("col", "row"),
            P("col", "row"),
            P("row", "col"),
            P("row", "col"),
            P("col", "row"),
            P(None, "row", "col"),
            P(None, "row", "col"),
        ),
        out_specs=(P("col", "row"), P("col", "row"), P(None, "row", "col", None, None, None)),
        check_vma=False,
    )
```

time: 364 us -> 332 us (0.912)
  Pallas kernels: 27.5 us -> 78.1 us
  matrix products: 29.6 us -> 0 us
  starting transfers between devices: 80.9 us -> 56.1 us
  local copies, waits for them, and re-layouts: 36.1 us -> 16.9 us
  other arithmetic: 23 us -> 13.3 us
    ppermute x4 -> x7, waiting for transfers between devices: 6.51 us -> 80.9 us  [the longest x3 74.6 us: across(): lax.ppermute(value, 'col', [(i, (i + ncol // 2) % ncol) for i in range(nc...]
    all_to_all x4, waiting for transfers between devices: 89.6 us -> 28.3 us  [plane_exchange(): lax.all_to_all(value, 'col', 0, 0, axis_index_groups=plane_groups(ncol),...]
    pallas_call x0 -> x5, Pallas kernels: none -> 50.1 us  [the longest x2 16.2 us: shares(): pl.pallas_call(functools.partial(shares_kernel, feat, 256, down), out_sha...]
    ppermute x4 -> x7, starting transfers between devices: 43.2 us -> 10.3 us  [the longest x3 5.09 us: across(): lax.ppermute(value, 'col', [(i, (i + ncol // 2) % ncol) for i in range(nc...]
    dot_general x4 -> x0, matrix products: 29.6 us -> none  [the longest x2 16.5 us: contract_last(): lax.dot_general(left, right, (((1,), (1,)), ((), ())), preferred_element_...]
    all_to_all x1, waiting for transfers between devices: 44.1 us -> 19.7 us  [shards(): got = lax.all_to_all(main, 'col', 0, 0, tiled=True)]
    unnamed x41 -> x23, local copies, waits for them, and re-layouts: 24.4 us -> 10.3 us
    ppermute x2, waiting for transfers between devices: 0.01 us -> 5.67 us  [row_sum(): mine = keep + lax.ppermute(send, 'row', pair)]
  transfers between devices with their start and end apart: 13 -> 16, of which waited for: 10 -> 12; matrix products, arithmetic and copies ran while one was open for 18% -> 4% of each run, Pallas kernels for 7% -> 23%
where the time goes in v2:
time: 332 us; the launch traced here: 330 us
  waiting for transfers between devices  162 us (49%)
  Pallas kernels  78.1 us (24%)
  starting transfers between devices  56.1 us (17%)
  local copies, waits for them, and re-layouts  16.9 us (5%)
  other arithmetic  13.3 us (4%)
    ppermute x3, waiting for transfers between devices, across(): lax.ppermute(value, 'col', [(i, (i + ncol // 2) % ncol) for i in range(nc...  74.6 us
    all_to_all x4, starting transfers between devices, plane_exchange(): lax.all_to_all(value, 'col', 0, 0, axis_index_groups=plane_groups(ncol),...  30.2 us
    all_to_all x4, waiting for transfers between devices, plane_exchange(): lax.all_to_all(value, 'col', 0, 0, axis_index_groups=plane_groups(ncol),...  28.3 us
    ppermute x2, waiting for transfers between devices, row_sum(): mine = mine + lax.ppermute(mine.astype(BF), 'row', far).astype(F32)  27.3 us
    pallas_call x1, Pallas kernels, pack_grads(): pl.pallas_call(functools.partial(pack_kernel, factor, brows, bcols, 4), o...  24.5 us
    all_to_all x1, waiting for transfers between devices, shards(): got = lax.all_to_all(main, 'col', 0, 0, tiled=True)  19.7 us
    pallas_call x2, Pallas kernels, shares(): pl.pallas_call(functools.partial(shares_kernel, feat, 256, down), out_sha...  16.2 us
    pallas_call x1, Pallas kernels, mask_weights(): pl.pallas_call(functools.partial(mask_kernel, bcols), grid=(feat // BLOCK...  13.4 us
  transfers between devices with their start and end apart: 16, of which 12 were waited for; matrix products, arithmetic and copies ran while one was open for 4% of the time, Pallas kernels for 23%

profile of v2, /device:TPU:2, one launch (start us, length us, event | category | flops | bytes accessed | tf_op | source)
XLA Modules:
  0.0 329.7 jit_solution(2335890007514903985)
XLA Ops:
  5.1 5.0 %collective-permute-done.8 = bf16[16,6272]{1,0:T(8,128)(2,1)S(1)} collective-permute-done((bf16[16,6272]{1,0:T(8,128)(2,1)S(1)}, bf16[16,6272]{1,0:T(8,128)(2,1)S(1)}, u32[]{:S(2)}, u32[]{:S(2)}) %collective-permute-start.8) | collective-permute-done | bytes 200736 | tf_op jit(solution)/shard_map/ppermute | solution.py:32
  13.0 7.6 %all-to-all-start.1 = ((bf16[16,32,3200]{2,1,0:T(8,128)(2,1)}), bf16[16,32,3200]{2,1,0:T(8,128)(2,1)S(1)}, u32[]{:S(2)}, u32[]{:S(2)}) async-start(bf16[16,32,3200]{2,1,0:T(8,128)(2,1)} %broadcast_in_dim.57), calls=%async_computation.1 | async-start | bytes 6553600 | tf_op jit(solution)/shard_map/all_to_all | solution.py:42
  27.9 13.4 %shard_map.94 = (bf16[3072,1536]{1,0:T(8,128)(2,1)}, bf16[768,3072]{1,0:T(8,128)(2,1)}) custom-call(s32[432]{0:T(512)S(1)} %reshape.143.kept_ref, bf16[3072,768]{1,0:T(8,128)(2,1)S(1)} %copy-done, bf16[3072,768]{1,0:T(8,128)(2,1)S(1)} %copy-done.1, bf16[768,3072]{1,0:T(8,128)(2,1)S(1)} %copy-done.2), custom_call_target="tpu_custom_call" | custom-call | tf_op jit(solution)/shard_map/pallas_call | solution.py:83
  42.0 18.9 %all-to-all-done.1 = bf16[16,32,3200]{2,1,0:T(8,128)(2,1)S(1)} async-done(((bf16[16,32,3200]{2,1,0:T(8,128)(2,1)}), bf16[16,32,3200]{2,1,0:T(8,128)(2,1)S(1)}, u32[]{:S(2)}, u32[]{:S(2)}) %all-to-all-start.1) | async-done | bytes 3276832 | tf_op jit(solution)/shard_map/all_to_all | solution.py:42
  64.1 8.1 %all-to-all-start.2 = ((bf16[16,32,3072]{2,1,0:T(8,128)(2,1)}), bf16[16,32,3072]{2,1,0:T(8,128)(2,1)}, u32[]{:S(2)}, u32[]{:S(2)}) async-start(bf16[16,32,3072]{2,1,0:T(8,128)(2,1)} %broadcast_in_dim.58), calls=%async_computation.2 | async-start | bytes 6291456 | tf_op jit(solution)/shard_map/all_to_all | solution.py:42
  77.2 47.2 %conditional.3 = (f32[256,1536]{1,0:T(8,128)}, f32[256,1536]{1,0:T(8,128)}, bf16[512,768]{1,0:T(8,128)(2,1)}, bf16[512,3072]{1,0:T(8,128)(2,1)}) conditional(s32[]{:T(128)} %convert_element_type.59, () %tuple.41, (s32[1]{0:T(128)}, bf16[512,3200]{1,0:T(8,128)(2,1)S(1)}, bf16[3072,1536]{1,0:T(8,128)(2,1)}, bf16[768,3072]{1,0:T(8,128)(2,1)}) %tuple.71), branch_computations={%region_2.3_spmd, %region_3.4_spmd} | conditional | flops 1572864 | bytes 39321800 | solution.py:24
  77.2 9.8 %branch_1_fun.5 = (f32[256,1536]{1,0:T(8,128)S(1)}, f32[256,1536]{1,0:T(8,128)S(1)}) custom-call(s32[1]{0:T(128)} %get-tuple-element.48.core_ref, bf16[512,3200]{1,0:T(8,128)(2,1)S(1)} %get-tuple-element.49.rows_ref, bf16[3072,1536]{1,0:T(8,128)(2,1)} %get-tuple-element.50.weight_ref), custom_call_target="tpu_custom_call" | custom-call | tf_op jit(solution)/shard_map/cond/branch_1_fun/pallas_call | solution.py:127
  94.2 17.8 %collective-permute-done.1 = bf16[256,1536]{1,0:T(8,128)(2,1)S(1)} collective-permute-done((bf16[256,1536]{1,0:T(8,128)(2,1)S(1)}, bf16[256,1536]{1,0:T(8,128)(2,1)S(1)}, u32[]{:S(2)}, u32[]{:S(2)}) %collective-permute-start.1) | collective-permute-done | bytes 786464 | tf_op jit(solution)/shard_map/cond/branch_1_fun/ppermute | solution.py:60
  113.4 3.7 %collective-permute-done.2.other_ref = f32[256,1536]{1,0:T(8,128)} collective-permute-done((f32[256,1536]{1,0:T(8,128)}, f32[256,1536]{1,0:T(8,128)}, u32[]{:S(2)}, u32[]{:S(2)}) %collective-permute-start.2) | collective-permute-done | bytes 1572896 | tf_op jit(solution)/shard_map/cond/branch_1_fun/ppermute | solution.py:61
  117.1 7.3 %branch_1_fun.6 = (bf16[512,768]{1,0:T(8,128)(2,1)}, bf16[512,3072]{1,0:T(8,128)(2,1)}) custom-call(s32[1]{0:T(128)} %get-tuple-element.48.core_ref, f32[256,1536]{1,0:T(8,128)} %convert_add_fusion.mine_ref, f32[256,1536]{1,0:T(8,128)} %collective-permute-done.2.other_ref, bf16[768,3072]{1,0:T(8,128)(2,1)S(1)} %bitcast.40), custom_call_target="tpu_custom_call" | custom-call | tf_op jit(solution)/shard_map/cond/branch_1_fun/pallas_call | solution.py:160
  124.5 7.3 %all-to-all-start.3 = ((bf16[16,32,3072]{2,1,0:T(8,128)(2,1)}), bf16[16,32,3072]{2,1,0:T(8,128)(2,1)}, u32[]{:S(2)}, u32[]{:S(2)}) async-start(bf16[16,32,3072]{2,1,0:T(8,128)(2,1)} %bitcast.17), calls=%async_computation.3 | async-start | bytes 6291456 | tf_op jit(solution)/shard_map/all_to_all | solution.py:42
  131.7 44.5 %conditional.4 = (s32[]{:T(128)}, bf16[512,1536]{1,0:T(8,128)(2,1)S(1)}, bf16[512,3072]{1,0:T(8,128)(2,1)}) conditional(s32[]{:T(128)} %convert_element_type.59, () %tuple.44, (s32[]{:T(128)}, s32[1]{0:T(128)}, bf16[512,3072]{1,0:T(8,128)(2,1)}, bf16[768,3072]{1,0:T(8,128)(2,1)}, f32[256,1536]{1,0:T(8,128)}, /*index=5*/f32[256,1536]{1,0:T(8,128)}, ...), branch_computations={%region_14.15_spmd, %region_15.16_spmd} | conditional | flops 786434 | bytes 12583192 | solution.py:24
  131.7 6.4 %branch_1_fun.7 = (f32[256,768]{1,0:T(8,128)S(1)}, f32[256,768]{1,0:T(8,128)S(1)}) custom-call(s32[1]{0:T(128)} %get-tuple-element.57.core_ref, bf16[512,3072]{1,0:T(8,128)(2,1)} %get-tuple-element.60.rows_ref, bf16[768,3072]{1,0:T(8,128)(2,1)} %get-tuple-element.61.weight_ref), custom_call_target="tpu_custom_call" | custom-call | tf_op jit(solution)/shard_map/cond/branch_1_fun/pallas_call | solution.py:127
  143.9 9.4 %collective-permute-done.6 = bf16[256,768]{1,0:T(8,128)(2,1)S(1)} collective-permute-done((bf16[256,768]{1,0:T(8,128)(2,1)S(1)}, bf16[256,768]{1,0:T(8,128)(2,1)S(1)}, u32[]{:S(2)}, u32[]{:S(2)}) %collective-permute-start.6) | collective-permute-done | bytes 393248 | tf_op jit(solution)/shard_map/cond/branch_1_fun/ppermute | solution.py:60
  157.2 4.6 %collective-permute-start.4 = (s32[]{:T(128)}, s32[]{:T(128)}, u32[]{:S(2)}, u32[]{:S(2)}) collective-permute-start(s32[]{:T(128)} %max.4), channel_id=1, source_target_pairs={{0,64},{32,96},{64,0},{96,32},{1,65},{33,97},{65,1},{97,33},{2,66}... | collective-permute-start | bytes 20 | tf_op jit(solution)/shard_map/cond/branch_1_fun/ppermute | solution.py:343
  163.1 13.2 %branch_1_fun.8 = (bf16[512,1536]{1,0:T(8,128)(2,1)S(1)}, bf16[512,3072]{1,0:T(8,128)(2,1)}) custom-call(s32[1]{0:T(128)} %get-tuple-element.57.core_ref, f32[256,1536]{1,0:T(8,128)} %get-tuple-element.58.mine_ref, f32[256,1536]{1,0:T(8,128)} %get-tuple-element.59.other_ref, f32[256,768]{1,0:T(8,128)S(1)} %convert_add_fusion.1.back_ref, ...), custom_call_target="tpu_custom_call" | custom-call | tf_op jit(solution)/shard_map/cond/branch_1_fun/pallas_call | solution.py:196
  177.5 7.2 %all-to-all-start.4 = ((bf16[16,32,3072]{2,1,0:T(8,128)(2,1)}), bf16[16,32,3072]{2,1,0:T(8,128)(2,1)S(1)}, u32[]{:S(2)}, u32[]{:S(2)}) async-start(bf16[16,32,3072]{2,1,0:T(8,128)(2,1)} %bitcast.19), calls=%async_computation.4 | async-start | bytes 6291456 | tf_op jit(solution)/shard_map/all_to_all | solution.py:42
  189.0 24.5 %shard_map.95 = (bf16[224,128,128]{2,1,0:T(8,128)(2,1)}, bf16[64,128,128]{2,1,0:T(8,128)(2,1)}) custom-call(s32[432]{0:T(512)S(1)} %reshape.150.where_ref, bf16[512,3200]{1,0:T(8,128)(2,1)S(1)} %bitcast.38, bf16[512,3072]{1,0:T(8,128)(2,1)} %bitcast.8.dy_ref, bf16[512,1536]{1,0:T(8,128)(2,1)} %copy-done.5, bf16[512,768]{1,0:T(8,128)(2,1)} %get-tuple-element.123.hidden_ref), custom_call_target="tpu_custom_call" | custom-call | tf_op jit(solution)/shard_map/pallas_call | solution.py:244
  214.1 9.4 %all-to-all-done.4 = bf16[16,32,3072]{2,1,0:T(8,128)(2,1)S(1)} async-done(((bf16[16,32,3072]{2,1,0:T(8,128)(2,1)}), bf16[16,32,3072]{2,1,0:T(8,128)(2,1)S(1)}, u32[]{:S(2)}, u32[]{:S(2)}) %all-to-all-start.4) | async-done | bytes 3145760 | tf_op jit(solution)/shard_map/all_to_all | solution.py:42
  223.6 8.7 %all-to-all-start.5 = ((bf16[224,128,128]{2,1,0:T(8,128)(2,1)}), bf16[224,128,128]{2,1,0:T(8,128)(2,1)}, u32[]{:S(2)}, u32[]{:S(2)}) async-start(bf16[224,128,128]{2,1,0:T(8,128)(2,1)} %get-tuple-element.131), calls=%async_computation.5 | async-start | bytes 14680064 | tf_op jit(solution)/shard_map/all_to_all | solution.py:357
  234.4 69.6 %collective-permute-done.10 = f32[16,3072]{1,0:T(8,128)S(1)} collective-permute-done((f32[16,3072]{1,0:T(8,128)S(1)}, f32[16,3072]{1,0:T(8,128)S(1)}, u32[]{:S(2)}, u32[]{:S(2)}) %collective-permute-start.10) | collective-permute-done | bytes 196640 | tf_op jit(solution)/shard_map/ppermute | solution.py:32
  304.7 19.7 %all-to-all-done.5 = bf16[224,128,128]{2,1,0:T(8,128)(2,1)} async-done(((bf16[224,128,128]{2,1,0:T(8,128)(2,1)}), bf16[224,128,128]{2,1,0:T(8,128)(2,1)}, u32[]{:S(2)}, u32[]{:S(2)}) %all-to-all-start.5) | async-done | bytes 7340064 | tf_op jit(solution)/shard_map/all_to_all | solution.py:357
  324.4 3.5 %conditional.5 = (bf16[3,1,1,36,128,128]{5,4,3,2,1,0:T(8,128)(2,1)S(1)}) conditional(s32[]{:T(128)} %convert_element_type.69, (s32[108]{0:T(128)S(1)}, bf16[224,128,128]{2,1,0:T(8,128)(2,1)}) %tuple.48, (bf16[64,128,128]{2,1,0:T(8,128)(2,1)}, bf16[224,128,128]{2,1,0:T(8,128)(2,1)}, s32[108]{0:T(128)S(1)}) %tuple.49), branch_computations={%region_18.19_spmd, %region_19.20_spmd} | conditional | flops 4718592 | bytes 23068680 | solution.py:367
  324.4 3.4 %branch_0_fun.1 = bf16[108,128,128]{2,1,0:T(8,128)(2,1)S(1)} custom-call(s32[108]{0:T(128)S(1)} %get-tuple-element.67.from_ref, bf16[224,128,128]{2,1,0:T(8,128)(2,1)} %get-tuple-element.68.got_ref), custom_call_target="tpu_custom_call" | custom-call | tf_op jit(solution)/shard_map/cond/branch_0_fun/pallas_call | solution.py:267
  (106 shorter events, 51.0 us)
Async XLA Ops:
  3.1 7.0 %collective-permute-start.8 = (bf16[16,6272]{1,0:T(8,128)(2,1)S(1)}, bf16[16,6272]{1,0:T(8,128)(2,1)S(1)}, u32[]{:S(2)}, u32[]{:S(2)}) collective-permute-start(bf16[16,6272]{1,0:T(8,128)(2,1)S(1)} %pad_maximum_fusion.2), channel_id=1, source_target_pairs={{0,16},{1,17},{2,18},{3,19},{4,20},{5,21},{6,22},{7,23},{8,24},{9,... | collective-permute-start | bytes 602120 | tf_op jit(solution)/shard_map/ppermute | solution.py:32
  13.0 7.6 %copy-start.9 = (s32[3,24,6]{1,2,0:T(8,128)S(1)}, s32[3,24,6]{1,2,0:T(8,128)}, u32[]{:S(2)}) copy-start(s32[3,24,6]{1,2,0:T(8,128)} %param.20) | copy-start | bytes 5188
  13.0 47.9 %all-to-all-start.1 = ((bf16[16,32,3200]{2,1,0:T(8,128)(2,1)}), bf16[16,32,3200]{2,1,0:T(8,128)(2,1)S(1)}, u32[]{:S(2)}, u32[]{:S(2)}) async-start(bf16[16,32,3200]{2,1,0:T(8,128)(2,1)} %broadcast_in_dim.57), calls=%async_computation.1 | async-start | bytes 6553600 | tf_op jit(solution)/shard_map/all_to_all | solution.py:42
  20.9 2.3 copy-start
  27.9 13.5 %copy-start.7 = (bf16[16,3072]{1,0:T(8,128)(2,1)S(1)}, bf16[16,3072]{1,0:T(8,128)(2,1)}, u32[]{:S(2)}) copy-start(bf16[16,3072]{1,0:T(8,128)(2,1)} %param.16) | copy-start | bytes 294916
  27.9 13.5 %copy-start.8 = (bf16[16,3072]{1,0:T(8,128)(2,1)S(1)}, bf16[16,3072]{1,0:T(8,128)(2,1)}, u32[]{:S(2)}) copy-start(bf16[16,3072]{1,0:T(8,128)(2,1)} %param.15) | copy-start | bytes 294916
  60.9 16.3 %copy-start.3 = (bf16[16,32,3200]{2,1,0:T(8,128)(2,1)}, bf16[16,32,3200]{2,1,0:T(8,128)(2,1)S(1)}, u32[]{:S(2)}) copy-start(bf16[16,32,3200]{2,1,0:T(8,128)(2,1)S(1)} %all-to-all-done.1) | copy-start | bytes 9830404
  64.1 60.4 %all-to-all-start.2 = ((bf16[16,32,3072]{2,1,0:T(8,128)(2,1)}), bf16[16,32,3072]{2,1,0:T(8,128)(2,1)}, u32[]{:S(2)}, u32[]{:S(2)}) async-start(bf16[16,32,3072]{2,1,0:T(8,128)(2,1)} %broadcast_in_dim.58), calls=%async_computation.2 | async-start | bytes 6291456 | tf_op jit(solution)/shard_map/all_to_all | solution.py:42
  87.0 3.5 %collective-permute-start = (f32[256,1536]{1,0:T(8,128)S(1)}, f32[256,1536]{1,0:T(8,128)S(1)}, u32[]{:S(2)}, u32[]{:S(2)}) collective-permute-start(f32[256,1536]{1,0:T(8,128)S(1)} %get-tuple-element.52), channel_id=1, source_target_pairs={{0,32},{32,0},{64,96},{96,64},{1,33},{33,1},{65,97},{97,65},{2,34}... | collective-permute-start | bytes 4718600 | tf_op jit(solution)/shard_map/cond/branch_1_fun/ppermute | solution.py:59
  90.5 26.6 %slice-start = ((s8[4718592]{0:T(1024)(128)(4,1)}), s8[4194304]{0:T(1024)(128)(4,1)S(1)}, s32[]{:S(2)}) async-start(s8[4718592]{0:T(1024)(128)(4,1)} %bitcast.39), calls=%async_computation.6 | async-start | bytes 8388608 | tf_op jit(solution)/shard_map/cond
  90.5 26.6 %slice-start.1 = ((s8[4718592]{0:T(1024)(128)(4,1)}), s8[524288]{0:T(1024)(128)(4,1)S(1)}, s32[]{:S(2)}) async-start(s8[4718592]{0:T(1024)(128)(4,1)} %bitcast.39), calls=%async_computation.7 | async-start | bytes 1048576 | tf_op jit(solution)/shard_map/cond
  90.7 21.3 %collective-permute-start.1 = (bf16[256,1536]{1,0:T(8,128)(2,1)S(1)}, bf16[256,1536]{1,0:T(8,128)(2,1)S(1)}, u32[]{:S(2)}, u32[]{:S(2)}) collective-permute-start(bf16[256,1536]{1,0:T(8,128)(2,1)S(1)} %get-tuple-element.150), channel_id=1, source_target_pairs={{0,64},{32,96},{64,0},{96,32},{1,65},{33,97},{65,1},{97,33},{2,66}... | collective-permute-start | bytes 2359304 | tf_op jit(solution)/shard_map/cond/branch_1_fun/ppermute | solution.py:60
  113.4 3.8 %collective-permute-start.2 = (f32[256,1536]{1,0:T(8,128)}, f32[256,1536]{1,0:T(8,128)}, u32[]{:S(2)}, u32[]{:S(2)}) collective-permute-start(f32[256,1536]{1,0:T(8,128)} %convert_add_fusion.mine_ref), channel_id=1, source_target_pairs={{0,32},{32,0},{64,96},{96,64},{1,33},{33,1},{65,97},{97,65},{2,34}... | collective-permute-start | bytes 4718600 | tf_op jit(solution)/shard_map/cond/branch_1_fun/ppermute | solution.py:61
  124.5 51.8 %all-to-all-start.3 = ((bf16[16,32,3072]{2,1,0:T(8,128)(2,1)}), bf16[16,32,3072]{2,1,0:T(8,128)(2,1)}, u32[]{:S(2)}, u32[]{:S(2)}) async-start(bf16[16,32,3072]{2,1,0:T(8,128)(2,1)} %bitcast.17), calls=%async_computation.3 | async-start | bytes 6291456 | tf_op jit(solution)/shard_map/all_to_all | solution.py:42
  138.2 2.4 collective-permute-start.5
  140.6 12.7 %collective-permute-start.6 = (bf16[256,768]{1,0:T(8,128)(2,1)S(1)}, bf16[256,768]{1,0:T(8,128)(2,1)S(1)}, u32[]{:S(2)}, u32[]{:S(2)}) collective-permute-start(bf16[256,768]{1,0:T(8,128)(2,1)S(1)} %get-tuple-element.152), channel_id=1, source_target_pairs={{0,64},{32,96},{64,0},{96,32},{1,65},{33,97},{65,1},{97,33},{2,66}... | collective-permute-start | bytes 1179656 | tf_op jit(solution)/shard_map/cond/branch_1_fun/ppermute | solution.py:60
  153.4 9.6 %collective-permute-start.7 = (f32[256,768]{1,0:T(8,128)S(1)}, f32[256,768]{1,0:T(8,128)S(1)}, u32[]{:S(2)}, u32[]{:S(2)}) collective-permute-start(f32[256,768]{1,0:T(8,128)S(1)} %convert_add_fusion.1.back_ref), channel_id=1, source_target_pairs={{0,32},{32,0},{64,96},{96,64},{1,33},{33,1},{65,97},{97,65},{2,34}... | collective-permute-start | bytes 2359304 | tf_op jit(solution)/shard_map/cond/branch_1_fun/ppermute | solution.py:61
  153.5 2.4 collective-permute-start.3
  157.2 5.2 %collective-permute-start.4 = (s32[]{:T(128)}, s32[]{:T(128)}, u32[]{:S(2)}, u32[]{:S(2)}) collective-permute-start(s32[]{:T(128)} %max.4), channel_id=1, source_target_pairs={{0,64},{32,96},{64,0},{96,32},{1,65},{33,97},{65,1},{97,33},{2,66}... | collective-permute-start | bytes 20 | tf_op jit(solution)/shard_map/cond/branch_1_fun/ppermute | solution.py:343
  177.5 46.0 %all-to-all-start.4 = ((bf16[16,32,3072]{2,1,0:T(8,128)(2,1)}), bf16[16,32,3072]{2,1,0:T(8,128)(2,1)S(1)}, u32[]{:S(2)}, u32[]{:S(2)}) async-start(bf16[16,32,3072]{2,1,0:T(8,128)(2,1)} %bitcast.19), calls=%async_computation.4 | async-start | bytes 6291456 | tf_op jit(solution)/shard_map/all_to_all | solution.py:42
  184.8 4.2 %copy-start.4 = (bf16[16,32,3200]{2,1,0:T(8,128)(2,1)S(1)}, bf16[16,32,3200]{2,1,0:T(8,128)(2,1)}, u32[]{:S(2)}) copy-start(bf16[16,32,3200]{2,1,0:T(8,128)(2,1)} %copy-done.3) | copy-start | bytes 9830404
  187.4 26.0 %collective-permute-start.9 = (f32[16,3072]{1,0:T(8,128)S(1)}, f32[16,3072]{1,0:T(8,128)S(1)}, u32[]{:S(2)}, u32[]{:S(2)}) collective-permute-start(f32[16,3072]{1,0:T(8,128)S(1)} %slice.61), channel_id=1, source_target_pairs={{0,16},{1,17},{2,18},{3,19},{4,20},{5,21},{6,22},{7,23},{8,24},{9,... | collective-permute-start | bytes 589832 | tf_op jit(solution)/shard_map/ppermute | solution.py:32
  223.6 100.9 %all-to-all-start.5 = ((bf16[224,128,128]{2,1,0:T(8,128)(2,1)}), bf16[224,128,128]{2,1,0:T(8,128)(2,1)}, u32[]{:S(2)}, u32[]{:S(2)}) async-start(bf16[224,128,128]{2,1,0:T(8,128)(2,1)} %get-tuple-element.131), calls=%async_computation.5 | async-start | bytes 14680064 | tf_op jit(solution)/shard_map/all_to_all | solution.py:357
  232.9 71.2 %collective-permute-start.10 = (f32[16,3072]{1,0:T(8,128)S(1)}, f32[16,3072]{1,0:T(8,128)S(1)}, u32[]{:S(2)}, u32[]{:S(2)}) collective-permute-start(f32[16,3072]{1,0:T(8,128)S(1)} %slice.63), channel_id=1, source_target_pairs={{0,16},{1,17},{2,18},{3,19},{4,20},{5,21},{6,22},{7,23},{8,24},{9,... | collective-permute-start | bytes 589832 | tf_op jit(solution)/shard_map/ppermute | solution.py:32
  (4 other events, 7.7 us)

commit v3 on v2

v3 whole, which is shorter than its diff:
```python
import functools

import jax
import jax.numpy as jnp
from jax import lax
from jax.experimental import pallas as pl
from jax.experimental.pallas import tpu as pltpu
from jax.sharding import PartitionSpec as P

BLOCK = 128
MAIN = 7
EXTRA = 2
LANES = 128
BF = jnp.bfloat16
F32 = jnp.float32


def contract_last(left, right):
    return lax.dot_general(left, right, (((1,), (1,)), ((), ())), preferred_element_type=F32)


def together(go, step, *args):
    shapes = jax.eval_shape(step, *args)
    return lax.cond(go, step, lambda *_: jax.tree.map(lambda v: jnp.zeros(v.shape, v.dtype), shapes), *args)


def plane_groups(ncol):
    return [list(range(ncol // 2)), list(range(ncol // 2, ncol))]


def across(value, ncol):
    return lax.ppermute(value, "col", [(i, (i + ncol // 2) % ncol) for i in range(ncol)])


def copies(part, many):
    return jnp.broadcast_to(part[None], (many,) + part.shape).reshape(many * part.shape[0], part.shape[1])


def plane_exchange(value, ncol):
    return lax.all_to_all(value, "col", 0, 0, axis_index_groups=plane_groups(ncol), tiled=True)


def add_parts(got, ncol):
    many = ncol // 2
    total = jnp.sum(got.reshape(many, got.shape[0] // many, -1).astype(F32), axis=0)
    rows = total.shape[0] // 2
    return (total[:rows] + across(total[rows:], ncol)).astype(BF)


def tie(*values):
    return lax.optimization_barrier(values)


def row_sum(keep, send):
    pair = [(0, 1), (1, 0), (2, 3), (3, 2)]
    far = [(0, 2), (1, 3), (2, 0), (3, 1)]
    mine = keep + lax.ppermute(send, "row", pair)
    mine = mine + lax.ppermute(mine.astype(BF), "row", far).astype(F32)
    return mine, lax.ppermute(mine, "row", pair)


def mask_kernel(bcols, kept_ref, gate_ref, up_ref, down_ref, both_ref, out_ref):
    i = pl.program_id(0)
    count = pl.num_programs(0) * bcols
    for f in range(bcols):
        cut = slice(f * BLOCK, (f + 1) * BLOCK)
        for which, from_ref in ((0, gate_ref), (1, up_ref)):
            keep = kept_ref[which * count + i * bcols + f] > 0
            value = from_ref[:, cut]
            both_ref[:, (which * bcols + f) * BLOCK:(which * bcols + f + 1) * BLOCK] = jnp.where(keep, value, jnp.zeros_like(value))
        keep = kept_ref[2 * count + i * bcols + f] > 0
        value = down_ref[cut, :]
        out_ref[cut, :] = jnp.where(keep, value, jnp.zeros_like(value))


def mask_weights(kept, gate, up, down):
    feat, hid = gate.shape
    bcols = hid // BLOCK
    side = pl.BlockSpec((BLOCK, hid), lambda i: (i, 0))
    flat = pl.BlockSpec((hid, BLOCK), lambda i: (0, i))
    return pl.pallas_call(
        functools.partial(mask_kernel, bcols),
        grid=(feat // BLOCK,),
        out_shape=(jax.ShapeDtypeStruct((feat, 2 * hid), BF), jax.ShapeDtypeStruct((hid, feat), BF)),
        in_specs=[pl.BlockSpec(memory_space=pltpu.SMEM), side, side, flat],
        out_specs=(pl.BlockSpec((BLOCK, 2 * hid), lambda i: (i, 0)), flat),
        compiler_params=pltpu.CompilerParams(vmem_limit_bytes=16 * 2**20),
    )(kept.reshape(-1), gate, up, down)


def shares_kernel(reorder, core_ref, rows_ref, weight_ref, *out_refs):
    keep_ref, send_ref = out_refs[:2]
    half, feat = keep_ref.shape[0], out_refs[2].shape[1] if reorder else rows_ref.shape[1]
    if reorder:
        rows = rows_ref.shape[2]

        @pl.when(pl.program_id(0) == 0)
        def _():
            for chip in range(rows_ref.shape[1]):
                for other in range(2):
                    plane = core_ref[1] if other == 0 else 1 - core_ref[1]
                    at = (2 * chip + other) * rows
                    out_refs[2][at:at + rows, :] = rows_ref[plane, chip, :, :feat]

        value = jnp.dot(out_refs[2][...], weight_ref[...], preferred_element_type=F32)
    else:
        value = contract_last(rows_ref[...], weight_ref[...])

    @pl.when(core_ref[0] == 0)
    def _():
        keep_ref[...] = value[:half]
        send_ref[...] = value[half:]

    @pl.when(core_ref[0] != 0)
    def _():
        keep_ref[...] = value[half:]
        send_ref[...] = value[:half]


def shares(core, rows, weight, reorder):
    vmem = pl.BlockSpec(memory_space=pltpu.VMEM)
    cut = 256
    if reorder:
        (feat, wide), tokens = weight.shape, rows.shape[0] * rows.shape[1] * rows.shape[2]
        part = pl.BlockSpec((feat, cut), lambda i: (0, i))
    else:
        (wide, feat), tokens = weight.shape, rows.shape[0]
        part = pl.BlockSpec((cut, feat), lambda i: (i, 0))
    shape = jax.ShapeDtypeStruct((tokens // 2, wide), F32)
    out = pl.BlockSpec((tokens // 2, cut), lambda i: (0, i))
    more = reorder * (jax.ShapeDtypeStruct((tokens, feat), BF),)
    return pl.pallas_call(
        functools.partial(shares_kernel, reorder),
        grid=(wide // cut,),
        out_shape=(shape, shape) + more,
        in_specs=[pl.BlockSpec(memory_space=pltpu.SMEM), vmem, part],
        out_specs=(out, out) + reorder * (pl.BlockSpec((tokens, feat), lambda i: (0, 0)),),
        compiler_params=pltpu.CompilerParams(vmem_limit_bytes=40 * 2**20),
    )(core, rows, weight)


def hidden_kernel(core_ref, mine_ref, other_ref, down_ref, hidden_ref, part_ref):
    half, hid = mine_ref.shape[0], hidden_ref.shape[1]

    def point(sums_ref, at):
        gate, up = sums_ref[:, :hid], sums_ref[:, hid:]
        hidden_ref[pl.ds(at, half), :] = (gate * jax.nn.sigmoid(gate) * up).astype(BF)

    @pl.when(pl.program_id(0) == 0)
    def _():
        place = pl.multiple_of(core_ref[0] * half, half)
        point(mine_ref, place)
        point(other_ref, pl.multiple_of(half - place, half))

    part_ref[...] = jnp.dot(hidden_ref[...], down_ref[...], preferred_element_type=F32).astype(BF)


def hidden_stage(core, mine, other, wd):
    hid, feat = wd.shape
    cut = 512
    rows = 2 * mine.shape[0]
    vmem = pl.BlockSpec(memory_space=pltpu.VMEM)
    return pl.pallas_call(
        hidden_kernel,
        grid=(feat // cut,),
        out_shape=(jax.ShapeDtypeStruct((rows, hid), BF), jax.ShapeDtypeStruct((rows, feat), BF)),
        in_specs=[pl.BlockSpec(memory_space=pltpu.SMEM), vmem, vmem, pl.BlockSpec((hid, cut), lambda i: (0, i))],
        out_specs=(pl.BlockSpec((rows, hid), lambda i: (0, 0)), pl.BlockSpec((rows, cut), lambda i: (0, i))),
        compiler_params=pltpu.CompilerParams(vmem_limit_bytes=40 * 2**20),
    )(core, mine, other, wd)


def grads_kernel(core_ref, mine_ref, other_ref, back_ref, back_other_ref, both_ref, grads_ref, part_ref):
    half, hid = back_ref.shape

    def point(sums_ref, hidden_grad_ref, at):
        gate, up, hidden_grad = sums_ref[:, :hid], sums_ref[:, hid:], hidden_grad_ref[...]
        sig = jax.nn.sigmoid(gate)
        rows = pl.ds(at, half)
        grads_ref[rows, :hid] = (hidden_grad * up * sig * (1.0 + gate * (1.0 - sig))).astype(BF)
        grads_ref[rows, hid:] = (hidden_grad * (gate * sig)).astype(BF)

    @pl.when(pl.program_id(0) == 0)
    def _():
        place = pl.multiple_of(core_ref[0] * half, half)
        point(mine_ref, back_ref, place)
        point(other_ref, back_other_ref, pl.multiple_of(half - place, half))

    part_ref[...] = contract_last(grads_ref[...], both_ref[...]).astype(BF)


def grads_stage(core, sums, back, both):
    feat, wide = both.shape
    cut = 512
    rows = 2 * back[0].shape[0]
    vmem = pl.BlockSpec(memory_space=pltpu.VMEM)
    return pl.pallas_call(
        grads_kernel,
        grid=(feat // cut,),
        out_shape=(jax.ShapeDtypeStruct((rows, wide), BF), jax.ShapeDtypeStruct((rows, feat), BF)),
        in_specs=[pl.BlockSpec(memory_space=pltpu.SMEM)] + [vmem] * 4 + [pl.BlockSpec((cut, wide), lambda i: (i, 0))],
        out_specs=(pl.BlockSpec((rows, wide), lambda i: (0, 0)), pl.BlockSpec((rows, cut), lambda i: (0, i))),
        compiler_params=pltpu.CompilerParams(vmem_limit_bytes=44 * 2**20),
    )(core, *sums, *back, both)


def dot_rows(left, right):
    return lax.dot_general(left, right, (((0,), (0,)), ((), ())), preferred_element_type=F32)


def pack_kernel(factor, brows, bcols, group, where_ref, x_ref, dy_ref, grads_ref, hidden_ref, main_ref, extra_ref, turned_ref, slots_ref, sems):
    cut = main_ref.shape[0]
    more = extra_ref.shape[0]
    wide = group * BLOCK

    def store(which, d, f, block):
        slots_ref[where_ref[which * brows * bcols + d * bcols + f]] = block

    turned_ref[...] = hidden_ref[...].T

    def step(i, carry):
        lanes = pl.ds(pl.multiple_of(i * wide, wide), wide)
        tile = (dot_rows(x_ref[:, lanes], grads_ref[...]) * factor).astype(BF)
        for which in (0, 1):
            for u in range(group):
                for f in range(bcols):
                    at = (which * bcols + f) * BLOCK
                    store(which, i * group + u, f, tile[u * BLOCK:(u + 1) * BLOCK, at:at + BLOCK])
        tile = (jnp.dot(turned_ref[...], dy_ref[:, lanes], preferred_element_type=F32) * factor).astype(BF)
        for u in range(group):
            for f in range(bcols):
                store(2, i * group + u, f, tile[f * BLOCK:(f + 1) * BLOCK, u * BLOCK:(u + 1) * BLOCK])
        return carry

    lax.fori_loop(0, brows // group, step, 0)
    first = pltpu.make_async_copy(slots_ref.at[pl.ds(0, cut)], main_ref, sems.at[0])
    second = pltpu.make_async_copy(slots_ref.at[pl.ds(cut, more)], extra_ref, sems.at[1])
    first.start()
    second.start()
    first.wait()
    second.wait()


def pack_grads(where, x_all, dy_all, grads, hidden, factor, brows, bcols, ncol):
    vmem = pl.BlockSpec(memory_space=pltpu.VMEM)
    return pl.pallas_call(
        functools.partial(pack_kernel, factor, brows, bcols, 4),
        out_shape=(
            jax.ShapeDtypeStruct((ncol * MAIN, BLOCK, BLOCK), BF),
            jax.ShapeDtypeStruct((ncol * EXTRA, BLOCK, BLOCK), BF),
        ),
        in_specs=[pl.BlockSpec(memory_space=pltpu.SMEM)] + [vmem] * 4,
        out_specs=(pl.BlockSpec(memory_space=pl.ANY),) * 2,
        scratch_shapes=[
            pltpu.VMEM((hidden.shape[1], hidden.shape[0]), BF),
            pltpu.VMEM((ncol * (MAIN + EXTRA) + 1, BLOCK, BLOCK), BF),
            pltpu.SemaphoreType.DMA((2,)),
        ],
        compiler_params=pltpu.CompilerParams(vmem_limit_bytes=48 * 2**20),
    )(where, x_all, dy_all, grads, hidden)


def pick_kernel(count, from_ref, got_ref, out_ref, sem):
    def start(i, carry):
        pltpu.make_async_copy(got_ref.at[from_ref[i]], out_ref.at[i], sem).start()
        return carry

    lax.fori_loop(0, count, start, 0, unroll=4)
    pltpu.make_async_copy(got_ref.at[pl.ds(0, count)], out_ref, sem).wait()


def pick_blocks(source, got):
    count = source.shape[0]
    return pl.pallas_call(
        functools.partial(pick_kernel, count),
        out_shape=jax.ShapeDtypeStruct((count, BLOCK, BLOCK), BF),
        in_specs=[pl.BlockSpec(memory_space=pltpu.SMEM), pl.BlockSpec(memory_space=pl.ANY)],
        out_specs=pl.BlockSpec(memory_space=pl.ANY),
        scratch_shapes=[pltpu.SemaphoreType.DMA],
    )(source, got)


def pair_counts(counts, offsets, ncol):
    owners = jnp.arange(ncol, dtype=jnp.int32)
    first = (owners[None, None, :] - offsets[:, :, None]) % ncol
    return (counts[:, :, None] - first + ncol - 1) // ncol


def send_places(active, counts, offsets, pairs, place, ncol):
    flat = active.reshape(3, -1)
    local = jnp.cumsum(flat, axis=1) - 1
    mine = offsets[:, place][:, None]
    owner = (mine + local) % ncol
    ahead = jnp.cumsum(pairs, axis=0) - pairs
    ahead = ahead[:, place]
    before = jnp.sum(jnp.where(owner[:, :, None] == jnp.arange(ncol)[None, None, :], ahead[:, None, :], 0), axis=2)
    slot = before + local // ncol
    at = jnp.where(slot < MAIN, owner * MAIN + slot, ncol * MAIN + owner * EXTRA + slot - MAIN)
    return jnp.where(flat > 0, at, ncol * (MAIN + EXTRA)).reshape(-1).astype(jnp.int32)


def pick_places(offsets, pairs, place, own, ncol):
    wanted = jnp.arange(own, dtype=jnp.int32)[None, :] * ncol + place
    source = jnp.sum((offsets[:, None, :] <= wanted[:, :, None]).astype(jnp.int32), axis=2) - 1
    ahead = (jnp.cumsum(pairs, axis=0) - pairs)[:, :, place]
    here = source[:, :, None] == jnp.arange(ncol)[None, None, :]
    start = jnp.sum(jnp.where(here, offsets[:, None, :], 0), axis=2)
    before = jnp.sum(jnp.where(here, ahead[:, None, :], 0), axis=2)
    slot = before + (wanted - start) // ncol
    at = jnp.where(slot < MAIN, source * MAIN + slot, ncol * MAIN + source * EXTRA + slot - MAIN)
    return at.reshape(-1).astype(jnp.int32)


def shards(tokens, cotangent, gate_weight, up_weight, down_weight, kept, regrown):
    feat, hid = gate_weight.shape
    brows, bcols = kept.shape[1], kept.shape[2]
    ncol = lax.axis_size("col")
    place = lax.axis_index("col")
    core = jnp.stack([lax.axis_index("row") % 2, place // (ncol // 2)]).astype(jnp.int32)
    own = brows * bcols // 4
    rows = tokens.shape[0]
    active = kept + regrown
    tally = jnp.sum(active, axis=(1, 2))
    note = jnp.zeros((rows, LANES), BF).at[0, :3].set(tally.astype(BF))
    go = jnp.sum(tally) >= 0

    x_all = lax.all_to_all(copies(jnp.concatenate([tokens, note], axis=1), ncol), "col", 0, 0, tiled=True)
    both, wd = mask_weights(kept, gate_weight, up_weight, down_weight)
    joint = jnp.concatenate([cotangent, across(cotangent, ncol)], axis=0)
    x_all, both, wd, late = tie(x_all, both, wd, copies(joint, ncol // 2))
    dy_all = plane_exchange(late, ncol)

    def forward(x_all, both, wd):
        keep, send, x_all = shares(core, x_all.reshape(2, ncol // 2, rows, -1), both, True)
        sums = row_sum(keep, send)
        return sums, hidden_stage(core, *sums, wd), x_all

    def backward(note, dy_all, sums, both, wd):
        counts = note.astype(jnp.int32).T
        offsets = jnp.cumsum(counts, axis=1) - counts
        pairs = pair_counts(counts, offsets, ncol)
        need = jnp.max(jnp.sum(pairs, axis=0))
        send_at = send_places(active, counts, offsets, pairs, place, ncol)
        pick_at = pick_places(offsets, pairs, place, own, ncol)
        back = row_sum(*shares(core, dy_all, wd, False))
        return grads_stage(core, sums, back, both), (send_at, pick_at, need)

    def blocks(send_at, need, x_all, dy_all, grads, hidden):
        need = jnp.maximum(need, lax.ppermute(need, "row", [(0, 1), (1, 0), (2, 3), (3, 2)]))
        need = jnp.maximum(need, lax.ppermute(need, "row", [(0, 2), (1, 3), (2, 0), (3, 1)]))
        factor = float(rows * ncol) ** (-0.5)
        return pack_grads(send_at, x_all, dy_all, grads, hidden, factor, brows, bcols, ncol), need

    note = x_all.reshape(ncol, rows, -1)[:, 0, feat:feat + 3]
    sums, (hidden, out_part), x_all = together(go, forward, x_all, both, wd)
    dy_all, sums, out_part = tie(dy_all, sums, out_part)
    got_out = plane_exchange(out_part, ncol)
    (grads, in_part), (send_at, pick_at, need) = together(go, backward, note, dy_all, sums, both, wd)
    got_out, in_part = tie(got_out, in_part)
    got_in = plane_exchange(in_part, ncol)
    (main, extra), need = together(go, blocks, send_at, need, x_all, dy_all, grads, hidden)
    output = add_parts(got_out, ncol)
    got_in, main, extra, output, need = tie(got_in, main, extra, output, need)
    got = lax.all_to_all(main, "col", 0, 0, tiled=True)
    input_grad = add_parts(got_in, ncol)

    def with_extra():
        more = lax.all_to_all(extra, "col", 0, 0, tiled=True)
        return pick_blocks(pick_at, jnp.concatenate([got, more], axis=0))

    def without():
        return pick_blocks(pick_at, got)

    grad_blocks = lax.cond(need > MAIN, with_extra, without)
    return (output, input_grad, grad_blocks.reshape(3, 1, 1, own, BLOCK, BLOCK))


def solution(mesh):
    return jax.shard_map(
        shards,
        mesh=mesh,
        in_specs=(
            P("col", "row"),
            P("col", "row"),
            P("row", "col"),
            P("row", "col"),
            P("col", "row"),
            P(None, "row", "col"),
            P(None, "row", "col"),
        ),
        out_specs=(P("col", "row"), P("col", "row"), P(None, "row", "col", None, None, None)),
        check_vma=False,
    )
```

time: 332 us -> 354 us (1.066)
  blocking collectives: 0 us -> 28 us
  Pallas kernels: 78.1 us -> 67.4 us
  other arithmetic: 13.3 us -> 19.8 us
  waiting for transfers between devices: 162 us -> 158 us
    all_to_all x0 -> x1, blocking collectives: none -> 28 us  [with_extra(): more = lax.all_to_all(extra, 'col', 0, 0, tiled=True)]
    all_to_all x4 -> x3, waiting for transfers between devices: 28.3 us -> 12.4 us  [plane_exchange(): lax.all_to_all(value, 'col', 0, 0, axis_index_groups=plane_groups(ncol),...]
    all_to_all x0 -> x1, starting transfers between devices: none -> 9.11 us  [shards(): lax.all_to_all(copies(jnp.concatenate([tokens, note], axis=1), ncol), 'co...]
    pallas_call x1, Pallas kernels: 24.5 us -> 16.1 us  [pack_grads(): pl.pallas_call(functools.partial(pack_kernel, factor, brows, bcols, 4), o...]
    all_to_all x4 -> x3, starting transfers between devices: 30.2 us -> 22.7 us  [plane_exchange(): lax.all_to_all(value, 'col', 0, 0, axis_index_groups=plane_groups(ncol),...]
    concatenate x2 -> x3, other arithmetic: 1.94 us -> 9.14 us  [the longest x1 7.34 us: with_extra(): return pick_blocks(pick_at, jnp.concatenate([got, more], axis=0))]
    ppermute x3, waiting for transfers between devices: 74.6 us -> 81.7 us  [across(): lax.ppermute(value, 'col', [(i, (i + ncol // 2) % ncol) for i in range(nc...]
    all_to_all x1, waiting for transfers between devices: 19.7 us -> 24.7 us  [shards(): got = lax.all_to_all(main, 'col', 0, 0, tiled=True)]
  transfers between devices with their start and end apart: 16 -> 16, of which waited for: 12 -> 12; matrix products, arithmetic and copies ran while one was open for 4% -> 4% of each run, Pallas kernels for 23% -> 18%
where the time goes in v3:
time: 354 us; the launch traced here: 353 us
  waiting for transfers between devices  158 us (45%)
  Pallas kernels  67.4 us (19%)
  starting transfers between devices  56.9 us (16%)
  blocking collectives  28 us (8%)
  other arithmetic  19.8 us (6%)
  local copies, waits for them, and re-layouts  19 us (5%)
    ppermute x3, waiting for transfers between devices, across(): lax.ppermute(value, 'col', [(i, (i + ncol // 2) % ncol) for i in range(nc...  81.7 us
    all_to_all x1, blocking collectives, with_extra(): more = lax.all_to_all(extra, 'col', 0, 0, tiled=True)  28 us
    ppermute x2, waiting for transfers between devices, row_sum(): mine = mine + lax.ppermute(mine.astype(BF), 'row', far).astype(F32)  27.2 us
    all_to_all x1, waiting for transfers between devices, shards(): got = lax.all_to_all(main, 'col', 0, 0, tiled=True)  24.7 us
    all_to_all x3, starting transfers between devices, plane_exchange(): lax.all_to_all(value, 'col', 0, 0, axis_index_groups=plane_groups(ncol),...  22.7 us
    pallas_call x2, Pallas kernels, shares(): pl.pallas_call(functools.partial(shares_kernel, reorder), grid=(wide // c...  16.5 us
    pallas_call x1, Pallas kernels, pack_grads(): pl.pallas_call(functools.partial(pack_kernel, factor, brows, bcols, 4), o...  16.1 us
    pallas_call x1, Pallas kernels, mask_weights(): pl.pallas_call(functools.partial(mask_kernel, bcols), grid=(feat // BLOCK...  13.4 us
  transfers between devices with their start and end apart: 16, of which 12 were waited for; matrix products, arithmetic and copies ran while one was open for 4% of the time, Pallas kernels for 18%

profile of v3, /device:TPU:2, one launch (start us, length us, event | category | flops | bytes accessed | tf_op | source)
XLA Modules:
  0.0 352.7 jit_solution(6858413772524179104)
XLA Ops:
  5.7 9.1 %all-to-all-start.1 = ((bf16[32,16,3200]{2,1,0:T(8,128)(2,1)}), bf16[32,16,3200]{2,1,0:T(8,128)(2,1)S(1)}, u32[]{:S(2)}, u32[]{:S(2)}) async-start(bf16[32,16,3200]{2,1,0:T(8,128)(2,1)} %broadcast_in_dim.60), calls=%async_computation.1 | async-start | bytes 6553600 | tf_op jit(solution)/shard_map/all_to_all | solution.py:327
  23.6 13.4 %shard_map.94 = (bf16[3072,1536]{1,0:T(8,128)(2,1)}, bf16[768,3072]{1,0:T(8,128)(2,1)}) custom-call(s32[432]{0:T(512)S(1)} %reshape.130.kept_ref, bf16[3072,768]{1,0:T(8,128)(2,1)S(1)} %copy-done, bf16[3072,768]{1,0:T(8,128)(2,1)S(1)} %copy-done.1, bf16[768,3072]{1,0:T(8,128)(2,1)S(1)} %copy-done.2), custom_call_target="tpu_custom_call" | custom-call | tf_op jit(solution)/shard_map/pallas_call | solution.py:81
  37.0 15.9 %collective-permute-done.8 = bf16[16,3072]{1,0:T(8,128)(2,1)} collective-permute-done((bf16[16,3072]{1,0:T(8,128)(2,1)S(1)}, bf16[16,3072]{1,0:T(8,128)(2,1)}, u32[]{:S(2)}, u32[]{:S(2)}) %collective-permute-start.8) | collective-permute-done | bytes 98336 | tf_op jit(solution)/shard_map/ppermute | solution.py:32
  59.5 4.5 %all-to-all-start.2 = ((bf16[16,32,3072]{2,1,0:T(8,128)(2,1)}), bf16[16,32,3072]{2,1,0:T(8,128)(2,1)}, u32[]{:S(2)}, u32[]{:S(2)}) async-start(bf16[16,32,3072]{2,1,0:T(8,128)(2,1)} %broadcast_in_dim.61), calls=%async_computation.2 | async-start | bytes 6291456 | tf_op jit(solution)/shard_map/all_to_all | solution.py:40
  64.8 48.1 %conditional.4 = (f32[256,1536]{1,0:T(8,128)}, f32[256,1536]{1,0:T(8,128)}, bf16[512,768]{1,0:T(8,128)(2,1)}, bf16[512,3072]{1,0:T(8,128)(2,1)}, bf16[512,3072]{1,0:T(8,128)(2,1)}) conditional(s32[]{:T(128)} %convert_element_type.58, () %tuple.49, (bf16[512,3200]{1,0:T(8,128)(2,1)S(1)}, s32[2]{0:T(128)S(1)}, bf16[3072,1536]{1,0:T(8,128)(2,1)}, ...), branch_computations={%region_2.3_spmd, %region_3.4_spmd} | conditional | flops 1572864 | bytes 39321808 | solution.py:24
  64.8 10.5 %branch_1_fun.6 = (f32[256,1536]{1,0:T(8,128)S(1)}, f32[256,1536]{1,0:T(8,128)S(1)}, bf16[512,3072]{1,0:T(8,128)(2,1)}) custom-call(s32[2]{0:T(128)S(1)} %get-tuple-element.67.core_ref, bf16[2,16,16,3200]{3,2,1,0:T(8,128)(2,1)S(1)} %bitcast.46, bf16[3072,1536]{1,0:T(8,128)(2,1)} %get-tuple-element.69.weight_ref), custom_call_target="tpu_custom_call" | custom-call | tf_op jit(solution)/shard_map/cond/branch_1_fun/pallas_call | solution.py:132
  82.6 17.8 %collective-permute-done.3 = bf16[256,1536]{1,0:T(8,128)(2,1)S(1)} collective-permute-done((bf16[256,1536]{1,0:T(8,128)(2,1)S(1)}, bf16[256,1536]{1,0:T(8,128)(2,1)S(1)}, u32[]{:S(2)}, u32[]{:S(2)}) %collective-permute-start.3) | collective-permute-done | bytes 786464 | tf_op jit(solution)/shard_map/cond/branch_1_fun/ppermute | solution.py:58
  105.6 7.3 %branch_1_fun.7 = (bf16[512,768]{1,0:T(8,128)(2,1)}, bf16[512,3072]{1,0:T(8,128)(2,1)}) custom-call(s32[2]{0:T(128)S(1)} %get-tuple-element.67.core_ref, f32[256,1536]{1,0:T(8,128)} %convert_add_fusion.mine_ref, f32[256,1536]{1,0:T(8,128)} %collective-permute-done.4.other_ref, bf16[768,3072]{1,0:T(8,128)(2,1)S(1)} %bitcast.43), custom_call_target="tpu_custom_call" | custom-call | tf_op jit(solution)/shard_map/cond/branch_1_fun/pallas_call | solution.py:163
  112.9 7.2 %all-to-all-start.3 = ((bf16[16,32,3072]{2,1,0:T(8,128)(2,1)}), bf16[16,32,3072]{2,1,0:T(8,128)(2,1)}, u32[]{:S(2)}, u32[]{:S(2)}) async-start(bf16[16,32,3072]{2,1,0:T(8,128)(2,1)} %bitcast.21), calls=%async_computation.3 | async-start | bytes 6291456 | tf_op jit(solution)/shard_map/all_to_all | solution.py:40
  120.1 39.0 %conditional.5 = (bf16[512,1536]{1,0:T(8,128)(2,1)}, bf16[512,3072]{1,0:T(8,128)(2,1)}, s32[432]{0:T(512)S(1)}, s32[108]{0:T(128)S(1)}, s32[]{:T(128)}) conditional(s32[]{:T(128)} %convert_element_type.58, () %tuple.52, (s32[2]{0:T(128)S(1)}, bf16[512,3072]{1,0:T(8,128)(2,1)}, bf16[768,3072]{1,0:T(8,128)(2,1)}, f32[256,1536]{1,0:T(8,128)}, ...), branch_computations={%region_4.5_spmd, %region_5.16_spmd} | conditional | flops 1172183 | bytes 25829260 | solution.py:24
  121.9 6.0 %branch_1_fun.8 = (f32[256,768]{1,0:T(8,128)S(1)}, f32[256,768]{1,0:T(8,128)S(1)}) custom-call(s32[2]{0:T(128)S(1)} %get-tuple-element.76.core_ref, bf16[512,3072]{1,0:T(8,128)(2,1)} %get-tuple-element.79.rows_ref, bf16[768,3072]{1,0:T(8,128)(2,1)} %get-tuple-element.80.weight_ref), custom_call_target="tpu_custom_call" | custom-call | tf_op jit(solution)/shard_map/cond/branch_1_fun/pallas_call | solution.py:132
  135.2 9.4 %collective-permute-done.6 = bf16[256,768]{1,0:T(8,128)(2,1)S(1)} collective-permute-done((bf16[256,768]{1,0:T(8,128)(2,1)S(1)}, bf16[256,768]{1,0:T(8,128)(2,1)S(1)}, u32[]{:S(2)}, u32[]{:S(2)}) %collective-permute-start.6) | collective-permute-done | bytes 393248 | tf_op jit(solution)/shard_map/cond/branch_1_fun/ppermute | solution.py:58
  147.0 11.5 %branch_1_fun.9 = (bf16[512,1536]{1,0:T(8,128)(2,1)}, bf16[512,3072]{1,0:T(8,128)(2,1)}) custom-call(s32[2]{0:T(128)S(1)} %get-tuple-element.76.core_ref, f32[256,1536]{1,0:T(8,128)} %get-tuple-element.77.mine_ref, f32[256,1536]{1,0:T(8,128)} %get-tuple-element.78.other_ref, f32[256,768]{1,0:T(8,128)S(1)} %convert_add_fusion.1.back_ref, ...), custom_call_target="tpu_custom_call" | custom-call | tf_op jit(solution)/shard_map/cond/branch_1_fun/pallas_call | solution.py:197
  162.1 10.9 %all-to-all-start.4 = ((bf16[16,32,3072]{2,1,0:T(8,128)(2,1)}), bf16[16,32,3072]{2,1,0:T(8,128)(2,1)S(1)}, u32[]{:S(2)}, u32[]{:S(2)}) async-start(bf16[16,32,3072]{2,1,0:T(8,128)(2,1)} %bitcast.23), calls=%async_computation.4 | async-start | bytes 6291456 | tf_op jit(solution)/shard_map/all_to_all | solution.py:40
  176.9 23.4 %conditional.6 = (bf16[224,128,128]{2,1,0:T(8,128)(2,1)}, bf16[64,128,128]{2,1,0:T(8,128)(2,1)}, s32[]{:T(128)}) conditional(s32[]{:T(128)} %convert_element_type.58, () %tuple.55, (s32[432]{0:T(512)S(1)}, bf16[512,3072]{1,0:T(8,128)(2,1)}, bf16[512,3072]{1,0:T(8,128)(2,1)}, bf16[512,1536]{1,0:T(8,128)(2,1)}, bf16[512,768]{1,0:T(8,128)(2,1)}, ...), branch_computations={%region_16.17_spmd, %region_17.18_spmd} | conditional | flops 2 | bytes 9437220 | solution.py:24
  177.7 16.1 %branch_1_fun.10 = (bf16[224,128,128]{2,1,0:T(8,128)(2,1)}, bf16[64,128,128]{2,1,0:T(8,128)(2,1)}) custom-call(s32[432]{0:T(512)S(1)} %get-tuple-element.89.where_ref, bf16[512,3072]{1,0:T(8,128)(2,1)} %get-tuple-element.90.x_ref, bf16[512,3072]{1,0:T(8,128)(2,1)} %get-tuple-element.91.dy_ref, bf16[512,1536]{1,0:T(8,128)(2,1)} %get-tuple-element.92.grads_ref, ...), custom_call_target="tpu_custom_call" | custom-call | tf_op jit(solution)/shard_map/cond/branch_1_fun/pallas_call | solution.py:246
  194.5 4.9 %collective-permute-start.1 = (s32[]{:T(128)}, s32[]{:T(128)}, u32[]{:S(2)}, u32[]{:S(2)}) collective-permute-start(s32[]{:T(128)} %max.4), channel_id=1, source_target_pairs={{0,64},{32,96},{64,0},{96,32},{1,65},{33,97},{65,1},{97,33},{2,66}... | collective-permute-start | bytes 20 | tf_op jit(solution)/shard_map/cond/branch_1_fun/ppermute | solution.py:350
  201.9 9.5 %all-to-all-done.4 = bf16[16,32,3072]{2,1,0:T(8,128)(2,1)S(1)} async-done(((bf16[16,32,3072]{2,1,0:T(8,128)(2,1)}), bf16[16,32,3072]{2,1,0:T(8,128)(2,1)S(1)}, u32[]{:S(2)}, u32[]{:S(2)}) %all-to-all-start.4) | async-done | bytes 3145760 | tf_op jit(solution)/shard_map/all_to_all | solution.py:40
  211.4 8.3 %all-to-all-start.5 = ((bf16[224,128,128]{2,1,0:T(8,128)(2,1)}), bf16[224,128,128]{2,1,0:T(8,128)(2,1)}, u32[]{:S(2)}, u32[]{:S(2)}) async-start(bf16[224,128,128]{2,1,0:T(8,128)(2,1)} %get-tuple-element.163), calls=%async_computation.5 | async-start | bytes 14680064 | tf_op jit(solution)/shard_map/all_to_all | solution.py:364
  221.9 65.8 %collective-permute-done.10 = f32[16,3072]{1,0:T(8,128)S(1)} collective-permute-done((f32[16,3072]{1,0:T(8,128)S(1)}, f32[16,3072]{1,0:T(8,128)S(1)}, u32[]{:S(2)}, u32[]{:S(2)}) %collective-permute-start.10) | collective-permute-done | bytes 196640 | tf_op jit(solution)/shard_map/ppermute | solution.py:32
  288.4 24.7 %all-to-all-done.5 = bf16[224,128,128]{2,1,0:T(8,128)(2,1)} async-done(((bf16[224,128,128]{2,1,0:T(8,128)(2,1)}), bf16[224,128,128]{2,1,0:T(8,128)(2,1)}, u32[]{:S(2)}, u32[]{:S(2)}) %all-to-all-start.5) | async-done | bytes 7340064 | tf_op jit(solution)/shard_map/all_to_all | solution.py:364
  313.1 37.8 %conditional.7 = (bf16[3,1,1,36,128,128]{5,4,3,2,1,0:T(8,128)(2,1)S(1)}) conditional(s32[]{:T(128)} %convert_element_type.65, (s32[108]{0:T(128)S(1)}, bf16[224,128,128]{2,1,0:T(8,128)(2,1)}) %tuple.58, (bf16[64,128,128]{2,1,0:T(8,128)(2,1)}, bf16[224,128,128]{2,1,0:T(8,128)(2,1)}, s32[108]{0:T(128)S(1)}) %tuple.59), branch_computations={%region_20.21_spmd, %region_21.22_spmd} | conditional | flops 4718592 | bytes 23068680 | solution.py:374
  313.1 28.0 %all_to_all.54 = bf16[64,128,128]{2,1,0:T(8,128)(2,1)S(1)} all-to-all(bf16[64,128,128]{2,1,0:T(8,128)(2,1)} %get-tuple-element.101), channel_id=1, replica_groups=mesh['row'=4,'col'=32] {'col'}, dimensions={0} | all-to-all | bytes 4194304 | tf_op jit(solution)/shard_map/cond/branch_1_fun/all_to_all | solution.py:368
  341.1 7.3 %pad_maximum_fusion.got_ref = bf16[288,128,128]{2,1,0:T(8,128)(2,1)} fusion(bf16[64,128,128]{2,1,0:T(8,128)(2,1)S(1)} %all_to_all.54, bf16[224,128,128]{2,1,0:T(8,128)(2,1)} %get-tuple-element.100), kind=kLoop, calls=%fused_computation.1 | loop fusion | flops 4718592 | bytes 18874368 | tf_op jit(solution)/shard_map/cond/branch_1_fun/concatenate | solution.py:369
  (98 shorter events, 60.9 us)
Async XLA Ops:
  5.7 9.1 %copy-start.5 = (bf16[16,3072]{1,0:T(8,128)(2,1)S(1)}, bf16[16,3072]{1,0:T(8,128)(2,1)}, u32[]{:S(2)}) copy-start(bf16[16,3072]{1,0:T(8,128)(2,1)} %param.18) | copy-start | bytes 294916
  5.7 51.7 %all-to-all-start.1 = ((bf16[32,16,3200]{2,1,0:T(8,128)(2,1)}), bf16[32,16,3200]{2,1,0:T(8,128)(2,1)S(1)}, u32[]{:S(2)}, u32[]{:S(2)}) async-start(bf16[32,16,3200]{2,1,0:T(8,128)(2,1)} %broadcast_in_dim.60), calls=%async_computation.1 | async-start | bytes 6553600 | tf_op jit(solution)/shard_map/all_to_all | solution.py:327
  14.9 38.0 %collective-permute-start.8 = (bf16[16,3072]{1,0:T(8,128)(2,1)S(1)}, bf16[16,3072]{1,0:T(8,128)(2,1)}, u32[]{:S(2)}, u32[]{:S(2)}) collective-permute-start(bf16[16,3072]{1,0:T(8,128)(2,1)S(1)} %copy-done.5), channel_id=1, source_target_pairs={{0,16},{1,17},{2,18},{3,19},{4,20},{5,21},{6,22},{7,23},{8,24},{9,... | collective-permute-start | bytes 294920 | tf_op jit(solution)/shard_map/ppermute | solution.py:32
  16.5 2.3 copy-start
  18.9 2.3 copy-start.1
  21.2 2.3 copy-start.2
  23.6 29.3 %copy-start.6 = (bf16[16,3072]{1,0:T(8,128)(2,1)S(1)}, bf16[16,3072]{1,0:T(8,128)(2,1)}, u32[]{:S(2)}) copy-start(bf16[16,3072]{1,0:T(8,128)(2,1)} %param.18) | copy-start | bytes 294916
  59.5 53.4 %all-to-all-start.2 = ((bf16[16,32,3072]{2,1,0:T(8,128)(2,1)}), bf16[16,32,3072]{2,1,0:T(8,128)(2,1)}, u32[]{:S(2)}, u32[]{:S(2)}) async-start(bf16[16,32,3072]{2,1,0:T(8,128)(2,1)} %broadcast_in_dim.61), calls=%async_computation.2 | async-start | bytes 6291456 | tf_op jit(solution)/shard_map/all_to_all | solution.py:40
  75.3 3.4 collective-permute-start.2
  78.7 26.9 %slice-start = ((s8[4718592]{0:T(1024)(128)(4,1)}), s8[4194304]{0:T(1024)(128)(4,1)S(1)}, s32[]{:S(2)}) async-start(s8[4718592]{0:T(1024)(128)(4,1)} %bitcast.42), calls=%async_computation.6 | async-start | bytes 8388608 | tf_op jit(solution)/shard_map/cond
  78.7 26.9 %slice-start.1 = ((s8[4718592]{0:T(1024)(128)(4,1)}), s8[524288]{0:T(1024)(128)(4,1)S(1)}, s32[]{:S(2)}) async-start(s8[4718592]{0:T(1024)(128)(4,1)} %bitcast.42), calls=%async_computation.7 | async-start | bytes 1048576 | tf_op jit(solution)/shard_map/cond
  79.0 21.5 %collective-permute-start.3 = (bf16[256,1536]{1,0:T(8,128)(2,1)S(1)}, bf16[256,1536]{1,0:T(8,128)(2,1)S(1)}, u32[]{:S(2)}, u32[]{:S(2)}) collective-permute-start(bf16[256,1536]{1,0:T(8,128)(2,1)S(1)} %get-tuple-element.182), channel_id=1, source_target_pairs={{0,64},{32,96},{64,0},{96,32},{1,65},{33,97},{65,1},{97,33},{2,66}... | collective-permute-start | bytes 2359304 | tf_op jit(solution)/shard_map/cond/branch_1_fun/ppermute | solution.py:58
  101.8 3.8 %collective-permute-start.4 = (f32[256,1536]{1,0:T(8,128)}, f32[256,1536]{1,0:T(8,128)}, u32[]{:S(2)}, u32[]{:S(2)}) collective-permute-start(f32[256,1536]{1,0:T(8,128)} %convert_add_fusion.mine_ref), channel_id=1, source_target_pairs={{0,32},{32,0},{64,96},{96,64},{1,33},{33,1},{65,97},{97,65},{2,34}... | collective-permute-start | bytes 4718600 | tf_op jit(solution)/shard_map/cond/branch_1_fun/ppermute | solution.py:59
  112.9 49.2 %all-to-all-start.3 = ((bf16[16,32,3072]{2,1,0:T(8,128)(2,1)}), bf16[16,32,3072]{2,1,0:T(8,128)(2,1)}, u32[]{:S(2)}, u32[]{:S(2)}) async-start(bf16[16,32,3072]{2,1,0:T(8,128)(2,1)} %bitcast.21), calls=%async_computation.3 | async-start | bytes 6291456 | tf_op jit(solution)/shard_map/all_to_all | solution.py:40
  127.8 3.5 %collective-permute-start.5 = (f32[256,768]{1,0:T(8,128)S(1)}, f32[256,768]{1,0:T(8,128)S(1)}, u32[]{:S(2)}, u32[]{:S(2)}) collective-permute-start(f32[256,768]{1,0:T(8,128)S(1)} %get-tuple-element.82), channel_id=1, source_target_pairs={{0,32},{32,0},{64,96},{96,64},{1,33},{33,1},{65,97},{97,65},{2,34}... | collective-permute-start | bytes 2359304 | tf_op jit(solution)/shard_map/cond/branch_1_fun/ppermute | solution.py:57
  131.5 13.1 %collective-permute-start.6 = (bf16[256,768]{1,0:T(8,128)(2,1)S(1)}, bf16[256,768]{1,0:T(8,128)(2,1)S(1)}, u32[]{:S(2)}, u32[]{:S(2)}) collective-permute-start(bf16[256,768]{1,0:T(8,128)(2,1)S(1)} %get-tuple-element.184), channel_id=1, source_target_pairs={{0,64},{32,96},{64,0},{96,32},{1,65},{33,97},{65,1},{97,33},{2,66}... | collective-permute-start | bytes 1179656 | tf_op jit(solution)/shard_map/cond/branch_1_fun/ppermute | solution.py:58
  144.6 2.4 collective-permute-start.7
  162.1 49.3 %all-to-all-start.4 = ((bf16[16,32,3072]{2,1,0:T(8,128)(2,1)}), bf16[16,32,3072]{2,1,0:T(8,128)(2,1)S(1)}, u32[]{:S(2)}, u32[]{:S(2)}) async-start(bf16[16,32,3072]{2,1,0:T(8,128)(2,1)} %bitcast.23), calls=%async_computation.4 | async-start | bytes 6291456 | tf_op jit(solution)/shard_map/all_to_all | solution.py:40
  176.2 24.1 %collective-permute-start.9 = (f32[16,3072]{1,0:T(8,128)}, f32[16,3072]{1,0:T(8,128)}, u32[]{:S(2)}, u32[]{:S(2)}) collective-permute-start(f32[16,3072]{1,0:T(8,128)} %slice.49), channel_id=1, source_target_pairs={{0,16},{1,17},{2,18},{3,19},{4,20},{5,21},{6,22},{7,23},{8,24},{9,... | collective-permute-start | bytes 589832 | tf_op jit(solution)/shard_map/ppermute | solution.py:32
  176.9 17.0 %collective-permute-start = (s32[]{:T(128)}, s32[]{:T(128)}, u32[]{:S(2)}, u32[]{:S(2)}) collective-permute-start(s32[]{:T(128)} %get-tuple-element.96), channel_id=1, source_target_pairs={{0,32},{32,0},{64,96},{96,64},{1,33},{33,1},{65,97},{97,65},{2,34}... | collective-permute-start | bytes 20 | tf_op jit(solution)/shard_map/cond/branch_1_fun/ppermute | solution.py:349
  194.5 5.1 %collective-permute-start.1 = (s32[]{:T(128)}, s32[]{:T(128)}, u32[]{:S(2)}, u32[]{:S(2)}) collective-permute-start(s32[]{:T(128)} %max.4), channel_id=1, source_target_pairs={{0,64},{32,96},{64,0},{96,32},{1,65},{33,97},{65,1},{97,33},{2,66}... | collective-permute-start | bytes 20 | tf_op jit(solution)/shard_map/cond/branch_1_fun/ppermute | solution.py:350
  211.4 101.7 %all-to-all-start.5 = ((bf16[224,128,128]{2,1,0:T(8,128)(2,1)}), bf16[224,128,128]{2,1,0:T(8,128)(2,1)}, u32[]{:S(2)}, u32[]{:S(2)}) async-start(bf16[224,128,128]{2,1,0:T(8,128)(2,1)} %get-tuple-element.163), calls=%async_computation.5 | async-start | bytes 14680064 | tf_op jit(solution)/shard_map/all_to_all | solution.py:364
  220.3 67.4 %collective-permute-start.10 = (f32[16,3072]{1,0:T(8,128)S(1)}, f32[16,3072]{1,0:T(8,128)S(1)}, u32[]{:S(2)}, u32[]{:S(2)}) collective-permute-start(f32[16,3072]{1,0:T(8,128)S(1)} %slice.51), channel_id=1, source_target_pairs={{0,16},{1,17},{2,18},{3,19},{4,20},{5,21},{6,22},{7,23},{8,24},{9,... | collective-permute-start | bytes 589832 | tf_op jit(solution)/shard_map/ppermute | solution.py:32
  350.9 1.8 copy-start.4
  (1 other events, 1.7 us)

commit v4 on v3

--- a/solution.py
+++ b/solution.py
@@ -8,8 +8,9 @@
 from jax.sharding import PartitionSpec as P
 
 BLOCK = 128
-MAIN = 7
-EXTRA = 2
+MAIN = 6
+EXTRA = 3
+HAND = 16
 LANES = 128
 BF = jnp.bfloat16
 F32 = jnp.float32
@@ -51,12 +52,17 @@
     return lax.optimization_barrier(values)
 
 
+def swap_cores(value):
+    return lax.ppermute(value, "row", [(0, 1), (1, 0), (2, 3), (3, 2)])
+
+
+def swap_far(value):
+    return lax.ppermute(value, "row", [(0, 2), (1, 3), (2, 0), (3, 1)])
+
+
 def row_sum(keep, send):
-    pair = [(0, 1), (1, 0), (2, 3), (3, 2)]
-    far = [(0, 2), (1, 3), (2, 0), (3, 1)]
-    mine = keep + lax.ppermute(send, "row", pair)
-    mine = mine + lax.ppermute(mine.astype(BF), "row", far).astype(F32)
-    return mine, lax.ppermute(mine, "row", pair)
+    mine = keep + swap_cores(send)
+    return mine + swap_far(mine.astype(BF)).astype(F32)
 
 
 def mask_kernel(bcols, kept_ref, gate_ref, up_ref, down_ref, both_ref, out_ref):
@@ -140,17 +146,13 @@
 
 
 def hidden_kernel(core_ref, mine_ref, other_ref, down_ref, hidden_ref, part_ref):
-    half, hid = mine_ref.shape[0], hidden_ref.shape[1]
-
-    def point(sums_ref, at):
-        gate, up = sums_ref[:, :hid], sums_ref[:, hid:]
-        hidden_ref[pl.ds(at, half), :] = (gate * jax.nn.sigmoid(gate) * up).astype(BF)
+    half = mine_ref.shape[0]
 
     @pl.when(pl.program_id(0) == 0)
     def _():
         place = pl.multiple_of(core_ref[0] * half, half)
-        point(mine_ref, place)
-        point(other_ref, pl.multiple_of(half - place, half))
+        hidden_ref[pl.ds(place, half), :] = mine_ref[...]
+        hidden_ref[pl.ds(pl.multiple_of(half - place, half), half), :] = other_ref[...]
 
     part_ref[...] = jnp.dot(hidden_ref[...], down_ref[...], preferred_element_type=F32).astype(BF)
 
@@ -208,13 +210,13 @@
     return lax.dot_general(left, right, (((0,), (0,)), ((), ())), preferred_element_type=F32)
 
 
-def pack_kernel(factor, brows, bcols, group, where_ref, x_ref, dy_ref, grads_ref, hidden_ref, main_ref, extra_ref, turned_ref, slots_ref, sems):
+def pack_kernel(factor, brows, bcols, group, where_ref, hand_at_ref, x_ref, dy_ref, grads_ref, hidden_ref, main_ref, extra_ref, hand_ref, turned_ref, slots_ref, sems):
     cut = main_ref.shape[0]
     more = extra_ref.shape[0]
     wide = group * BLOCK
 
     def store(which, d, f, block):
-        slots_ref[where_ref[which * brows * bcols + d * bcols + f]] = block
+        slots_ref[where_ref[which, d * bcols + f]] = block
 
     turned_ref[...] = hidden_ref[...].T
 
@@ -237,78 +239,163 @@
     second = pltpu.make_async_copy(slots_ref.at[pl.ds(cut, more)], extra_ref, sems.at[1])
     first.start()
     second.start()
+    for t in range(HAND):
+        hand_ref[t] = slots_ref[hand_at_ref[0, t]]
     first.wait()
     second.wait()
 
 
-def pack_grads(where, x_all, dy_all, grads, hidden, factor, brows, bcols, ncol):
+def pack_grads(where, hand_at, x_all, dy_all, grads, hidden, factor, brows, bcols, ncol):
     vmem = pl.BlockSpec(memory_space=pltpu.VMEM)
+    smem = pl.BlockSpec(memory_space=pltpu.SMEM)
+    far = pl.BlockSpec(memory_space=pl.ANY)
     return pl.pallas_call(
         functools.partial(pack_kernel, factor, brows, bcols, 4),
-        out_shape=(
-            jax.ShapeDtypeStruct((ncol * MAIN, BLOCK, BLOCK), BF),
-            jax.ShapeDtypeStruct((ncol * EXTRA, BLOCK, BLOCK), BF),
-        ),
-        in_specs=[pl.BlockSpec(memory_space=pltpu.SMEM)] + [vmem] * 4,
-        out_specs=(pl.BlockSpec(memory_space=pl.ANY),) * 2,
+        out_shape=tuple(jax.ShapeDtypeStruct((n, BLOCK, BLOCK), BF) for n in (ncol * MAIN, ncol * EXTRA, HAND)),
+        in_specs=[smem, smem] + [vmem] * 4,
+        out_specs=(far, far, vmem),
         scratch_shapes=[
             pltpu.VMEM((hidden.shape[1], hidden.shape[0]), BF),
             pltpu.VMEM((ncol * (MAIN + EXTRA) + 1, BLOCK, BLOCK), BF),
             pltpu.SemaphoreType.DMA((2,)),
         ],
         compiler_params=pltpu.CompilerParams(vmem_limit_bytes=48 * 2**20),
-    )(where, x_all, dy_all, grads, hidden)
-
-
-def pick_kernel(count, from_ref, got_ref, out_ref, sem):
+    )(where, hand_at, x_all, dy_all, grads, hidden)
+
+
+def insert_kernel(at_ref, got_ref, old_ref, main_ref, spare_ref, sem):
+    for t in range(HAND):
+        at = at_ref[0, t]
+
+        @pl.when(at >= 0)
+        def _():
+            pltpu.make_async_copy(got_ref.at[t], main_ref.at[at], sem).start()
+
+        @pl.when(at < 0)
+        def _():
+            pltpu.make_async_copy(got_ref.at[t], spare_ref.at[t], sem).start()
+
+    pltpu.make_async_copy(got_ref, spare_ref, sem).wait()
+
+
+def insert_blocks(at, got, main):
+    far = pl.BlockSpec(memory_space=pl.ANY)
+    return pl.pallas_call(
+        insert_kernel,
+        out_shape=jax.ShapeDtypeStruct(main.shape, main.dtype),
+        in_specs=[pl.BlockSpec(memory_space=pltpu.SMEM), far, far],
+        out_specs=far,
+        scratch_shapes=[pltpu.VMEM((HAND, BLOCK, BLOCK), BF), pltpu.SemaphoreType.DMA],
+        input_output_aliases={2: 0},
+    )(at, got, main)
+
+
+def pick_kernel(own, from_ref, got_ref, out_ref, sem):
     def start(i, carry):
-        pltpu.make_async_copy(got_ref.at[from_ref[i]], out_ref.at[i], sem).start()
+        for m in range(3):
+            pltpu.make_async_copy(got_ref.at[from_ref[m, i]], out_ref.at[m * own + i], sem).start()
         return carry
 
-    lax.fori_loop(0, count, start, 0, unroll=4)
-    pltpu.make_async_copy(got_ref.at[pl.ds(0, count)], out_ref, sem).wait()
-
-
-def pick_blocks(source, got):
-    count = source.shape[0]
-    return pl.pallas_call(
-        functools.partial(pick_kernel, count),
-        out_shape=jax.ShapeDtypeStruct((count, BLOCK, BLOCK), BF),
+    lax.fori_loop(0, own, start, 0)
+    pltpu.make_async_copy(got_ref.at[pl.ds(0, 3 * own)], out_ref, sem).wait()
+
+
+def pick_blocks(source, got, own):
+    return pl.pallas_call(
+        functools.partial(pick_kernel, own),
+        out_shape=jax.ShapeDtypeStruct((3 * own, BLOCK, BLOCK), BF),
         in_specs=[pl.BlockSpec(memory_space=pltpu.SMEM), pl.BlockSpec(memory_space=pl.ANY)],
         out_specs=pl.BlockSpec(memory_space=pl.ANY),
         scratch_shapes=[pltpu.SemaphoreType.DMA],
     )(source, got)
 
 
-def pair_counts(counts, offsets, ncol):
-    owners = jnp.arange(ncol, dtype=jnp.int32)
-    first = (owners[None, None, :] - offsets[:, :, None]) % ncol
-    return (counts[:, :, None] - first + ncol - 1) // ncol
-
-
-def send_places(active, counts, offsets, pairs, place, ncol):
-    flat = active.reshape(3, -1)
-    local = jnp.cumsum(flat, axis=1) - 1
-    mine = offsets[:, place][:, None]
-    owner = (mine + local) % ncol
-    ahead = jnp.cumsum(pairs, axis=0) - pairs
-    ahead = ahead[:, place]
-    before = jnp.sum(jnp.where(owner[:, :, None] == jnp.arange(ncol)[None, None, :], ahead[:, None, :], 0), axis=2)
-    slot = before + local // ncol
-    at = jnp.where(slot < MAIN, owner * MAIN + slot, ncol * MAIN + owner * EXTRA + slot - MAIN)
-    return jnp.where(flat > 0, at, ncol * (MAIN + EXTRA)).reshape(-1).astype(jnp.int32)
-
-
-def pick_places(offsets, pairs, place, own, ncol):
-    wanted = jnp.arange(own, dtype=jnp.int32)[None, :] * ncol + place
-    source = jnp.sum((offsets[:, None, :] <= wanted[:, :, None]).astype(jnp.int32), axis=2) - 1
-    ahead = (jnp.cumsum(pairs, axis=0) - pairs)[:, :, place]
-    here = source[:, :, None] == jnp.arange(ncol)[None, None, :]
-    start = jnp.sum(jnp.where(here, offsets[:, None, :], 0), axis=2)
-    before = jnp.sum(jnp.where(here, ahead[:, None, :], 0), axis=2)
-    slot = before + (wanted - start) // ncol
-    at = jnp.where(slot < MAIN, source * MAIN + slot, ncol * MAIN + source * EXTRA + slot - MAIN)
-    return at.reshape(-1).astype(jnp.int32)
+def index_kernel(ncol, place_ref, notes_ref, local_ref, send_ref, hand_ref, insert_ref, shared_ref, direct_ref, misfit_ref):
+    place = place_ref[0]
+    half = ncol // 2
+    neighbour = (place + half) % ncol
+    rows = lax.broadcasted_iota(jnp.int32, (ncol, LANES), 0)
+    lanes = lax.broadcasted_iota(jnp.int32, (ncol, LANES), 1)
+    inside = lanes < ncol
+    zero = jnp.zeros((ncol, LANES), jnp.int32)
+
+    def across_lanes(value):
+        return jnp.sum(value.astype(F32), axis=1, keepdims=True).astype(jnp.int32)
+
+    def down_rows(value):
+        return jnp.sum(value.astype(F32), axis=0, keepdims=True).astype(jnp.int32)
+
+    def column(matrix, at):
+        return across_lanes(jnp.where(lanes == at, matrix, zero))
+
+    def swapped(matrix):
+        return jnp.concatenate([matrix[half:], matrix[:half]], axis=0)
+
+    note = notes_ref[...].astype(F32)[:, :, 0, :].reshape(ncol, LANES)
+    turned = jnp.concatenate([note] * (LANES // ncol), axis=0).T.astype(jnp.int32)
+    total, total_t = zero, zero
+    weights = []
+    for m in range(3):
+        n_row = turned[m:m + 1, :] + zero
+        n_col = column(note.astype(jnp.int32), m)
+        off_col = across_lanes(jnp.where(lanes < rows, n_row, zero))
+        off_row = down_rows(jnp.where(rows < lanes, n_col + zero, zero))
+        pairs = jnp.where(inside, (n_col - ((lanes - off_col) & (ncol - 1)) + ncol - 1) // ncol, zero)
+        pairs_t = jnp.where(inside, (n_row - ((rows - off_row) & (ncol - 1)) + ncol - 1) // ncol, zero)
+        weights.append((off_col, total, column(total_t, place)))
+        total, total_t = total + pairs, total_t + pairs_t
+    over_t = jnp.maximum(total_t - MAIN, 0)
+    over = jnp.maximum(total - MAIN, 0)
+    most = jnp.max((total + swapped(total)).astype(F32)) > 2 * MAIN
+    many = jnp.max(across_lanes(over).astype(F32)) > HAND
+    misfit_ref[0] = (most | many).astype(jnp.int32)
+
+    def ranks(device):
+        count = column(over_t, device)
+        row = down_rows(jnp.where(rows == device, over, zero))
+        rank = lanes - across_lanes(jnp.where(lanes < rows, row + zero, zero))
+        return rank, (rank >= 0) & (rank < count)
+
+    rest = ncol * (MAIN + EXTRA)
+    rank, hit = ranks(place)
+    hand_ref[...] = rest + down_rows(jnp.where(hit, ncol * MAIN + rows * EXTRA + rank - rest, zero))
+    rank, hit = ranks(neighbour)
+    slot = column(total_t, place) + rank
+    insert_ref[...] = down_rows(jnp.where(hit & (slot < MAIN), rows * MAIN + slot + 1, zero)) - 1
+    helped = column(swapped(total), place)
+    for m, (off_col, ahead, ahead_t) in enumerate(weights):
+        start = down_rows(jnp.where(rows == place, off_col + zero, zero))[:, :1]
+        local = local_ref[m:m + 1, :]
+        owner = (start + local) & (ncol - 1)
+        tall = lax.broadcasted_iota(jnp.int32, (ncol, local.shape[1]), 0)
+        slot = down_rows(jnp.where(tall == owner, ahead_t, jnp.zeros_like(tall))) + local // ncol
+        at = jnp.where(slot < MAIN, owner * MAIN + slot, ncol * MAIN + owner * EXTRA + slot - MAIN)
+        send_ref[m:m + 1, :] = jnp.where(local < 0, rest, at)
+        wanted = lax.broadcasted_iota(jnp.int32, (1, LANES), 1) * ncol + place
+        source = down_rows((off_col <= wanted).astype(jnp.int32)) - 1
+        here = rows == source
+        start = down_rows(jnp.where(here, off_col, zero))
+        slot = down_rows(jnp.where(here, column(ahead, place), zero)) + (wanted - start) // ncol
+        used = down_rows(jnp.where(here, helped, zero))
+        near = source * MAIN + slot
+        helper = (source + half) & (ncol - 1)
+        shared_ref[m:m + 1, :] = jnp.where(slot < MAIN, near, helper * MAIN + used + slot - MAIN)
+        direct_ref[m:m + 1, :] = jnp.where(slot < MAIN, near, ncol * MAIN + source * EXTRA + slot - MAIN)
+
+
+def index_tables(place, x_all, local, feat, ncol):
+    planes, chips, rows, _ = x_all.shape
+    smem = pl.BlockSpec(memory_space=pltpu.SMEM)
+    vmem = pl.BlockSpec(memory_space=pltpu.VMEM)
+    wide = jax.ShapeDtypeStruct((1, LANES), jnp.int32)
+    three = jax.ShapeDtypeStruct((8, LANES), jnp.int32)
+    return pl.pallas_call(
+        functools.partial(index_kernel, ncol),
+        grid=(1,),
+        out_shape=(jax.ShapeDtypeStruct(local.shape, jnp.int32), wide, wide, three, three, jax.ShapeDtypeStruct((1,), jnp.int32)),
+        in_specs=[smem, pl.BlockSpec((planes, chips, rows, LANES), lambda i: (0, 0, 0, feat // LANES)), vmem],
+        out_specs=(vmem,) * 5 + (smem,),
+    )(place.astype(jnp.int32).reshape(1), x_all, local)
 
 
 def shards(tokens, cotangent, gate_weight, up_weight, down_weight, kept, regrown):
@@ -327,51 +414,55 @@
     x_all = lax.all_to_all(copies(jnp.concatenate([tokens, note], axis=1), ncol), "col", 0, 0, tiled=True)
     both, wd = mask_weights(kept, gate_weight, up_weight, down_weight)
     joint = jnp.concatenate([cotangent, across(cotangent, ncol)], axis=0)
-    x_all, both, wd, late = tie(x_all, both, wd, copies(joint, ncol // 2))
+    flat = active.reshape(3, -1)
+    local = jnp.where(flat > 0, jnp.cumsum(flat, axis=1) - 1, -1)
+    local = jnp.pad(local, ((0, 5), (0, -flat.shape[1] % LANES)), constant_values=-1)
+    x_all, both, wd, late, local = tie(x_all, both, wd, copies(joint, ncol // 2), local)
     dy_all = plane_exchange(late, ncol)
 
-    def forward(x_all, both, wd):
-        keep, send, x_all = shares(core, x_all.reshape(2, ncol // 2, rows, -1), both, True)
-        sums = row_sum(keep, send)
-        return sums, hidden_stage(core, *sums, wd), x_all
-
-    def backward(note, dy_all, sums, both, wd):
-        counts = note.astype(jnp.int32).T
-        offsets = jnp.cumsum(counts, axis=1) - counts
-        pairs = pair_counts(counts, offsets, ncol)
-        need = jnp.max(jnp.sum(pairs, axis=0))
-        send_at = send_places(active, counts, offsets, pairs, place, ncol)
-        pick_at = pick_places(offsets, pairs, place, own, ncol)
+    def forward(spread, both, wd):
+        keep, send, x_all = shares(core, spread, both, True)
+        gate_up = row_sum(keep, send)
+        gate, up = gate_up[:, :hid], gate_up[:, hid:]
+        hidden = (gate * jax.nn.sigmoid(gate) * up).astype(BF)
+        return gate_up, hidden_stage(core, hidden, swap_cores(hidden), wd), x_all
+
+    def backward(spread, local, dy_all, gate_up, both, wd):
+        tables = index_tables(place, spread, local, feat, ncol)
+        gate_up_other = swap_cores(gate_up)
         back = row_sum(*shares(core, dy_all, wd, False))
-        return grads_stage(core, sums, back, both), (send_at, pick_at, need)
-
-    def blocks(send_at, need, x_all, dy_all, grads, hidden):
-        need = jnp.maximum(need, lax.ppermute(need, "row", [(0, 1), (1, 0), (2, 3), (3, 2)]))
-        need = jnp.maximum(need, lax.ppermute(need, "row", [(0, 2), (1, 3), (2, 0), (3, 1)]))
+        done = grads_stage(core, (gate_up, gate_up_other), (back, swap_cores(back)), both)
+        return done, tables
+
+    def blocks(send_at, hand_at, insert_at, misfit, x_all, dy_all, grads, hidden):
+        misfit = jnp.maximum(misfit, swap_cores(misfit))
+        misfit = jnp.maximum(misfit, swap_far(misfit))[0]
         factor = float(rows * ncol) ** (-0.5)
-        return pack_grads(send_at, x_all, dy_all, grads, hidden, factor, brows, bcols, ncol), need
-
-    note = x_all.reshape(ncol, rows, -1)[:, 0, feat:feat + 3]
-    sums, (hidden, out_part), x_all = together(go, forward, x_all, both, wd)
-    dy_all, sums, out_part = tie(dy_all, sums, out_part)
+        main, extra, hand = pack_grads(send_at, hand_at, x_all, dy_all, grads, hidden, factor, brows, bcols, ncol)
+        return insert_blocks(insert_at, across(hand, ncol), main), extra, misfit
+
+    spread = x_all.reshape(2, ncol // 2, rows, -1)
+    gate_up, (hidden, out_part), x_all = together(go, forward, spread, both, wd)
+    dy_all, gate_up, out_part = tie(dy_all, gate_up, out_part)
     got_out = plane_exchange(out_part, ncol)
-    (grads, in_part), (send_at, pick_at, need) = together(go, backward, note, dy_all, sums, both, wd)
+    (grads, in_part), (send_at, hand_at, insert_at, shared, direct, misfit) = together(
+        go, backward, spread, local, dy_all, gate_up, both, wd)
     got_out, in_part = tie(got_out, in_part)
     got_in = plane_exchange(in_part, ncol)
-    (main, extra), need = together(go, blocks, send_at, need, x_all, dy_all, grads, hidden)
+    main, extra, misfit = together(go, blocks, send_at, hand_at, insert_at, misfit, x_all, dy_all, grads, hidden)
     output = add_parts(got_out, ncol)
-    got_in, main, extra, output, need = tie(got_in, main, extra, output, need)
+    got_in, main, extra, output, misfit = tie(got_in, main, extra, output, misfit)
     got = lax.all_to_all(main, "col", 0, 0, tiled=True)
     input_grad = add_parts(got_in, ncol)
 
     def with_extra():
         more = lax.all_to_all(extra, "col", 0, 0, tiled=True)
-        return pick_blocks(pick_at, jnp.concatenate([got, more], axis=0))
+        return pick_blocks(direct, jnp.concatenate([got, more], axis=0), own)
 
     def without():
-        return pick_blocks(pick_at, got)
-
-    grad_blocks = lax.cond(need > MAIN, with_extra, without)
+        return pick_blocks(shared, got, own)
+
+    grad_blocks = lax.cond(misfit > 0, with_extra, without)
     return (output, input_grad, grad_blocks.reshape(3, 1, 1, own, BLOCK, BLOCK))
 
 

time: 354 us -> 303 us (0.86)
  blocking collectives: 28 us -> 0 us
  waiting for transfers between devices: 158 us -> 137 us
  other arithmetic: 19.8 us -> 13.1 us
  local copies, waits for them, and re-layouts: 19 us -> 15 us
  starting transfers between devices: 56.9 us -> 60.8 us
    all_to_all x1 -> x0, blocking collectives: 28 us -> none  [with_extra(): more = lax.all_to_all(extra, 'col', 0, 0, tiled=True)]
    all_to_all x1, waiting for transfers between devices: 24.7 us -> 16 us  [shards(): got = lax.all_to_all(main, 'col', 0, 0, tiled=True)]
    ppermute x3 -> x4, waiting for transfers between devices: 81.7 us -> 73.4 us  [across(): lax.ppermute(value, 'col', [(i, (i + ncol // 2) % ncol) for i in range(nc...]
    concatenate x1 -> x0, other arithmetic: 7.34 us -> none  [with_extra(): return pick_blocks(pick_at, jnp.concatenate([got, more], axis=0))]
    all_to_all x3, waiting for transfers between devices: 12.4 us -> 5.19 us  [plane_exchange(): lax.all_to_all(value, 'col', 0, 0, axis_index_groups=plane_groups(ncol),...]
    pallas_call x1 -> x3, Pallas kernels: 2.5 us -> 6.19 us  [the longest x1 2.57 us: pick_blocks(): pl.pallas_call(functools.partial(pick_kernel, own), out_shape=jax.ShapeDt...]
    ppermute x8 -> x9, starting transfers between devices: 12.9 us -> 16.4 us  [the longest x3 14.7 us: swap_far(): return lax.ppermute(value, 'row', [(0, 2), (1, 3), (2, 0), (3, 1)])]
    ppermute x8 -> x9, waiting for transfers between devices: 35.6 us -> 38.7 us  [the longest x3 30.9 us: swap_far(): return lax.ppermute(value, 'row', [(0, 2), (1, 3), (2, 0), (3, 1)])]
  transfers between devices with their start and end apart: 16 -> 18, of which waited for: 12 -> 13; matrix products, arithmetic and copies ran while one was open for 4% -> 4% of each run, Pallas kernels for 18% -> 23%
where the time goes in v4:
time: 303 us; the launch traced here: 299 us
  waiting for transfers between devices  137 us (45%)
  Pallas kernels  70.2 us (23%)
  starting transfers between devices  60.8 us (20%)
  local copies, waits for them, and re-layouts  15 us (5%)
  other arithmetic  13.1 us (4%)
    ppermute x4, waiting for transfers between devices, across(): lax.ppermute(value, 'col', [(i, (i + ncol // 2) % ncol) for i in range(nc...  73.4 us
    ppermute x3, waiting for transfers between devices, swap_far(): return lax.ppermute(value, 'row', [(0, 2), (1, 3), (2, 0), (3, 1)])  30.9 us
    all_to_all x3, starting transfers between devices, plane_exchange(): lax.all_to_all(value, 'col', 0, 0, axis_index_groups=plane_groups(ncol),...  22.7 us
    pallas_call x2, Pallas kernels, shares(): pl.pallas_call(functools.partial(shares_kernel, reorder), grid=(wide // c...  17.8 us
    pallas_call x1, Pallas kernels, pack_grads(): pl.pallas_call(functools.partial(pack_kernel, factor, brows, bcols, 4), o...  16.1 us
    all_to_all x1, waiting for transfers between devices, shards(): got = lax.all_to_all(main, 'col', 0, 0, tiled=True)  16 us
    ppermute x3, starting transfers between devices, swap_far(): return lax.ppermute(value, 'row', [(0, 2), (1, 3), (2, 0), (3, 1)])  14.7 us
    pallas_call x1, Pallas kernels, mask_weights(): pl.pallas_call(functools.partial(mask_kernel, bcols), grid=(feat // BLOCK...  13.3 us
  transfers between devices with their start and end apart: 18, of which 13 were waited for; matrix products, arithmetic and copies ran while one was open for 4% of the time, Pallas kernels for 23%

profile of v4, /device:TPU:2, one launch (start us, length us, event | category | flops | bytes accessed | tf_op | source)
XLA Modules:
  0.0 299.5 jit_solution(7570779482075492835)
XLA Ops:
  5.0 9.1 %all-to-all-start.1 = ((bf16[32,16,3200]{2,1,0:T(8,128)(2,1)}), bf16[32,16,3200]{2,1,0:T(8,128)(2,1)S(1)}, u32[]{:S(2)}, u32[]{:S(2)}) async-start(bf16[32,16,3200]{2,1,0:T(8,128)(2,1)} %broadcast_in_dim.5), calls=%async_computation.1 | async-start | bytes 6553600 | tf_op jit(solution)/shard_map/all_to_all | solution.py:414
  24.5 13.3 %shard_map.94 = (bf16[3072,1536]{1,0:T(8,128)(2,1)}, bf16[768,3072]{1,0:T(8,128)(2,1)}) custom-call(s32[432]{0:T(512)S(1)} %reshape.90.kept_ref, bf16[3072,768]{1,0:T(8,128)(2,1)S(1)} %copy-done, bf16[3072,768]{1,0:T(8,128)(2,1)S(1)} %copy-done.1, bf16[768,3072]{1,0:T(8,128)(2,1)S(1)} %copy-done.2), custom_call_target="tpu_custom_call" | custom-call | tf_op jit(solution)/shard_map/pallas_call | solution.py:87
  37.8 14.3 %collective-permute-done.10 = bf16[16,3072]{1,0:T(8,128)(2,1)} collective-permute-done((bf16[16,3072]{1,0:T(8,128)(2,1)S(1)}, bf16[16,3072]{1,0:T(8,128)(2,1)}, u32[]{:S(2)}, u32[]{:S(2)}) %collective-permute-start.10) | collective-permute-done | bytes 98336 | tf_op jit(solution)/shard_map/ppermute | solution.py:33
  53.0 3.7 %all-to-all-done.1 = bf16[32,16,3200]{2,1,0:T(8,128)(2,1)S(1)} async-done(((bf16[32,16,3200]{2,1,0:T(8,128)(2,1)}), bf16[32,16,3200]{2,1,0:T(8,128)(2,1)S(1)}, u32[]{:S(2)}, u32[]{:S(2)}) %all-to-all-start.1) | async-done | bytes 3276832 | tf_op jit(solution)/shard_map/all_to_all | solution.py:414
  58.8 4.5 %all-to-all-start.2 = ((bf16[16,32,3072]{2,1,0:T(8,128)(2,1)}), bf16[16,32,3072]{2,1,0:T(8,128)(2,1)}, u32[]{:S(2)}, u32[]{:S(2)}) async-start(bf16[16,32,3072]{2,1,0:T(8,128)(2,1)} %broadcast_in_dim.7), calls=%async_computation.2 | async-start | bytes 6291456 | tf_op jit(solution)/shard_map/all_to_all | solution.py:41
  64.0 46.3 %conditional.4 = (f32[256,1536]{1,0:T(8,128)}, bf16[512,768]{1,0:T(8,128)(2,1)}, bf16[512,3072]{1,0:T(8,128)(2,1)}, bf16[512,3072]{1,0:T(8,128)(2,1)}) conditional(s32[]{:T(128)} %convert_element_type.54, () %tuple.49, (s32[2]{0:T(128)S(1)}, bf16[2,16,16,3200]{3,2,1,0:T(8,128)(2,1)S(1)}, bf16[3072,1536]{1,0:T(8,128)(2,1)}, ...), branch_computations={%region_4.5_spmd, %region_5.6_spmd} | conditional | flops 2752512 | bytes 36569288 | solution.py:25
  64.0 10.7 %branch_1_fun.8 = (f32[256,1536]{1,0:T(8,128)S(1)}, f32[256,1536]{1,0:T(8,128)S(1)}, bf16[512,3072]{1,0:T(8,128)(2,1)}) custom-call(s32[2]{0:T(128)S(1)} %get-tuple-element.66.core_ref, bf16[2,16,16,3200]{3,2,1,0:T(8,128)(2,1)S(1)} %get-tuple-element.67.rows_ref, bf16[3072,1536]{1,0:T(8,128)(2,1)} %get-tuple-element.68.weight_ref), custom_call_target="tpu_custom_call" | custom-call | tf_op jit(solution)/shard_map/cond/branch_1_fun/pallas_call | solution.py:138
  78.4 3.7 %collective-permute-start.4 = (bf16[256,1536]{1,0:T(8,128)(2,1)S(1)}, bf16[256,1536]{1,0:T(8,128)(2,1)S(1)}, u32[]{:S(2)}, u32[]{:S(2)}) collective-permute-start(bf16[256,1536]{1,0:T(8,128)(2,1)S(1)} %get-tuple-element.185), channel_id=1, source_target_pairs={{0,64},{32,96},{64,0},{96,32},{1,65},{33,97},{65,1},{97,33},{2,66}... | collective-permute-start | bytes 2359304 | tf_op jit(solution)/shard_map/cond/branch_1_fun/ppermute | solution.py:60
  82.0 17.8 %collective-permute-done.4 = bf16[256,1536]{1,0:T(8,128)(2,1)S(1)} collective-permute-done((bf16[256,1536]{1,0:T(8,128)(2,1)S(1)}, bf16[256,1536]{1,0:T(8,128)(2,1)S(1)}, u32[]{:S(2)}, u32[]{:S(2)}) %collective-permute-start.4) | collective-permute-done | bytes 786464 | tf_op jit(solution)/shard_map/cond/branch_1_fun/ppermute | solution.py:60
  104.6 5.7 %branch_1_fun.9 = (bf16[512,768]{1,0:T(8,128)(2,1)}, bf16[512,3072]{1,0:T(8,128)(2,1)}) custom-call(s32[2]{0:T(128)S(1)} %get-tuple-element.66.core_ref, bf16[256,768]{1,0:T(8,128)(2,1)S(1)} %fusion.mine_ref, bf16[256,768]{1,0:T(8,128)(2,1)S(1)} %collective-permute-done.5.other_ref, bf16[768,3072]{1,0:T(8,128)(2,1)S(1)} %bitcast.34), custom_call_target="tpu_custom_call" | custom-call | tf_op jit(solution)/shard_map/cond/branch_1_fun/pallas_call | solution.py:165
  110.3 7.2 %all-to-all-start.3 = ((bf16[16,32,3072]{2,1,0:T(8,128)(2,1)}), bf16[16,32,3072]{2,1,0:T(8,128)(2,1)}, u32[]{:S(2)}, u32[]{:S(2)}) async-start(bf16[16,32,3072]{2,1,0:T(8,128)(2,1)} %bitcast.17), calls=%async_computation.3 | async-start | bytes 6291456 | tf_op jit(solution)/shard_map/all_to_all | solution.py:41
  117.6 36.8 %conditional.5 = (bf16[512,1536]{1,0:T(8,128)(2,1)}, bf16[512,3072]{1,0:T(8,128)(2,1)}, s32[8,256]{1,0:T(8,128)S(1)}, s32[1,128]{1,0:T(1,128)}, s32[1,128]{1,0:T...) conditional(s32[]{:T(128)} %convert_element_type.54, () %tuple.52, (f32[256,1536]{1,0:T(8,128)}, ...), branch_computations={%region_6.7_spmd, %region_7.8_spmd} | conditional | flops 786432 | bytes 31981820 | solution.py:25
  117.6 7.2 %branch_1_fun.10 = (f32[256,768]{1,0:T(8,128)S(1)}, f32[256,768]{1,0:T(8,128)S(1)}) custom-call(s32[2]{0:T(128)S(1)} %get-tuple-element.75.core_ref, bf16[512,3072]{1,0:T(8,128)(2,1)} %get-tuple-element.77.rows_ref, bf16[768,3072]{1,0:T(8,128)(2,1)} %get-tuple-element.78.weight_ref), custom_call_target="tpu_custom_call" | custom-call | tf_op jit(solution)/shard_map/cond/branch_1_fun/pallas_call | solution.py:138
  130.7 9.4 %collective-permute-done.8 = bf16[256,768]{1,0:T(8,128)(2,1)S(1)} collective-permute-done((bf16[256,768]{1,0:T(8,128)(2,1)S(1)}, bf16[256,768]{1,0:T(8,128)(2,1)S(1)}, u32[]{:S(2)}, u32[]{:S(2)}) %collective-permute-start.8) | collective-permute-done | bytes 393248 | tf_op jit(solution)/shard_map/cond/branch_1_fun/ppermute | solution.py:60
  142.6 11.1 %branch_1_fun.11 = (bf16[512,1536]{1,0:T(8,128)(2,1)}, bf16[512,3072]{1,0:T(8,128)(2,1)}) custom-call(s32[2]{0:T(128)S(1)} %get-tuple-element.75.core_ref, f32[256,1536]{1,0:T(8,128)} %get-tuple-element.76.mine_ref, f32[256,1536]{1,0:T(8,128)S(1)} %collective-permute-done.6.other_ref, f32[256,768]{1,0:T(8,128)S(1)} %convert_add_fusion.1.back_ref, ...), custom_call_target="tpu_custom_call" | custom-call | tf_op jit(solution)/shard_map/cond/branch_1_fun/pallas_call | solution.py:199
  154.3 5.2 %all-to-all-done.3 = bf16[16,32,3072]{2,1,0:T(8,128)(2,1)} async-done(((bf16[16,32,3072]{2,1,0:T(8,128)(2,1)}), bf16[16,32,3072]{2,1,0:T(8,128)(2,1)}, u32[]{:S(2)}, u32[]{:S(2)}) %all-to-all-start.3) | async-done | bytes 3145760 | tf_op jit(solution)/shard_map/all_to_all | solution.py:41
  159.5 10.9 %all-to-all-start.4 = ((bf16[16,32,3072]{2,1,0:T(8,128)(2,1)}), bf16[16,32,3072]{2,1,0:T(8,128)(2,1)S(1)}, u32[]{:S(2)}, u32[]{:S(2)}) async-start(bf16[16,32,3072]{2,1,0:T(8,128)(2,1)} %bitcast.19), calls=%async_computation.4 | async-start | bytes 6291456 | tf_op jit(solution)/shard_map/all_to_all | solution.py:41
  174.3 33.8 %conditional.6 = (bf16[192,128,128]{2,1,0:T(8,128)(2,1)}, bf16[96,128,128]{2,1,0:T(8,128)(2,1)}, s32[]{:T(128)}) conditional(s32[]{:T(128)} %convert_element_type.54, () %tuple.55, (s32[8,256]{1,0:T(8,128)S(1)}, s32[1,128]{1,0:T(1,128)}, bf16[512,3072]{1,0:T(8,128)(2,1)}, bf16[512,3072]{1,0:T(8,128)(2,1)}, bf16[512,1536]{1,0:T(8,128)(2,1)}, ...), branch_computations={%region_8.9_spmd, %region_9.10_spmd} | conditional | flops 2 | bytes 9437220 | solution.py:25
  174.3 16.1 %branch_1_fun.13 = (bf16[192,128,128]{2,1,0:T(8,128)(2,1)}, bf16[96,128,128]{2,1,0:T(8,128)(2,1)}, bf16[16,128,128]{2,1,0:T(8,128)(2,1)S(1)}) custom-call(s32[8,256]{1,0:T(8,128)S(1)} %get-tuple-element.94.where_ref, s32[1,128]{1,0:T(1,128)} %get-tuple-element.95.hand_at_ref, bf16[512,3072]{1,0:T(8,128)(2,1)} %get-tuple-element.96.x_ref, ...), custom_call_target="tpu_custom_call" | custom-call | tf_op jit(solution)/shard_map/cond/branch_1_fun/pallas_call | solution.py:252
  193.7 7.7 %collective-permute-start.2 = (s32[1]{0:T(128)}, s32[1]{0:T(128)}, u32[]{:S(2)}, u32[]{:S(2)}) collective-permute-start(s32[1]{0:T(128)} %max.4), channel_id=1, source_target_pairs={{0,64},{32,96},{64,0},{96,32},{1,65},{33,97},{65,1},{97,33},{2,66}... | collective-permute-start | bytes 20 | tf_op jit(solution)/shard_map/cond/branch_1_fun/ppermute | solution.py:60
  201.4 3.7 %collective-permute-done.2 = s32[1]{0:T(128)} collective-permute-done((s32[1]{0:T(128)}, s32[1]{0:T(128)}, u32[]{:S(2)}, u32[]{:S(2)}) %collective-permute-start.2) | collective-permute-done | bytes 36 | tf_op jit(solution)/shard_map/cond/branch_1_fun/ppermute | solution.py:60
  209.8 7.4 %all-to-all-start.5 = ((bf16[192,128,128]{2,1,0:T(8,128)(2,1)}), bf16[192,128,128]{2,1,0:T(8,128)(2,1)}, u32[]{:S(2)}, u32[]{:S(2)}) async-start(bf16[192,128,128]{2,1,0:T(8,128)(2,1)} %get-tuple-element.173), calls=%async_computation.5 | async-start | bytes 12582912 | tf_op jit(solution)/shard_map/all_to_all | solution.py:455
  219.3 59.1 %collective-permute-done.12 = f32[16,3072]{1,0:T(8,128)S(1)} collective-permute-done((f32[16,3072]{1,0:T(8,128)S(1)}, f32[16,3072]{1,0:T(8,128)S(1)}, u32[]{:S(2)}, u32[]{:S(2)}) %collective-permute-start.12) | collective-permute-done | bytes 196640 | tf_op jit(solution)/shard_map/ppermute | solution.py:33
  279.1 16.0 %all-to-all-done.5 = bf16[192,128,128]{2,1,0:T(8,128)(2,1)} async-done(((bf16[192,128,128]{2,1,0:T(8,128)(2,1)}), bf16[192,128,128]{2,1,0:T(8,128)(2,1)}, u32[]{:S(2)}, u32[]{:S(2)}) %all-to-all-start.5) | async-done | bytes 6291488 | tf_op jit(solution)/shard_map/all_to_all | solution.py:455
  (82 shorter events, 54.9 us)
Async XLA Ops:
  5.0 9.1 %copy-start.6 = (bf16[16,3072]{1,0:T(8,128)(2,1)S(1)}, bf16[16,3072]{1,0:T(8,128)(2,1)}, u32[]{:S(2)}) copy-start(bf16[16,3072]{1,0:T(8,128)(2,1)} %param.18) | copy-start | bytes 294916
  5.0 12.2 %copy-start.8 = (s32[3,24,6]{1,2,0:T(8,128)S(1)}, s32[3,24,6]{1,2,0:T(8,128)}, u32[]{:S(2)}) copy-start(s32[3,24,6]{1,2,0:T(8,128)} %param.22) | copy-start | bytes 5188
  5.0 51.7 %all-to-all-start.1 = ((bf16[32,16,3200]{2,1,0:T(8,128)(2,1)}), bf16[32,16,3200]{2,1,0:T(8,128)(2,1)S(1)}, u32[]{:S(2)}, u32[]{:S(2)}) async-start(bf16[32,16,3200]{2,1,0:T(8,128)(2,1)} %broadcast_in_dim.5), calls=%async_computation.1 | async-start | bytes 6553600 | tf_op jit(solution)/shard_map/all_to_all | solution.py:414
  14.1 38.0 %collective-permute-start.10 = (bf16[16,3072]{1,0:T(8,128)(2,1)S(1)}, bf16[16,3072]{1,0:T(8,128)(2,1)}, u32[]{:S(2)}, u32[]{:S(2)}) collective-permute-start(bf16[16,3072]{1,0:T(8,128)(2,1)S(1)} %copy-done.6), channel_id=1, source_target_pairs={{0,16},{1,17},{2,18},{3,19},{4,20},{5,21},{6,22},{7,23},{8,24},{9,... | collective-permute-start | bytes 294920 | tf_op jit(solution)/shard_map/ppermute | solution.py:33
  24.5 27.6 %copy-start.7 = (bf16[16,3072]{1,0:T(8,128)(2,1)S(1)}, bf16[16,3072]{1,0:T(8,128)(2,1)}, u32[]{:S(2)}) copy-start(bf16[16,3072]{1,0:T(8,128)(2,1)} %param.18) | copy-start | bytes 294916
  58.8 51.6 %all-to-all-start.2 = ((bf16[16,32,3072]{2,1,0:T(8,128)(2,1)}), bf16[16,32,3072]{2,1,0:T(8,128)(2,1)}, u32[]{:S(2)}, u32[]{:S(2)}) async-start(bf16[16,32,3072]{2,1,0:T(8,128)(2,1)} %broadcast_in_dim.7), calls=%async_computation.2 | async-start | bytes 6291456 | tf_op jit(solution)/shard_map/all_to_all | solution.py:41
  64.0 40.6 %slice-start = ((s8[4718592]{0:T(1024)(128)(4,1)}), s8[4194304]{0:T(1024)(128)(4,1)S(1)}, s32[]{:S(2)}) async-start(s8[4718592]{0:T(1024)(128)(4,1)} %bitcast.33), calls=%async_computation.6 | async-start | bytes 8388608 | tf_op jit(solution)/shard_map/cond
  64.0 40.6 %slice-start.1 = ((s8[4718592]{0:T(1024)(128)(4,1)}), s8[524288]{0:T(1024)(128)(4,1)S(1)}, s32[]{:S(2)}) async-start(s8[4718592]{0:T(1024)(128)(4,1)} %bitcast.33), calls=%async_computation.7 | async-start | bytes 1048576 | tf_op jit(solution)/shard_map/cond
  74.7 3.4 %collective-permute-start.3 = (f32[256,1536]{1,0:T(8,128)S(1)}, f32[256,1536]{1,0:T(8,128)S(1)}, u32[]{:S(2)}, u32[]{:S(2)}) collective-permute-start(f32[256,1536]{1,0:T(8,128)S(1)} %get-tuple-element.70), channel_id=1, source_target_pairs={{0,32},{32,0},{64,96},{96,64},{1,33},{33,1},{65,97},{97,65},{2,34}... | collective-permute-start | bytes 4718600 | tf_op jit(solution)/shard_map/cond/branch_1_fun/ppermute | solution.py:56
  78.4 21.5 %collective-permute-start.4 = (bf16[256,1536]{1,0:T(8,128)(2,1)S(1)}, bf16[256,1536]{1,0:T(8,128)(2,1)S(1)}, u32[]{:S(2)}, u32[]{:S(2)}) collective-permute-start(bf16[256,1536]{1,0:T(8,128)(2,1)S(1)} %get-tuple-element.185), channel_id=1, source_target_pairs={{0,64},{32,96},{64,0},{96,32},{1,65},{33,97},{65,1},{97,33},{2,66}... | collective-permute-start | bytes 2359304 | tf_op jit(solution)/shard_map/cond/branch_1_fun/ppermute | solution.py:60
  102.8 1.8 collective-permute-start.5
  110.3 49.2 %all-to-all-start.3 = ((bf16[16,32,3072]{2,1,0:T(8,128)(2,1)}), bf16[16,32,3072]{2,1,0:T(8,128)(2,1)}, u32[]{:S(2)}, u32[]{:S(2)}) async-start(bf16[16,32,3072]{2,1,0:T(8,128)(2,1)} %bitcast.17), calls=%async_computation.3 | async-start | bytes 6291456 | tf_op jit(solution)/shard_map/all_to_all | solution.py:41
  117.6 7.2 %copy-start.3 = (bf16[2,16,16,3200]{3,2,1,0:T(8,128)(2,1)}, bf16[2,16,16,3200]{3,2,1,0:T(8,128)(2,1)S(1)}, u32[]{:S(2)}) copy-start(bf16[2,16,16,3200]{3,2,1,0:T(8,128)(2,1)S(1)} %get-tuple-element.85.notes_ref) | copy-start | bytes 9830404 | tf_op jit(solution)/shard_map/cond
  124.8 2.6 collective-permute-start.7
  124.9 17.4 %collective-permute-start.6 = (f32[256,1536]{1,0:T(8,128)}, f32[256,1536]{1,0:T(8,128)S(1)}, u32[]{:S(2)}, u32[]{:S(2)}) collective-permute-start(f32[256,1536]{1,0:T(8,128)} %get-tuple-element.76.mine_ref), channel_id=1, source_target_pairs={{0,32},{32,0},{64,96},{96,64},{1,33},{33,1},{65,97},{97,65},{2,34}... | collective-permute-start | bytes 4718600 | tf_op jit(solution)/shard_map/cond/branch_1_fun/ppermute | solution.py:56
  127.4 12.7 %collective-permute-start.8 = (bf16[256,768]{1,0:T(8,128)(2,1)S(1)}, bf16[256,768]{1,0:T(8,128)(2,1)S(1)}, u32[]{:S(2)}, u32[]{:S(2)}) collective-permute-start(bf16[256,768]{1,0:T(8,128)(2,1)S(1)} %get-tuple-element.187), channel_id=1, source_target_pairs={{0,64},{32,96},{64,0},{96,32},{1,65},{33,97},{65,1},{97,33},{2,66}... | collective-permute-start | bytes 1179656 | tf_op jit(solution)/shard_map/cond/branch_1_fun/ppermute | solution.py:60
  140.2 2.4 collective-permute-start.9
  159.5 50.2 %all-to-all-start.4 = ((bf16[16,32,3072]{2,1,0:T(8,128)(2,1)}), bf16[16,32,3072]{2,1,0:T(8,128)(2,1)S(1)}, u32[]{:S(2)}, u32[]{:S(2)}) async-start(bf16[16,32,3072]{2,1,0:T(8,128)(2,1)} %bitcast.19), calls=%async_computation.4 | async-start | bytes 6291456 | tf_op jit(solution)/shard_map/all_to_all | solution.py:41
  173.6 34.5 %collective-permute-start.11 = (f32[16,3072]{1,0:T(8,128)}, f32[16,3072]{1,0:T(8,128)}, u32[]{:S(2)}, u32[]{:S(2)}) collective-permute-start(f32[16,3072]{1,0:T(8,128)} %slice.55), channel_id=1, source_target_pairs={{0,16},{1,17},{2,18},{3,19},{4,20},{5,21},{6,22},{7,23},{8,24},{9,... | collective-permute-start | bytes 589832 | tf_op jit(solution)/shard_map/ppermute | solution.py:33
  190.4 15.2 %collective-permute-start = (bf16[16,128,128]{2,1,0:T(8,128)(2,1)S(1)}, bf16[16,128,128]{2,1,0:T(8,128)(2,1)S(1)}, u32[]{:S(2)}, u32[]{:S(2)}) collective-permute-start(bf16[16,128,128]{2,1,0:T(8,128)(2,1)S(1)} %get-tuple-element.100), channel_id=1, source_target_pairs={{0,16},{1,17},{2,18},{3,19},{4,20},{5,21},{6,22},{7,23},{8,24},{9,... | collective-permute-start | bytes 1572872 | tf_op jit(solution)/shard_map/cond/branch_1_fun/ppermute | solution.py:33
  191.8 1.3 collective-permute-start.1
  193.7 11.4 %collective-permute-start.2 = (s32[1]{0:T(128)}, s32[1]{0:T(128)}, u32[]{:S(2)}, u32[]{:S(2)}) collective-permute-start(s32[1]{0:T(128)} %max.4), channel_id=1, source_target_pairs={{0,64},{32,96},{64,0},{96,32},{1,65},{33,97},{65,1},{97,33},{2,66}... | collective-permute-start | bytes 20 | tf_op jit(solution)/shard_map/cond/branch_1_fun/ppermute | solution.py:60
  209.8 85.3 %all-to-all-start.5 = ((bf16[192,128,128]{2,1,0:T(8,128)(2,1)}), bf16[192,128,128]{2,1,0:T(8,128)(2,1)}, u32[]{:S(2)}, u32[]{:S(2)}) async-start(bf16[192,128,128]{2,1,0:T(8,128)(2,1)} %get-tuple-element.173), calls=%async_computation.5 | async-start | bytes 12582912 | tf_op jit(solution)/shard_map/all_to_all | solution.py:455
  217.8 60.7 %collective-permute-start.12 = (f32[16,3072]{1,0:T(8,128)S(1)}, f32[16,3072]{1,0:T(8,128)S(1)}, u32[]{:S(2)}, u32[]{:S(2)}) collective-permute-start(f32[16,3072]{1,0:T(8,128)S(1)} %slice.57), channel_id=1, source_target_pairs={{0,16},{1,17},{2,18},{3,19},{4,20},{5,21},{6,22},{7,23},{8,24},{9,... | collective-permute-start | bytes 589832 | tf_op jit(solution)/shard_map/ppermute | solution.py:33
  (5 other events, 9.6 us)

commit v5 on v4

--- a/solution.py
+++ b/solution.py
@@ -94,53 +94,53 @@
     )(kept.reshape(-1), gate, up, down)
 
 
-def shares_kernel(reorder, core_ref, rows_ref, weight_ref, *out_refs):
-    keep_ref, send_ref = out_refs[:2]
-    half, feat = keep_ref.shape[0], out_refs[2].shape[1] if reorder else rows_ref.shape[1]
+def shares_kernel(reorder, core_ref, rows_ref, weight_ref, keep_ref, send_ref):
+    half = keep_ref.shape[0]
     if reorder:
-        rows = rows_ref.shape[2]
-
-        @pl.when(pl.program_id(0) == 0)
-        def _():
-            for chip in range(rows_ref.shape[1]):
-                for other in range(2):
-                    plane = core_ref[1] if other == 0 else 1 - core_ref[1]
-                    at = (2 * chip + other) * rows
-                    out_refs[2][at:at + rows, :] = rows_ref[plane, chip, :, :feat]
-
-        value = jnp.dot(out_refs[2][...], weight_ref[...], preferred_element_type=F32)
+        value = jnp.dot(rows_ref[...], weight_ref[...], preferred_element_type=F32)
     else:
-        value = contract_last(rows_ref[...], weight_ref[...])
+        value = contract_last(rows_ref[:, :weight_ref.shape[1]], weight_ref[...])
+
+    def put(out_ref, which):
+        if not reorder:
+            out_ref[...] = value[which * half:(which + 1) * half]
+            return
+        rows = reorder
+        chips = 2 * half // rows // 2
+        for chip in range(chips // 2):
+            for plane in range(2):
+                other = jnp.where(core_ref[1] == plane, 0, 1)
+                at = pl.multiple_of(2 * chip * rows + other * rows, rows)
+                start = (plane * chips + which * chips // 2 + chip) * rows
+                out_ref[pl.ds(at, rows), :] = value[start:start + rows]
 
     @pl.when(core_ref[0] == 0)
     def _():
-        keep_ref[...] = value[:half]
-        send_ref[...] = value[half:]
+        put(keep_ref, 0)
+        put(send_ref, 1)
 
     @pl.when(core_ref[0] != 0)
     def _():
-        keep_ref[...] = value[half:]
-        send_ref[...] = value[:half]
+        put(keep_ref, 1)
+        put(send_ref, 0)
 
 
 def shares(core, rows, weight, reorder):
-    vmem = pl.BlockSpec(memory_space=pltpu.VMEM)
     cut = 256
     if reorder:
-        (feat, wide), tokens = weight.shape, rows.shape[0] * rows.shape[1] * rows.shape[2]
+        feat, wide = weight.shape
         part = pl.BlockSpec((feat, cut), lambda i: (0, i))
     else:
-        (wide, feat), tokens = weight.shape, rows.shape[0]
+        wide, feat = weight.shape
         part = pl.BlockSpec((cut, feat), lambda i: (i, 0))
-    shape = jax.ShapeDtypeStruct((tokens // 2, wide), F32)
-    out = pl.BlockSpec((tokens // 2, cut), lambda i: (0, i))
-    more = reorder * (jax.ShapeDtypeStruct((tokens, feat), BF),)
+    shape = jax.ShapeDtypeStruct((rows.shape[0] // 2, wide), F32)
+    out = pl.BlockSpec((rows.shape[0] // 2, cut), lambda i: (0, i))
     return pl.pallas_call(
         functools.partial(shares_kernel, reorder),
         grid=(wide // cut,),
-        out_shape=(shape, shape) + more,
-        in_specs=[pl.BlockSpec(memory_space=pltpu.SMEM), vmem, part],
-        out_specs=(out, out) + reorder * (pl.BlockSpec((tokens, feat), lambda i: (0, 0)),),
+        out_shape=(shape, shape),
+        in_specs=[pl.BlockSpec(memory_space=pltpu.SMEM), pl.BlockSpec(memory_space=pltpu.VMEM), part],
+        out_specs=(out, out),
         compiler_params=pltpu.CompilerParams(vmem_limit_bytes=40 * 2**20),
     )(core, rows, weight)
 
@@ -193,7 +193,7 @@
 
 def grads_stage(core, sums, back, both):
     feat, wide = both.shape
-    cut = 512
+    cut = 1024
     rows = 2 * back[0].shape[0]
     vmem = pl.BlockSpec(memory_space=pltpu.VMEM)
     return pl.pallas_call(
@@ -210,7 +210,7 @@
     return lax.dot_general(left, right, (((0,), (0,)), ((), ())), preferred_element_type=F32)
 
 
-def pack_kernel(factor, brows, bcols, group, where_ref, hand_at_ref, x_ref, dy_ref, grads_ref, hidden_ref, main_ref, extra_ref, hand_ref, turned_ref, slots_ref, sems):
+def pack_kernel(factor, brows, bcols, group, core_ref, where_ref, hand_at_ref, x_ref, dy_ref, grads_ref, hidden_ref, main_ref, extra_ref, hand_ref, turned_ref, slots_ref, sems):
     cut = main_ref.shape[0]
     more = extra_ref.shape[0]
     wide = group * BLOCK
@@ -222,7 +222,9 @@
 
     def step(i, carry):
         lanes = pl.ds(pl.multiple_of(i * wide, wide), wide)
-        tile = (dot_rows(x_ref[:, lanes], grads_ref[...]) * factor).astype(BF)
+        planes = (core_ref[1], 1 - core_ref[1])
+        x = jnp.concatenate([x_ref[plane, chip, :, lanes] for chip in range(x_ref.shape[1]) for plane in planes], axis=0)
+        tile = (dot_rows(x, grads_ref[...]) * factor).astype(BF)
         for which in (0, 1):
             for u in range(group):
                 for f in range(bcols):
@@ -245,14 +247,14 @@
     second.wait()
 
 
-def pack_grads(where, hand_at, x_all, dy_all, grads, hidden, factor, brows, bcols, ncol):
+def pack_grads(core, where, hand_at, x_all, dy_all, grads, hidden, factor, brows, bcols, ncol):
     vmem = pl.BlockSpec(memory_space=pltpu.VMEM)
     smem = pl.BlockSpec(memory_space=pltpu.SMEM)
     far = pl.BlockSpec(memory_space=pl.ANY)
     return pl.pallas_call(
         functools.partial(pack_kernel, factor, brows, bcols, 4),
         out_shape=tuple(jax.ShapeDtypeStruct((n, BLOCK, BLOCK), BF) for n in (ncol * MAIN, ncol * EXTRA, HAND)),
-        in_specs=[smem, smem] + [vmem] * 4,
+        in_specs=[smem] * 3 + [vmem] * 4,
         out_specs=(far, far, vmem),
         scratch_shapes=[
             pltpu.VMEM((hidden.shape[1], hidden.shape[0]), BF),
@@ -260,7 +262,7 @@
             pltpu.SemaphoreType.DMA((2,)),
         ],
         compiler_params=pltpu.CompilerParams(vmem_limit_bytes=48 * 2**20),
-    )(where, hand_at, x_all, dy_all, grads, hidden)
+    )(core, where, hand_at, x_all, dy_all, grads, hidden)
 
 
 def insert_kernel(at_ref, got_ref, old_ref, main_ref, spare_ref, sem):
@@ -331,7 +333,9 @@
     def swapped(matrix):
         return jnp.concatenate([matrix[half:], matrix[:half]], axis=0)
 
-    note = notes_ref[...].astype(F32)[:, :, 0, :].reshape(ncol, LANES)
+    note = notes_ref[...].astype(F32)[:, :, 0, :]
+    own, other = note[:, 0], note[:, 1]
+    note = jnp.concatenate([jnp.where(place < half, own, other), jnp.where(place < half, other, own)], axis=0)
     turned = jnp.concatenate([note] * (LANES // ncol), axis=0).T.astype(jnp.int32)
     total, total_t = zero, zero
     weights = []
@@ -383,8 +387,8 @@
         direct_ref[m:m + 1, :] = jnp.where(slot < MAIN, near, ncol * MAIN + source * EXTRA + slot - MAIN)
 
 
-def index_tables(place, x_all, local, feat, ncol):
-    planes, chips, rows, _ = x_all.shape
+def index_tables(place, noted, local, feat, ncol):
+    chips, planes, rows, _ = noted.shape
     smem = pl.BlockSpec(memory_space=pltpu.SMEM)
     vmem = pl.BlockSpec(memory_space=pltpu.VMEM)
     wide = jax.ShapeDtypeStruct((1, LANES), jnp.int32)
@@ -393,9 +397,9 @@
         functools.partial(index_kernel, ncol),
         grid=(1,),
         out_shape=(jax.ShapeDtypeStruct(local.shape, jnp.int32), wide, wide, three, three, jax.ShapeDtypeStruct((1,), jnp.int32)),
-        in_specs=[smem, pl.BlockSpec((planes, chips, rows, LANES), lambda i: (0, 0, 0, feat // LANES)), vmem],
+        in_specs=[smem, pl.BlockSpec((chips, planes, rows, LANES), lambda i: (0, 0, 0, feat // LANES)), vmem],
         out_specs=(vmem,) * 5 + (smem,),
-    )(place.astype(jnp.int32).reshape(1), x_all, local)
+    )(place.astype(jnp.int32).reshape(1), noted, local)
 
 
 def shards(tokens, cotangent, gate_weight, up_weight, down_weight, kept, regrown):
@@ -411,26 +415,26 @@
     note = jnp.zeros((rows, LANES), BF).at[0, :3].set(tally.astype(BF))
     go = jnp.sum(tally) >= 0
 
-    x_all = lax.all_to_all(copies(jnp.concatenate([tokens, note], axis=1), ncol), "col", 0, 0, tiled=True)
+    x_all = lax.all_to_all(copies(tokens, ncol), "col", 0, 0, tiled=True)
     both, wd = mask_weights(kept, gate_weight, up_weight, down_weight)
-    joint = jnp.concatenate([cotangent, across(cotangent, ncol)], axis=0)
+    mine = jnp.concatenate([cotangent, note], axis=1)
+    joint = jnp.concatenate([mine, across(mine, ncol)], axis=0)
     flat = active.reshape(3, -1)
     local = jnp.where(flat > 0, jnp.cumsum(flat, axis=1) - 1, -1)
     local = jnp.pad(local, ((0, 5), (0, -flat.shape[1] % LANES)), constant_values=-1)
     x_all, both, wd, late, local = tie(x_all, both, wd, copies(joint, ncol // 2), local)
     dy_all = plane_exchange(late, ncol)
 
-    def forward(spread, both, wd):
-        keep, send, x_all = shares(core, spread, both, True)
-        gate_up = row_sum(keep, send)
+    def forward(x_all, both, wd):
+        gate_up = row_sum(*shares(core, x_all, both, rows))
         gate, up = gate_up[:, :hid], gate_up[:, hid:]
         hidden = (gate * jax.nn.sigmoid(gate) * up).astype(BF)
-        return gate_up, hidden_stage(core, hidden, swap_cores(hidden), wd), x_all
-
-    def backward(spread, local, dy_all, gate_up, both, wd):
-        tables = index_tables(place, spread, local, feat, ncol)
+        return gate_up, hidden_stage(core, hidden, swap_cores(hidden), wd)
+
+    def backward(local, dy_all, gate_up, both, wd):
+        tables = index_tables(place, dy_all.reshape(ncol // 2, 2, rows, -1), local, feat, ncol)
         gate_up_other = swap_cores(gate_up)
-        back = row_sum(*shares(core, dy_all, wd, False))
+        back = row_sum(*shares(core, dy_all, wd, 0))
         done = grads_stage(core, (gate_up, gate_up_other), (back, swap_cores(back)), both)
         return done, tables
 
@@ -438,15 +442,15 @@
         misfit = jnp.maximum(misfit, swap_cores(misfit))
         misfit = jnp.maximum(misfit, swap_far(misfit))[0]
         factor = float(rows * ncol) ** (-0.5)
-        main, extra, hand = pack_grads(send_at, hand_at, x_all, dy_all, grads, hidden, factor, brows, bcols, ncol)
+        spread = x_all.reshape(2, ncol // 2, rows, feat)
+        main, extra, hand = pack_grads(core, send_at, hand_at, spread, dy_all, grads, hidden, factor, brows, bcols, ncol)
         return insert_blocks(insert_at, across(hand, ncol), main), extra, misfit
 
-    spread = x_all.reshape(2, ncol // 2, rows, -1)
-    gate_up, (hidden, out_part), x_all = together(go, forward, spread, both, wd)
+    gate_up, (hidden, out_part) = together(go, forward, x_all, both, wd)
     dy_all, gate_up, out_part = tie(dy_all, gate_up, out_part)
     got_out = plane_exchange(out_part, ncol)
     (grads, in_part), (send_at, hand_at, insert_at, shared, direct, misfit) = together(
-        go, backward, spread, local, dy_all, gate_up, both, wd)
+        go, backward, local, dy_all, gate_up, both, wd)
     got_out, in_part = tie(got_out, in_part)
     got_in = plane_exchange(in_part, ncol)
     main, extra, misfit = together(go, blocks, send_at, hand_at, insert_at, misfit, x_all, dy_all, grads, hidden)

time: 303 us -> 302 us (level)
  Pallas kernels: 70.2 us -> 65.9 us
    unnamed x16 -> x28, local copies, waits for them, and re-layouts: 8.91 us -> 9.55 us
  transfers between devices with their start and end apart: 18 -> 18, of which waited for: 13 -> 14; matrix products, arithmetic and copies ran while one was open for 4% -> 5% of each run, Pallas kernels for 23% -> 21%
where the time goes in v5:
time: 302 us; the launch traced here: 299 us
  waiting for transfers between devices  137 us (45%)
  Pallas kernels  65.9 us (22%)
  starting transfers between devices  62.4 us (21%)
  local copies, waits for them, and re-layouts  17.3 us (6%)
  other arithmetic  12.6 us (4%)
    ppermute x4, waiting for transfers between devices, across(): lax.ppermute(value, 'col', [(i, (i + ncol // 2) % ncol) for i in range(nc...  73 us
    ppermute x3, waiting for transfers between devices, swap_far(): return lax.ppermute(value, 'row', [(0, 2), (1, 3), (2, 0), (3, 1)])  31.1 us
    all_to_all x3, starting transfers between devices, plane_exchange(): lax.all_to_all(value, 'col', 0, 0, axis_index_groups=plane_groups(ncol),...  23.2 us
    pallas_call x2, Pallas kernels, shares(): pl.pallas_call(functools.partial(shares_kernel, reorder), grid=(wide // c...  16 us
    ppermute x3, starting transfers between devices, swap_far(): return lax.ppermute(value, 'row', [(0, 2), (1, 3), (2, 0), (3, 1)])  14.7 us
    pallas_call x1, Pallas kernels, pack_grads(): pl.pallas_call(functools.partial(pack_kernel, factor, brows, bcols, 4), o...  14.5 us
    all_to_all x1, waiting for transfers between devices, shards(): got = lax.all_to_all(main, 'col', 0, 0, tiled=True)  13.5 us
    pallas_call x1, Pallas kernels, mask_weights(): pl.pallas_call(functools.partial(mask_kernel, bcols), grid=(feat // BLOCK...  13.4 us
  transfers between devices with their start and end apart: 18, of which 14 were waited for; matrix products, arithmetic and copies ran while one was open for 5% of the time, Pallas kernels for 21%

profile of v5, /device:TPU:2, one launch (start us, length us, event | category | flops | bytes accessed | tf_op | source)
XLA Modules:
  0.0 298.5 jit_solution(9692007104659802119)
XLA Ops:
  3.6 9.1 %all-to-all-start.1 = ((bf16[32,16,3072]{2,1,0:T(8,128)(2,1)}), bf16[32,16,3072]{2,1,0:T(8,128)(2,1)S(1)}, u32[]{:S(2)}, u32[]{:S(2)}) async-start(bf16[32,16,3072]{2,1,0:T(8,128)(2,1)} %broadcast_in_dim.5), calls=%async_computation.1 | async-start | bytes 6291456 | tf_op jit(solution)/shard_map/all_to_all | solution.py:418
  24.4 13.4 %shard_map.94 = (bf16[3072,1536]{1,0:T(8,128)(2,1)}, bf16[768,3072]{1,0:T(8,128)(2,1)}) custom-call(s32[432]{0:T(512)S(1)} %reshape.93.kept_ref, bf16[3072,768]{1,0:T(8,128)(2,1)S(1)} %copy-done, bf16[3072,768]{1,0:T(8,128)(2,1)S(1)} %copy-done.1, bf16[768,3072]{1,0:T(8,128)(2,1)S(1)} %copy-done.2), custom_call_target="tpu_custom_call" | custom-call | tf_op jit(solution)/shard_map/pallas_call | solution.py:87
  37.7 11.6 %collective-permute-done.10 = bf16[16,3200]{1,0:T(8,128)(2,1)S(1)} collective-permute-done((bf16[16,3200]{1,0:T(8,128)(2,1)S(1)}, bf16[16,3200]{1,0:T(8,128)(2,1)S(1)}, u32[]{:S(2)}, u32[]{:S(2)}) %collective-permute-start.10) | collective-permute-done | bytes 102432 | tf_op jit(solution)/shard_map/ppermute | solution.py:33
  49.4 4.1 %all-to-all-done.1 = bf16[32,16,3072]{2,1,0:T(8,128)(2,1)S(1)} async-done(((bf16[32,16,3072]{2,1,0:T(8,128)(2,1)}), bf16[32,16,3072]{2,1,0:T(8,128)(2,1)S(1)}, u32[]{:S(2)}, u32[]{:S(2)}) %all-to-all-start.1) | async-done | bytes 3145760 | tf_op jit(solution)/shard_map/all_to_all | solution.py:418
  56.2 4.8 %all-to-all-start.2 = ((bf16[16,32,3200]{2,1,0:T(8,128)(2,1)}), bf16[16,32,3200]{2,1,0:T(8,128)(2,1)S(1)}, u32[]{:S(2)}, u32[]{:S(2)}) async-start(bf16[16,32,3200]{2,1,0:T(8,128)(2,1)} %broadcast_in_dim.7), calls=%async_computation.2 | async-start | bytes 6553600 | tf_op jit(solution)/shard_map/all_to_all | solution.py:41
  61.8 45.6 %conditional.4 = (f32[256,1536]{1,0:T(8,128)}, bf16[512,768]{1,0:T(8,128)(2,1)}, bf16[512,3072]{1,0:T(8,128)(2,1)}) conditional(s32[]{:T(128)} %convert_element_type.54, () %tuple.49, (s32[2]{0:T(128)S(1)}, bf16[512,3072]{1,0:T(8,128)(2,1)}, bf16[3072,1536]{1,0:T(8,128)(2,1)}, bf16[768,3072]{1,0:T(8,128)(2,1)}) %tuple.79), branch_computations={%region_4.5_spmd, %region_5.6_spmd} | conditional | flops 2752512 | bytes 36569280 | solution.py:25
  61.8 9.8 %branch_1_fun.8 = (f32[256,1536]{1,0:T(8,128)S(1)}, f32[256,1536]{1,0:T(8,128)S(1)}) custom-call(s32[2]{0:T(128)S(1)} %get-tuple-element.66.core_ref, bf16[512,3072]{1,0:T(8,128)(2,1)} %get-tuple-element.67.rows_ref, bf16[3072,1536]{1,0:T(8,128)(2,1)} %get-tuple-element.68.weight_ref), custom_call_target="tpu_custom_call" | custom-call | tf_op jit(solution)/shard_map/cond/branch_1_fun/pallas_call | solution.py:138
  75.3 3.7 %collective-permute-start.4 = (bf16[256,1536]{1,0:T(8,128)(2,1)S(1)}, bf16[256,1536]{1,0:T(8,128)(2,1)S(1)}, u32[]{:S(2)}, u32[]{:S(2)}) collective-permute-start(bf16[256,1536]{1,0:T(8,128)(2,1)S(1)} %get-tuple-element.182), channel_id=1, source_target_pairs={{0,64},{32,96},{64,0},{96,32},{1,65},{33,97},{65,1},{97,33},{2,66}... | collective-permute-start | bytes 2359304 | tf_op jit(solution)/shard_map/cond/branch_1_fun/ppermute | solution.py:60
  79.0 17.8 %collective-permute-done.4 = bf16[256,1536]{1,0:T(8,128)(2,1)S(1)} collective-permute-done((bf16[256,1536]{1,0:T(8,128)(2,1)S(1)}, bf16[256,1536]{1,0:T(8,128)(2,1)S(1)}, u32[]{:S(2)}, u32[]{:S(2)}) %collective-permute-start.4) | collective-permute-done | bytes 786464 | tf_op jit(solution)/shard_map/cond/branch_1_fun/ppermute | solution.py:60
  101.7 5.7 %branch_1_fun.9 = (bf16[512,768]{1,0:T(8,128)(2,1)}, bf16[512,3072]{1,0:T(8,128)(2,1)}) custom-call(s32[2]{0:T(128)S(1)} %get-tuple-element.66.core_ref, bf16[256,768]{1,0:T(8,128)(2,1)S(1)} %fusion.mine_ref, bf16[256,768]{1,0:T(8,128)(2,1)S(1)} %collective-permute-done.5.other_ref, bf16[768,3072]{1,0:T(8,128)(2,1)S(1)} %bitcast.39), custom_call_target="tpu_custom_call" | custom-call | tf_op jit(solution)/shard_map/cond/branch_1_fun/pallas_call | solution.py:165
  107.4 7.2 %all-to-all-start.3 = ((bf16[16,32,3072]{2,1,0:T(8,128)(2,1)}), bf16[16,32,3072]{2,1,0:T(8,128)(2,1)}, u32[]{:S(2)}, u32[]{:S(2)}) async-start(bf16[16,32,3072]{2,1,0:T(8,128)(2,1)} %bitcast.18), calls=%async_computation.3 | async-start | bytes 6291456 | tf_op jit(solution)/shard_map/all_to_all | solution.py:41
  114.6 34.9 %conditional.5 = (bf16[512,1536]{1,0:T(8,128)(2,1)}, bf16[512,3072]{1,0:T(8,128)(2,1)}, s32[8,256]{1,0:T(8,128)S(1)}, s32[1,128]{1,0:T(1,128)}, s32[1,128]{1,0:T...) conditional(s32[]{:T(128)} %convert_element_type.54, () %tuple.52, (f32[256,1536]{1,0:T(8,128)}, ...), branch_computations={%region_6.7_spmd, %region_7.8_spmd} | conditional | flops 786432 | bytes 31981820 | solution.py:25
  114.7 6.2 %branch_1_fun.10 = (f32[256,768]{1,0:T(8,128)S(1)}, f32[256,768]{1,0:T(8,128)S(1)}) custom-call(s32[2]{0:T(128)S(1)} %get-tuple-element.74.core_ref, bf16[512,3200]{1,0:T(8,128)(2,1)S(1)} %get-tuple-element.76.rows_ref, bf16[768,3072]{1,0:T(8,128)(2,1)} %get-tuple-element.77.weight_ref), custom_call_target="tpu_custom_call" | custom-call | tf_op jit(solution)/shard_map/cond/branch_1_fun/pallas_call | solution.py:138
  126.8 9.4 %collective-permute-done.8 = bf16[256,768]{1,0:T(8,128)(2,1)S(1)} collective-permute-done((bf16[256,768]{1,0:T(8,128)(2,1)S(1)}, bf16[256,768]{1,0:T(8,128)(2,1)S(1)}, u32[]{:S(2)}, u32[]{:S(2)}) %collective-permute-start.8) | collective-permute-done | bytes 393248 | tf_op jit(solution)/shard_map/cond/branch_1_fun/ppermute | solution.py:60
  138.7 10.2 %branch_1_fun.11 = (bf16[512,1536]{1,0:T(8,128)(2,1)}, bf16[512,3072]{1,0:T(8,128)(2,1)}) custom-call(s32[2]{0:T(128)S(1)} %get-tuple-element.74.core_ref, f32[256,1536]{1,0:T(8,128)} %get-tuple-element.75.mine_ref, f32[256,1536]{1,0:T(8,128)S(1)} %collective-permute-done.6.other_ref, f32[256,768]{1,0:T(8,128)S(1)} %convert_add_fusion.1.back_ref, ...), custom_call_target="tpu_custom_call" | custom-call | tf_op jit(solution)/shard_map/cond/branch_1_fun/pallas_call | solution.py:199
  149.6 7.0 %all-to-all-done.3 = bf16[16,32,3072]{2,1,0:T(8,128)(2,1)} async-done(((bf16[16,32,3072]{2,1,0:T(8,128)(2,1)}), bf16[16,32,3072]{2,1,0:T(8,128)(2,1)}, u32[]{:S(2)}, u32[]{:S(2)}) %all-to-all-start.3) | async-done | bytes 3145760 | tf_op jit(solution)/shard_map/all_to_all | solution.py:41
  156.6 11.1 %all-to-all-start.4 = ((bf16[16,32,3072]{2,1,0:T(8,128)(2,1)}), bf16[16,32,3072]{2,1,0:T(8,128)(2,1)}, u32[]{:S(2)}, u32[]{:S(2)}) async-start(bf16[16,32,3072]{2,1,0:T(8,128)(2,1)} %bitcast.20), calls=%async_computation.4 | async-start | bytes 6291456 | tf_op jit(solution)/shard_map/all_to_all | solution.py:41
  172.2 31.9 %conditional.6 = (bf16[192,128,128]{2,1,0:T(8,128)(2,1)}, bf16[96,128,128]{2,1,0:T(8,128)(2,1)}, s32[]{:T(128)}) conditional(s32[]{:T(128)} %convert_element_type.54, () %tuple.55, (bf16[512,3072]{1,0:T(8,128)(2,1)S(1)}, s32[2]{0:T(128)}, s32[8,256]{1,0:T(8,128)S(1)}, s32[1,128]{1,0:T(1,128)}, bf16[512,3200]{1,0:T(8,128)(2,1)S(1)}, ...), branch_computations={%region_8.9_spmd, %region_9.10_spmd} | conditional | flops 2 | bytes 9437220 | solution.py:25
  172.2 14.5 %branch_1_fun.13 = (bf16[192,128,128]{2,1,0:T(8,128)(2,1)}, bf16[96,128,128]{2,1,0:T(8,128)(2,1)}, bf16[16,128,128]{2,1,0:T(8,128)(2,1)S(1)}) custom-call(s32[2]{0:T(128)} %get-tuple-element.92.core_ref, s32[8,256]{1,0:T(8,128)S(1)} %get-tuple-element.93.where_ref, s32[1,128]{1,0:T(1,128)} %get-tuple-element.94.hand_at_ref, ...), custom_call_target="tpu_custom_call" | custom-call | tf_op jit(solution)/shard_map/cond/branch_1_fun/pallas_call | solution.py:254
  189.5 7.7 %collective-permute-start.2 = (s32[1]{0:T(128)}, s32[1]{0:T(128)}, u32[]{:S(2)}, u32[]{:S(2)}) collective-permute-start(s32[1]{0:T(128)} %max.4), channel_id=1, source_target_pairs={{0,64},{32,96},{64,0},{96,32},{1,65},{33,97},{65,1},{97,33},{2,66}... | collective-permute-start | bytes 20 | tf_op jit(solution)/shard_map/cond/branch_1_fun/ppermute | solution.py:60
  197.2 3.8 %collective-permute-done.2 = s32[1]{0:T(128)} collective-permute-done((s32[1]{0:T(128)}, s32[1]{0:T(128)}, u32[]{:S(2)}, u32[]{:S(2)}) %collective-permute-start.2) | collective-permute-done | bytes 36 | tf_op jit(solution)/shard_map/cond/branch_1_fun/ppermute | solution.py:60
  206.2 8.3 %all-to-all-start.5 = ((bf16[192,128,128]{2,1,0:T(8,128)(2,1)}), bf16[192,128,128]{2,1,0:T(8,128)(2,1)}, u32[]{:S(2)}, u32[]{:S(2)}) async-start(bf16[192,128,128]{2,1,0:T(8,128)(2,1)} %get-tuple-element.170), calls=%async_computation.5 | async-start | bytes 12582912 | tf_op jit(solution)/shard_map/all_to_all | solution.py:459
  218.6 61.4 %collective-permute-done.12 = f32[16,3072]{1,0:T(8,128)S(1)} collective-permute-done((f32[16,3072]{1,0:T(8,128)S(1)}, f32[16,3072]{1,0:T(8,128)S(1)}, u32[]{:S(2)}, u32[]{:S(2)}) %collective-permute-start.12) | collective-permute-done | bytes 196640 | tf_op jit(solution)/shard_map/ppermute | solution.py:33
  280.7 13.5 %all-to-all-done.5 = bf16[192,128,128]{2,1,0:T(8,128)(2,1)} async-done(((bf16[192,128,128]{2,1,0:T(8,128)(2,1)}), bf16[192,128,128]{2,1,0:T(8,128)(2,1)}, u32[]{:S(2)}, u32[]{:S(2)}) %all-to-all-start.5) | async-done | bytes 6291488 | tf_op jit(solution)/shard_map/all_to_all | solution.py:459
  (95 shorter events, 57.3 us)
Async XLA Ops:
  3.6 9.1 %copy-start.14 = (s32[3,24,6]{1,2,0:T(8,128)S(1)}, s32[3,24,6]{1,2,0:T(8,128)}, u32[]{:S(2)}) copy-start(s32[3,24,6]{1,2,0:T(8,128)} %param.23) | copy-start | bytes 5188
  3.6 9.8 %copy-start.10 = (bf16[16,3072]{1,0:T(8,128)(2,1)S(1)}, bf16[16,3072]{1,0:T(8,128)(2,1)}, u32[]{:S(2)}) copy-start(bf16[16,3072]{1,0:T(8,128)(2,1)} %param.18) | copy-start | bytes 294916
  3.6 49.9 %all-to-all-start.1 = ((bf16[32,16,3072]{2,1,0:T(8,128)(2,1)}), bf16[32,16,3072]{2,1,0:T(8,128)(2,1)S(1)}, u32[]{:S(2)}, u32[]{:S(2)}) async-start(bf16[32,16,3072]{2,1,0:T(8,128)(2,1)} %broadcast_in_dim.5), calls=%async_computation.1 | async-start | bytes 6291456 | tf_op jit(solution)/shard_map/all_to_all | solution.py:418
  13.4 35.9 %collective-permute-start.10 = (bf16[16,3200]{1,0:T(8,128)(2,1)S(1)}, bf16[16,3200]{1,0:T(8,128)(2,1)S(1)}, u32[]{:S(2)}, u32[]{:S(2)}) collective-permute-start(bf16[16,3200]{1,0:T(8,128)(2,1)S(1)} %pad_maximum_fusion.2), channel_id=1, source_target_pairs={{0,16},{1,17},{2,18},{3,19},{4,20},{5,21},{6,22},{7,23},{8,24},{9,... | collective-permute-start | bytes 307208 | tf_op jit(solution)/shard_map/ppermute | solution.py:33
  56.2 51.2 %all-to-all-start.2 = ((bf16[16,32,3200]{2,1,0:T(8,128)(2,1)}), bf16[16,32,3200]{2,1,0:T(8,128)(2,1)S(1)}, u32[]{:S(2)}, u32[]{:S(2)}) async-start(bf16[16,32,3200]{2,1,0:T(8,128)(2,1)} %broadcast_in_dim.7), calls=%async_computation.2 | async-start | bytes 6553600 | tf_op jit(solution)/shard_map/all_to_all | solution.py:41
  61.8 52.9 %copy-start.13 = (s32[2]{0:T(128)}, s32[2]{0:T(128)S(1)}, u32[]{:S(2)}) copy-start(s32[2]{0:T(128)S(1)} %pad_add_fusion) | copy-start | bytes 28
  61.8 39.9 %slice-start = ((s8[4718592]{0:T(1024)(128)(4,1)}), s8[4194304]{0:T(1024)(128)(4,1)S(1)}, s32[]{:S(2)}) async-start(s8[4718592]{0:T(1024)(128)(4,1)} %bitcast.38), calls=%async_computation.6 | async-start | bytes 8388608 | tf_op jit(solution)/shard_map/cond
  61.8 39.9 %slice-start.1 = ((s8[4718592]{0:T(1024)(128)(4,1)}), s8[524288]{0:T(1024)(128)(4,1)S(1)}, s32[]{:S(2)}) async-start(s8[4718592]{0:T(1024)(128)(4,1)} %bitcast.38), calls=%async_computation.7 | async-start | bytes 1048576 | tf_op jit(solution)/shard_map/cond
  71.6 3.5 %collective-permute-start.3 = (f32[256,1536]{1,0:T(8,128)S(1)}, f32[256,1536]{1,0:T(8,128)S(1)}, u32[]{:S(2)}, u32[]{:S(2)}) collective-permute-start(f32[256,1536]{1,0:T(8,128)S(1)} %get-tuple-element.70), channel_id=1, source_target_pairs={{0,32},{32,0},{64,96},{96,64},{1,33},{33,1},{65,97},{97,65},{2,34}... | collective-permute-start | bytes 4718600 | tf_op jit(solution)/shard_map/cond/branch_1_fun/ppermute | solution.py:56
  75.3 21.5 %collective-permute-start.4 = (bf16[256,1536]{1,0:T(8,128)(2,1)S(1)}, bf16[256,1536]{1,0:T(8,128)(2,1)S(1)}, u32[]{:S(2)}, u32[]{:S(2)}) collective-permute-start(bf16[256,1536]{1,0:T(8,128)(2,1)S(1)} %get-tuple-element.182), channel_id=1, source_target_pairs={{0,64},{32,96},{64,0},{96,32},{1,65},{33,97},{65,1},{97,33},{2,66}... | collective-permute-start | bytes 2359304 | tf_op jit(solution)/shard_map/cond/branch_1_fun/ppermute | solution.py:60
  99.9 1.8 collective-permute-start.5
  107.4 49.2 %all-to-all-start.3 = ((bf16[16,32,3072]{2,1,0:T(8,128)(2,1)}), bf16[16,32,3072]{2,1,0:T(8,128)(2,1)}, u32[]{:S(2)}, u32[]{:S(2)}) async-start(bf16[16,32,3072]{2,1,0:T(8,128)(2,1)} %bitcast.18), calls=%async_computation.3 | async-start | bytes 6291456 | tf_op jit(solution)/shard_map/all_to_all | solution.py:41
  120.9 2.6 collective-permute-start.7
  121.0 17.4 %collective-permute-start.6 = (f32[256,1536]{1,0:T(8,128)}, f32[256,1536]{1,0:T(8,128)S(1)}, u32[]{:S(2)}, u32[]{:S(2)}) collective-permute-start(f32[256,1536]{1,0:T(8,128)} %get-tuple-element.75.mine_ref), channel_id=1, source_target_pairs={{0,32},{32,0},{64,96},{96,64},{1,33},{33,1},{65,97},{97,65},{2,34}... | collective-permute-start | bytes 4718600 | tf_op jit(solution)/shard_map/cond/branch_1_fun/ppermute | solution.py:56
  123.5 12.7 %collective-permute-start.8 = (bf16[256,768]{1,0:T(8,128)(2,1)S(1)}, bf16[256,768]{1,0:T(8,128)(2,1)S(1)}, u32[]{:S(2)}, u32[]{:S(2)}) collective-permute-start(bf16[256,768]{1,0:T(8,128)(2,1)S(1)} %get-tuple-element.184), channel_id=1, source_target_pairs={{0,64},{32,96},{64,0},{96,32},{1,65},{33,97},{65,1},{97,33},{2,66}... | collective-permute-start | bytes 1179656 | tf_op jit(solution)/shard_map/cond/branch_1_fun/ppermute | solution.py:60
  136.3 2.4 collective-permute-start.9
  156.6 15.7 %copy-start.7 = (bf16[32,16,3072]{2,1,0:T(8,128)(2,1)S(1)}, bf16[32,16,3072]{2,1,0:T(8,128)(2,1)}, u32[]{:S(2)}) copy-start(bf16[32,16,3072]{2,1,0:T(8,128)(2,1)} %copy-done.6) | copy-start | bytes 9437188
  156.6 49.6 %all-to-all-start.4 = ((bf16[16,32,3072]{2,1,0:T(8,128)(2,1)}), bf16[16,32,3072]{2,1,0:T(8,128)(2,1)}, u32[]{:S(2)}, u32[]{:S(2)}) async-start(bf16[16,32,3072]{2,1,0:T(8,128)(2,1)} %bitcast.20), calls=%async_computation.4 | async-start | bytes 6291456 | tf_op jit(solution)/shard_map/all_to_all | solution.py:41
  171.0 33.1 %collective-permute-start.11 = (f32[16,3072]{1,0:T(8,128)}, f32[16,3072]{1,0:T(8,128)}, u32[]{:S(2)}, u32[]{:S(2)}) collective-permute-start(f32[16,3072]{1,0:T(8,128)} %slice.55), channel_id=1, source_target_pairs={{0,16},{1,17},{2,18},{3,19},{4,20},{5,21},{6,22},{7,23},{8,24},{9,... | collective-permute-start | bytes 589832 | tf_op jit(solution)/shard_map/ppermute | solution.py:33
  186.8 14.8 %collective-permute-start = (bf16[16,128,128]{2,1,0:T(8,128)(2,1)S(1)}, bf16[16,128,128]{2,1,0:T(8,128)(2,1)S(1)}, u32[]{:S(2)}, u32[]{:S(2)}) collective-permute-start(bf16[16,128,128]{2,1,0:T(8,128)(2,1)S(1)} %get-tuple-element.99), channel_id=1, source_target_pairs={{0,16},{1,17},{2,18},{3,19},{4,20},{5,21},{6,22},{7,23},{8,24},{9,... | collective-permute-start | bytes 1572872 | tf_op jit(solution)/shard_map/cond/branch_1_fun/ppermute | solution.py:33
  187.7 1.3 collective-permute-start.1
  189.5 11.5 %collective-permute-start.2 = (s32[1]{0:T(128)}, s32[1]{0:T(128)}, u32[]{:S(2)}, u32[]{:S(2)}) collective-permute-start(s32[1]{0:T(128)} %max.4), channel_id=1, source_target_pairs={{0,64},{32,96},{64,0},{96,32},{1,65},{33,97},{65,1},{97,33},{2,66}... | collective-permute-start | bytes 20 | tf_op jit(solution)/shard_map/cond/branch_1_fun/ppermute | solution.py:60
  206.2 88.0 %all-to-all-start.5 = ((bf16[192,128,128]{2,1,0:T(8,128)(2,1)}), bf16[192,128,128]{2,1,0:T(8,128)(2,1)}, u32[]{:S(2)}, u32[]{:S(2)}) async-start(bf16[192,128,128]{2,1,0:T(8,128)(2,1)} %get-tuple-element.170), calls=%async_computation.5 | async-start | bytes 12582912 | tf_op jit(solution)/shard_map/all_to_all | solution.py:459
  217.0 63.1 %collective-permute-start.12 = (f32[16,3072]{1,0:T(8,128)S(1)}, f32[16,3072]{1,0:T(8,128)S(1)}, u32[]{:S(2)}, u32[]{:S(2)}) collective-permute-start(f32[16,3072]{1,0:T(8,128)S(1)} %slice.57), channel_id=1, source_target_pairs={{0,16},{1,17},{2,18},{3,19},{4,20},{5,21},{6,22},{7,23},{8,24},{9,... | collective-permute-start | bytes 589832 | tf_op jit(solution)/shard_map/ppermute | solution.py:33
  (11 other events, 46.7 us)

commit v6 on v5

--- a/solution.py
+++ b/solution.py
@@ -41,11 +41,12 @@
     return lax.all_to_all(value, "col", 0, 0, axis_index_groups=plane_groups(ncol), tiled=True)
 
 
-def add_parts(got, ncol):
+def add_parts(parts, ncol):
     many = ncol // 2
-    total = jnp.sum(got.reshape(many, got.shape[0] // many, -1).astype(F32), axis=0)
-    rows = total.shape[0] // 2
-    return (total[:rows] + across(total[rows:], ncol)).astype(BF)
+    sums = [jnp.sum(got.reshape(many, got.shape[0] // many, -1).astype(F32), axis=0) for got in parts]
+    rows = sums[0].shape[0] // 2
+    came = across(jnp.concatenate([total[rows:].astype(BF) for total in sums], axis=0), ncol).astype(F32)
+    return [(total[:rows] + came[i * rows:(i + 1) * rows]).astype(BF) for i, total in enumerate(sums)]
 
 
 def tie(*values):
@@ -454,10 +455,9 @@
     got_out, in_part = tie(got_out, in_part)
     got_in = plane_exchange(in_part, ncol)
     main, extra, misfit = together(go, blocks, send_at, hand_at, insert_at, misfit, x_all, dy_all, grads, hidden)
-    output = add_parts(got_out, ncol)
-    got_in, main, extra, output, misfit = tie(got_in, main, extra, output, misfit)
+    got_in, main, extra, got_out, misfit = tie(got_in, main, extra, got_out, misfit)
     got = lax.all_to_all(main, "col", 0, 0, tiled=True)
-    input_grad = add_parts(got_in, ncol)
+    output, input_grad = add_parts([got_out, got_in], ncol)
 
     def with_extra():
         more = lax.all_to_all(extra, "col", 0, 0, tiled=True)

time: 302 us -> 302 us (level)
  waiting for transfers between devices: 137 us -> 142 us
    all_to_all x1, waiting for transfers between devices: 13.5 us -> 19.8 us  [shards(): got = lax.all_to_all(main, 'col', 0, 0, tiled=True)]
    ppermute x4 -> x3, waiting for transfers between devices: 73 us -> 66.9 us  [across(): lax.ppermute(value, 'col', [(i, (i + ncol // 2) % ncol) for i in range(nc...]
    all_to_all x3, waiting for transfers between devices: 7.45 us -> 11.8 us  [plane_exchange(): lax.all_to_all(value, 'col', 0, 0, axis_index_groups=plane_groups(ncol),...]
    unnamed x28 -> x24, local copies, waits for them, and re-layouts: 9.55 us -> 9.58 us
  transfers between devices with their start and end apart: 18 -> 17, of which waited for: 14 -> 14; matrix products, arithmetic and copies ran while one was open for 5% -> 4% of each run, Pallas kernels for 21% -> 21%
where the time goes in v6:
time: 302 us; the launch traced here: 301 us
  waiting for transfers between devices  142 us (47%)
  Pallas kernels  66.7 us (22%)
  starting transfers between devices  61.8 us (20%)
  local copies, waits for them, and re-layouts  16.7 us (6%)
  other arithmetic  9.93 us (3%)
    ppermute x3, waiting for transfers between devices, across(): lax.ppermute(value, 'col', [(i, (i + ncol // 2) % ncol) for i in range(nc...  66.9 us
    ppermute x3, waiting for transfers between devices, swap_far(): return lax.ppermute(value, 'row', [(0, 2), (1, 3), (2, 0), (3, 1)])  31.3 us
    all_to_all x3, starting transfers between devices, plane_exchange(): lax.all_to_all(value, 'col', 0, 0, axis_index_groups=plane_groups(ncol),...  23.3 us
    all_to_all x1, waiting for transfers between devices, shards(): got = lax.all_to_all(main, 'col', 0, 0, tiled=True)  19.8 us
    pallas_call x2, Pallas kernels, shares(): pl.pallas_call(functools.partial(shares_kernel, reorder), grid=(wide // c...  16 us
    pallas_call x1, Pallas kernels, pack_grads(): pl.pallas_call(functools.partial(pack_kernel, factor, brows, bcols, 4), o...  15.5 us
    ppermute x3, starting transfers between devices, swap_far(): return lax.ppermute(value, 'row', [(0, 2), (1, 3), (2, 0), (3, 1)])  15 us
    pallas_call x1, Pallas kernels, mask_weights(): pl.pallas_call(functools.partial(mask_kernel, bcols), grid=(feat // BLOCK...  13.5 us
  transfers between devices with their start and end apart: 17, of which 14 were waited for; matrix products, arithmetic and copies ran while one was open for 4% of the time, Pallas kernels for 21%

profile of v6, /device:TPU:2, one launch (start us, length us, event | category | flops | bytes accessed | tf_op | source)
XLA Modules:
  0.0 300.5 jit_solution(8363948566963230754)
XLA Ops:
  3.6 9.1 %all-to-all-start.1 = ((bf16[32,16,3072]{2,1,0:T(8,128)(2,1)}), bf16[32,16,3072]{2,1,0:T(8,128)(2,1)S(1)}, u32[]{:S(2)}, u32[]{:S(2)}) async-start(bf16[32,16,3072]{2,1,0:T(8,128)(2,1)} %broadcast_in_dim.5), calls=%async_computation.1 | async-start | bytes 6291456 | tf_op jit(solution)/shard_map/all_to_all | solution.py:419
  24.4 13.5 %shard_map.94 = (bf16[3072,1536]{1,0:T(8,128)(2,1)}, bf16[768,3072]{1,0:T(8,128)(2,1)}) custom-call(s32[432]{0:T(512)S(1)} %reshape.93.kept_ref, bf16[3072,768]{1,0:T(8,128)(2,1)S(1)} %copy-done, bf16[3072,768]{1,0:T(8,128)(2,1)S(1)} %copy-done.1, bf16[768,3072]{1,0:T(8,128)(2,1)S(1)} %copy-done.2), custom_call_target="tpu_custom_call" | custom-call | tf_op jit(solution)/shard_map/pallas_call | solution.py:88
  37.9 11.4 %collective-permute-done.10 = bf16[16,3200]{1,0:T(8,128)(2,1)S(1)} collective-permute-done((bf16[16,3200]{1,0:T(8,128)(2,1)S(1)}, bf16[16,3200]{1,0:T(8,128)(2,1)S(1)}, u32[]{:S(2)}, u32[]{:S(2)}) %collective-permute-start.10) | collective-permute-done | bytes 102432 | tf_op jit(solution)/shard_map/ppermute | solution.py:33
  49.4 4.1 %all-to-all-done.1 = bf16[32,16,3072]{2,1,0:T(8,128)(2,1)S(1)} async-done(((bf16[32,16,3072]{2,1,0:T(8,128)(2,1)}), bf16[32,16,3072]{2,1,0:T(8,128)(2,1)S(1)}, u32[]{:S(2)}, u32[]{:S(2)}) %all-to-all-start.1) | async-done | bytes 3145760 | tf_op jit(solution)/shard_map/all_to_all | solution.py:419
  56.2 4.8 %all-to-all-start.2 = ((bf16[16,32,3200]{2,1,0:T(8,128)(2,1)}), bf16[16,32,3200]{2,1,0:T(8,128)(2,1)S(1)}, u32[]{:S(2)}, u32[]{:S(2)}) async-start(bf16[16,32,3200]{2,1,0:T(8,128)(2,1)} %broadcast_in_dim.7), calls=%async_computation.2 | async-start | bytes 6553600 | tf_op jit(solution)/shard_map/all_to_all | solution.py:41
  61.8 45.5 %conditional.4 = (f32[256,1536]{1,0:T(8,128)}, bf16[512,768]{1,0:T(8,128)(2,1)}, bf16[512,3072]{1,0:T(8,128)(2,1)}) conditional(s32[]{:T(128)} %convert_element_type.59, () %tuple.49, (s32[2]{0:T(128)S(1)}, bf16[512,3072]{1,0:T(8,128)(2,1)}, bf16[3072,1536]{1,0:T(8,128)(2,1)}, bf16[768,3072]{1,0:T(8,128)(2,1)}) %tuple.81), branch_computations={%region_4.5_spmd, %region_5.6_spmd} | conditional | flops 2752512 | bytes 36569280 | solution.py:25
  61.8 9.8 %branch_1_fun.8 = (f32[256,1536]{1,0:T(8,128)S(1)}, f32[256,1536]{1,0:T(8,128)S(1)}) custom-call(s32[2]{0:T(128)S(1)} %get-tuple-element.66.core_ref, bf16[512,3072]{1,0:T(8,128)(2,1)} %get-tuple-element.67.rows_ref, bf16[3072,1536]{1,0:T(8,128)(2,1)} %get-tuple-element.68.weight_ref), custom_call_target="tpu_custom_call" | custom-call | tf_op jit(solution)/shard_map/cond/branch_1_fun/pallas_call | solution.py:139
  79.0 17.8 %collective-permute-done.4 = bf16[256,1536]{1,0:T(8,128)(2,1)S(1)} collective-permute-done((bf16[256,1536]{1,0:T(8,128)(2,1)S(1)}, bf16[256,1536]{1,0:T(8,128)(2,1)S(1)}, u32[]{:S(2)}, u32[]{:S(2)}) %collective-permute-start.4) | collective-permute-done | bytes 786464 | tf_op jit(solution)/shard_map/cond/branch_1_fun/ppermute | solution.py:61
  101.6 5.6 %branch_1_fun.9 = (bf16[512,768]{1,0:T(8,128)(2,1)}, bf16[512,3072]{1,0:T(8,128)(2,1)}) custom-call(s32[2]{0:T(128)S(1)} %get-tuple-element.66.core_ref, bf16[256,768]{1,0:T(8,128)(2,1)S(1)} %fusion.mine_ref, bf16[256,768]{1,0:T(8,128)(2,1)S(1)} %collective-permute-done.5.other_ref, bf16[768,3072]{1,0:T(8,128)(2,1)S(1)} %bitcast.39), custom_call_target="tpu_custom_call" | custom-call | tf_op jit(solution)/shard_map/cond/branch_1_fun/pallas_call | solution.py:166
  107.3 7.2 %all-to-all-start.3 = ((bf16[16,32,3072]{2,1,0:T(8,128)(2,1)}), bf16[16,32,3072]{2,1,0:T(8,128)(2,1)}, u32[]{:S(2)}, u32[]{:S(2)}) async-start(bf16[16,32,3072]{2,1,0:T(8,128)(2,1)} %bitcast.18), calls=%async_computation.3 | async-start | bytes 6291456 | tf_op jit(solution)/shard_map/all_to_all | solution.py:41
  114.5 34.8 %conditional.5 = (bf16[512,1536]{1,0:T(8,128)(2,1)}, bf16[512,3072]{1,0:T(8,128)(2,1)}, s32[8,256]{1,0:T(8,128)S(1)}, s32[1,128]{1,0:T(1,128)S(1)}, s32[1,128]{1...) conditional(s32[]{:T(128)} %convert_element_type.59, () %tuple.52, ...), branch_computations={%region_6.7_spmd, %region_7.8_spmd} | conditional | flops 786432 | bytes 31981820 | solution.py:25
  114.6 6.2 %branch_1_fun.10 = (f32[256,768]{1,0:T(8,128)S(1)}, f32[256,768]{1,0:T(8,128)S(1)}) custom-call(s32[2]{0:T(128)S(1)} %get-tuple-element.74.core_ref, bf16[512,3200]{1,0:T(8,128)(2,1)S(1)} %get-tuple-element.76.rows_ref, bf16[768,3072]{1,0:T(8,128)(2,1)} %get-tuple-element.77.weight_ref), custom_call_target="tpu_custom_call" | custom-call | tf_op jit(solution)/shard_map/cond/branch_1_fun/pallas_call | solution.py:139
  126.7 9.4 %collective-permute-done.8 = bf16[256,768]{1,0:T(8,128)(2,1)S(1)} collective-permute-done((bf16[256,768]{1,0:T(8,128)(2,1)S(1)}, bf16[256,768]{1,0:T(8,128)(2,1)S(1)}, u32[]{:S(2)}, u32[]{:S(2)}) %collective-permute-start.8) | collective-permute-done | bytes 393248 | tf_op jit(solution)/shard_map/cond/branch_1_fun/ppermute | solution.py:61
  138.6 10.1 %branch_1_fun.11 = (bf16[512,1536]{1,0:T(8,128)(2,1)}, bf16[512,3072]{1,0:T(8,128)(2,1)}) custom-call(s32[2]{0:T(128)S(1)} %get-tuple-element.74.core_ref, f32[256,1536]{1,0:T(8,128)} %get-tuple-element.75.mine_ref, f32[256,1536]{1,0:T(8,128)S(1)} %collective-permute-done.6.other_ref, f32[256,768]{1,0:T(8,128)S(1)} %convert_add_fusion.1.back_ref, ...), custom_call_target="tpu_custom_call" | custom-call | tf_op jit(solution)/shard_map/cond/branch_1_fun/pallas_call | solution.py:200
  149.3 7.1 %all-to-all-done.3 = bf16[16,32,3072]{2,1,0:T(8,128)(2,1)} async-done(((bf16[16,32,3072]{2,1,0:T(8,128)(2,1)}), bf16[16,32,3072]{2,1,0:T(8,128)(2,1)}, u32[]{:S(2)}, u32[]{:S(2)}) %all-to-all-start.3) | async-done | bytes 3145760 | tf_op jit(solution)/shard_map/all_to_all | solution.py:41
  156.5 11.2 %all-to-all-start.4 = ((bf16[16,32,3072]{2,1,0:T(8,128)(2,1)}), bf16[16,32,3072]{2,1,0:T(8,128)(2,1)}, u32[]{:S(2)}, u32[]{:S(2)}) async-start(bf16[16,32,3072]{2,1,0:T(8,128)(2,1)} %bitcast.20), calls=%async_computation.4 | async-start | bytes 6291456 | tf_op jit(solution)/shard_map/all_to_all | solution.py:41
  167.6 33.8 %conditional.6 = (bf16[192,128,128]{2,1,0:T(8,128)(2,1)}, bf16[96,128,128]{2,1,0:T(8,128)(2,1)}, s32[]{:T(128)}) conditional(s32[]{:T(128)} %convert_element_type.59, () %tuple.55, (bf16[512,3072]{1,0:T(8,128)(2,1)}, s32[2]{0:T(128)S(1)}, s32[8,256]{1,0:T(8,128)S(1)}, s32[1,128]{1,0:T(1,128)S(1)}, bf16[512,3200]{1,0:T(8,128)(2,1)S(1)}, ...), branch_computations={%region_8.9_spmd, %region_9.10_spmd} | conditional | flops 2 | bytes 9437220 | solution.py:25
  167.8 15.5 %branch_1_fun.13 = (bf16[192,128,128]{2,1,0:T(8,128)(2,1)}, bf16[96,128,128]{2,1,0:T(8,128)(2,1)}, bf16[16,128,128]{2,1,0:T(8,128)(2,1)S(1)}) custom-call(s32[2]{0:T(128)S(1)} %get-tuple-element.92.core_ref, s32[8,256]{1,0:T(8,128)S(1)} %get-tuple-element.93.where_ref, s32[1,128]{1,0:T(1,128)S(1)} %get-tuple-element.94.hand_at_ref, ...), custom_call_target="tpu_custom_call" | custom-call | tf_op jit(solution)/shard_map/cond/branch_1_fun/pallas_call | solution.py:255
  186.3 8.0 %collective-permute-start.2 = (s32[1]{0:T(128)}, s32[1]{0:T(128)}, u32[]{:S(2)}, u32[]{:S(2)}) collective-permute-start(s32[1]{0:T(128)} %max.4), channel_id=1, source_target_pairs={{0,64},{32,96},{64,0},{96,32},{1,65},{33,97},{65,1},{97,33},{2,66}... | collective-permute-start | bytes 20 | tf_op jit(solution)/shard_map/cond/branch_1_fun/ppermute | solution.py:61
  194.4 4.0 %collective-permute-done.2 = s32[1]{0:T(128)} collective-permute-done((s32[1]{0:T(128)}, s32[1]{0:T(128)}, u32[]{:S(2)}, u32[]{:S(2)}) %collective-permute-start.2) | collective-permute-done | bytes 36 | tf_op jit(solution)/shard_map/cond/branch_1_fun/ppermute | solution.py:61
  201.4 4.7 %all-to-all-done.4 = bf16[16,32,3072]{2,1,0:T(8,128)(2,1)} async-done(((bf16[16,32,3072]{2,1,0:T(8,128)(2,1)}), bf16[16,32,3072]{2,1,0:T(8,128)(2,1)}, u32[]{:S(2)}, u32[]{:S(2)}) %all-to-all-start.4) | async-done | bytes 3145760 | tf_op jit(solution)/shard_map/all_to_all | solution.py:41
  206.1 8.3 %all-to-all-start.5 = ((bf16[192,128,128]{2,1,0:T(8,128)(2,1)}), bf16[192,128,128]{2,1,0:T(8,128)(2,1)}, u32[]{:S(2)}, u32[]{:S(2)}) async-start(bf16[192,128,128]{2,1,0:T(8,128)(2,1)} %get-tuple-element.170), calls=%async_computation.5 | async-start | bytes 12582912 | tf_op jit(solution)/shard_map/all_to_all | solution.py:459
  220.1 55.5 %collective-permute-done.11 = bf16[32,3072]{1,0:T(8,128)(2,1)S(1)} collective-permute-done((bf16[32,3072]{1,0:T(8,128)(2,1)S(1)}, bf16[32,3072]{1,0:T(8,128)(2,1)S(1)}, u32[]{:S(2)}, u32[]{:S(2)}) %collective-permute-start.11) | collective-permute-done | bytes 196640 | tf_op jit(solution)/shard_map/ppermute | solution.py:33
  276.3 19.8 %all-to-all-done.5 = bf16[192,128,128]{2,1,0:T(8,128)(2,1)} async-done(((bf16[192,128,128]{2,1,0:T(8,128)(2,1)}), bf16[192,128,128]{2,1,0:T(8,128)(2,1)}, u32[]{:S(2)}, u32[]{:S(2)}) %all-to-all-start.5) | async-done | bytes 6291488 | tf_op jit(solution)/shard_map/all_to_all | solution.py:459
  (89 shorter events, 56.0 us)
Async XLA Ops:
  3.6 9.1 %copy-start.10 = (s32[3,24,6]{1,2,0:T(8,128)S(1)}, s32[3,24,6]{1,2,0:T(8,128)}, u32[]{:S(2)}) copy-start(s32[3,24,6]{1,2,0:T(8,128)} %param.22) | copy-start | bytes 5188
  3.6 9.1 %copy-start.12 = (s32[3,24,6]{1,2,0:T(8,128)S(1)}, s32[3,24,6]{1,2,0:T(8,128)}, u32[]{:S(2)}) copy-start(s32[3,24,6]{1,2,0:T(8,128)} %param.23) | copy-start | bytes 5188
  3.6 9.8 %copy-start.9 = (bf16[16,3072]{1,0:T(8,128)(2,1)S(1)}, bf16[16,3072]{1,0:T(8,128)(2,1)}, u32[]{:S(2)}) copy-start(bf16[16,3072]{1,0:T(8,128)(2,1)} %param.18) | copy-start | bytes 294916
  3.6 49.9 %all-to-all-start.1 = ((bf16[32,16,3072]{2,1,0:T(8,128)(2,1)}), bf16[32,16,3072]{2,1,0:T(8,128)(2,1)S(1)}, u32[]{:S(2)}, u32[]{:S(2)}) async-start(bf16[32,16,3072]{2,1,0:T(8,128)(2,1)} %broadcast_in_dim.5), calls=%async_computation.1 | async-start | bytes 6291456 | tf_op jit(solution)/shard_map/all_to_all | solution.py:419
  13.4 35.9 %collective-permute-start.10 = (bf16[16,3200]{1,0:T(8,128)(2,1)S(1)}, bf16[16,3200]{1,0:T(8,128)(2,1)S(1)}, u32[]{:S(2)}, u32[]{:S(2)}) collective-permute-start(bf16[16,3200]{1,0:T(8,128)(2,1)S(1)} %pad_maximum_fusion.3), channel_id=1, source_target_pairs={{0,16},{1,17},{2,18},{3,19},{4,20},{5,21},{6,22},{7,23},{8,24},{9,... | collective-permute-start | bytes 307208 | tf_op jit(solution)/shard_map/ppermute | solution.py:33
  56.2 51.0 %all-to-all-start.2 = ((bf16[16,32,3200]{2,1,0:T(8,128)(2,1)}), bf16[16,32,3200]{2,1,0:T(8,128)(2,1)S(1)}, u32[]{:S(2)}, u32[]{:S(2)}) async-start(bf16[16,32,3200]{2,1,0:T(8,128)(2,1)} %broadcast_in_dim.7), calls=%async_computation.2 | async-start | bytes 6553600 | tf_op jit(solution)/shard_map/all_to_all | solution.py:41
  61.8 39.8 %slice-start = ((s8[4718592]{0:T(1024)(128)(4,1)}), s8[4194304]{0:T(1024)(128)(4,1)S(1)}, s32[]{:S(2)}) async-start(s8[4718592]{0:T(1024)(128)(4,1)} %bitcast.38), calls=%async_computation.6 | async-start | bytes 8388608 | tf_op jit(solution)/shard_map/cond
  61.8 39.8 %slice-start.1 = ((s8[4718592]{0:T(1024)(128)(4,1)}), s8[524288]{0:T(1024)(128)(4,1)S(1)}, s32[]{:S(2)}) async-start(s8[4718592]{0:T(1024)(128)(4,1)} %bitcast.38), calls=%async_computation.7 | async-start | bytes 1048576 | tf_op jit(solution)/shard_map/cond
  71.6 3.5 %collective-permute-start.3 = (f32[256,1536]{1,0:T(8,128)S(1)}, f32[256,1536]{1,0:T(8,128)S(1)}, u32[]{:S(2)}, u32[]{:S(2)}) collective-permute-start(f32[256,1536]{1,0:T(8,128)S(1)} %get-tuple-element.70), channel_id=1, source_target_pairs={{0,32},{32,0},{64,96},{96,64},{1,33},{33,1},{65,97},{97,65},{2,34}... | collective-permute-start | bytes 4718600 | tf_op jit(solution)/shard_map/cond/branch_1_fun/ppermute | solution.py:57
  75.3 21.5 %collective-permute-start.4 = (bf16[256,1536]{1,0:T(8,128)(2,1)S(1)}, bf16[256,1536]{1,0:T(8,128)(2,1)S(1)}, u32[]{:S(2)}, u32[]{:S(2)}) collective-permute-start(bf16[256,1536]{1,0:T(8,128)(2,1)S(1)} %get-tuple-element.182), channel_id=1, source_target_pairs={{0,64},{32,96},{64,0},{96,32},{1,65},{33,97},{65,1},{97,33},{2,66}... | collective-permute-start | bytes 2359304 | tf_op jit(solution)/shard_map/cond/branch_1_fun/ppermute | solution.py:61
  99.8 1.8 collective-permute-start.5
  107.3 7.3 %copy-start.3 = (bf16[16,32,3200]{2,1,0:T(8,128)(2,1)}, bf16[16,32,3200]{2,1,0:T(8,128)(2,1)S(1)}, u32[]{:S(2)}) copy-start(bf16[16,32,3200]{2,1,0:T(8,128)(2,1)S(1)} %all-to-all-done.2) | copy-start | bytes 9830404
  107.3 49.2 %all-to-all-start.3 = ((bf16[16,32,3072]{2,1,0:T(8,128)(2,1)}), bf16[16,32,3072]{2,1,0:T(8,128)(2,1)}, u32[]{:S(2)}, u32[]{:S(2)}) async-start(bf16[16,32,3072]{2,1,0:T(8,128)(2,1)} %bitcast.18), calls=%async_computation.3 | async-start | bytes 6291456 | tf_op jit(solution)/shard_map/all_to_all | solution.py:41
  120.8 2.6 collective-permute-start.7
  120.9 17.3 %collective-permute-start.6 = (f32[256,1536]{1,0:T(8,128)}, f32[256,1536]{1,0:T(8,128)S(1)}, u32[]{:S(2)}, u32[]{:S(2)}) collective-permute-start(f32[256,1536]{1,0:T(8,128)} %get-tuple-element.75.mine_ref), channel_id=1, source_target_pairs={{0,32},{32,0},{64,96},{96,64},{1,33},{33,1},{65,97},{97,65},{2,34}... | collective-permute-start | bytes 4718600 | tf_op jit(solution)/shard_map/cond/branch_1_fun/ppermute | solution.py:57
  123.4 12.7 %collective-permute-start.8 = (bf16[256,768]{1,0:T(8,128)(2,1)S(1)}, bf16[256,768]{1,0:T(8,128)(2,1)S(1)}, u32[]{:S(2)}, u32[]{:S(2)}) collective-permute-start(bf16[256,768]{1,0:T(8,128)(2,1)S(1)} %get-tuple-element.184), channel_id=1, source_target_pairs={{0,64},{32,96},{64,0},{96,32},{1,65},{33,97},{65,1},{97,33},{2,66}... | collective-permute-start | bytes 1179656 | tf_op jit(solution)/shard_map/cond/branch_1_fun/ppermute | solution.py:61
  136.2 2.4 collective-permute-start.9
  156.5 11.2 %copy-start.4 = (bf16[16,32,3200]{2,1,0:T(8,128)(2,1)S(1)}, bf16[16,32,3200]{2,1,0:T(8,128)(2,1)}, u32[]{:S(2)}) copy-start(bf16[16,32,3200]{2,1,0:T(8,128)(2,1)} %copy-done.3) | copy-start | bytes 9830404
  156.5 49.7 %all-to-all-start.4 = ((bf16[16,32,3072]{2,1,0:T(8,128)(2,1)}), bf16[16,32,3072]{2,1,0:T(8,128)(2,1)}, u32[]{:S(2)}, u32[]{:S(2)}) async-start(bf16[16,32,3072]{2,1,0:T(8,128)(2,1)} %bitcast.20), calls=%async_computation.4 | async-start | bytes 6291456 | tf_op jit(solution)/shard_map/all_to_all | solution.py:41
  183.3 15.7 %collective-permute-start = (bf16[16,128,128]{2,1,0:T(8,128)(2,1)S(1)}, bf16[16,128,128]{2,1,0:T(8,128)(2,1)S(1)}, u32[]{:S(2)}, u32[]{:S(2)}) collective-permute-start(bf16[16,128,128]{2,1,0:T(8,128)(2,1)S(1)} %get-tuple-element.99), channel_id=1, source_target_pairs={{0,16},{1,17},{2,18},{3,19},{4,20},{5,21},{6,22},{7,23},{8,24},{9,... | collective-permute-start | bytes 1572872 | tf_op jit(solution)/shard_map/cond/branch_1_fun/ppermute | solution.py:33
  184.6 1.1 collective-permute-start.1
  186.3 12.1 %collective-permute-start.2 = (s32[1]{0:T(128)}, s32[1]{0:T(128)}, u32[]{:S(2)}, u32[]{:S(2)}) collective-permute-start(s32[1]{0:T(128)} %max.4), channel_id=1, source_target_pairs={{0,64},{32,96},{64,0},{96,32},{1,65},{33,97},{65,1},{97,33},{2,66}... | collective-permute-start | bytes 20 | tf_op jit(solution)/shard_map/cond/branch_1_fun/ppermute | solution.py:61
  206.1 90.0 %all-to-all-start.5 = ((bf16[192,128,128]{2,1,0:T(8,128)(2,1)}), bf16[192,128,128]{2,1,0:T(8,128)(2,1)}, u32[]{:S(2)}, u32[]{:S(2)}) async-start(bf16[192,128,128]{2,1,0:T(8,128)(2,1)} %get-tuple-element.170), calls=%async_computation.5 | async-start | bytes 12582912 | tf_op jit(solution)/shard_map/all_to_all | solution.py:459
  218.4 57.1 %collective-permute-start.11 = (bf16[32,3072]{1,0:T(8,128)(2,1)S(1)}, bf16[32,3072]{1,0:T(8,128)(2,1)S(1)}, u32[]{:S(2)}, u32[]{:S(2)}) collective-permute-start(bf16[32,3072]{1,0:T(8,128)(2,1)S(1)} %pad_maximum_fusion.2), channel_id=1, source_target_pairs={{0,16},{1,17},{2,18},{3,19},{4,20},{5,21},{6,22},{7,23},{8,24},{9,... | collective-permute-start | bytes 589832 | tf_op jit(solution)/shard_map/ppermute | solution.py:33
  (8 other events, 25.8 us)

commit v7 on v5

--- a/solution.py
+++ b/solution.py
@@ -60,9 +60,13 @@
     return lax.ppermute(value, "row", [(0, 2), (1, 3), (2, 0), (3, 1)])
 
 
-def row_sum(keep, send):
+def row_parts(keep, send):
     mine = keep + swap_cores(send)
-    return mine + swap_far(mine.astype(BF)).astype(F32)
+    return mine, swap_far(mine.astype(BF))
+
+
+def row_sum(mine, far):
+    return mine + far.astype(F32)
 
 
 def mask_kernel(bcols, kept_ref, gate_ref, up_ref, down_ref, both_ref, out_ref):
@@ -426,15 +430,17 @@
     dy_all = plane_exchange(late, ncol)
 
     def forward(x_all, both, wd):
-        gate_up = row_sum(*shares(core, x_all, both, rows))
+        gate_up_parts = row_parts(*shares(core, x_all, both, rows))
+        gate_up = row_sum(*gate_up_parts)
         gate, up = gate_up[:, :hid], gate_up[:, hid:]
         hidden = (gate * jax.nn.sigmoid(gate) * up).astype(BF)
-        return gate_up, hidden_stage(core, hidden, swap_cores(hidden), wd)
-
-    def backward(local, dy_all, gate_up, both, wd):
+        return gate_up_parts, hidden_stage(core, hidden, swap_cores(hidden), wd)
+
+    def backward(local, dy_all, gate_up_parts, both, wd):
         tables = index_tables(place, dy_all.reshape(ncol // 2, 2, rows, -1), local, feat, ncol)
+        gate_up = row_sum(*gate_up_parts)
         gate_up_other = swap_cores(gate_up)
-        back = row_sum(*shares(core, dy_all, wd, 0))
+        back = row_sum(*row_parts(*shares(core, dy_all, wd, 0)))
         done = grads_stage(core, (gate_up, gate_up_other), (back, swap_cores(back)), both)
         return done, tables
 
@@ -446,11 +452,11 @@
         main, extra, hand = pack_grads(core, send_at, hand_at, spread, dy_all, grads, hidden, factor, brows, bcols, ncol)
         return insert_blocks(insert_at, across(hand, ncol), main), extra, misfit
 
-    gate_up, (hidden, out_part) = together(go, forward, x_all, both, wd)
-    dy_all, gate_up, out_part = tie(dy_all, gate_up, out_part)
+    gate_up_parts, (hidden, out_part) = together(go, forward, x_all, both, wd)
+    dy_all, gate_up_parts, out_part = tie(dy_all, gate_up_parts, out_part)
     got_out = plane_exchange(out_part, ncol)
     (grads, in_part), (send_at, hand_at, insert_at, shared, direct, misfit) = together(
-        go, backward, local, dy_all, gate_up, both, wd)
+        go, backward, local, dy_all, gate_up_parts, both, wd)
     got_out, in_part = tie(got_out, in_part)
     got_in = plane_exchange(in_part, ncol)
     main, extra, misfit = together(go, blocks, send_at, hand_at, insert_at, misfit, x_all, dy_all, grads, hidden)

time: 302 us -> 304 us (level)
    all_to_all x1, waiting for transfers between devices: 13.5 us -> 21.2 us  [shards(): got = lax.all_to_all(main, 'col', 0, 0, tiled=True)]
    ppermute x4, waiting for transfers between devices: 73 us -> 67.4 us  [across(): lax.ppermute(value, 'col', [(i, (i + ncol // 2) % ncol) for i in range(nc...]
  transfers between devices with their start and end apart: 18 -> 18, of which waited for: 14 -> 13; matrix products, arithmetic and copies ran while one was open for 5% -> 6% of each run, Pallas kernels for 21% -> 21%
where the time goes in v7:
time: 304 us; the launch traced here: 301 us
  waiting for transfers between devices  137 us (45%)
  Pallas kernels  65.9 us (22%)
  starting transfers between devices  62.4 us (21%)
  local copies, waits for them, and re-layouts  17.3 us (6%)
  other arithmetic  14.7 us (5%)
    ppermute x4, waiting for transfers between devices, across(): lax.ppermute(value, 'col', [(i, (i + ncol // 2) % ncol) for i in range(nc...  67.4 us
    ppermute x3, waiting for transfers between devices, swap_far(): return lax.ppermute(value, 'row', [(0, 2), (1, 3), (2, 0), (3, 1)])  31 us
    all_to_all x3, starting transfers between devices, plane_exchange(): lax.all_to_all(value, 'col', 0, 0, axis_index_groups=plane_groups(ncol),...  23.3 us
    all_to_all x1, waiting for transfers between devices, shards(): got = lax.all_to_all(main, 'col', 0, 0, tiled=True)  21.2 us
    pallas_call x2, Pallas kernels, shares(): pl.pallas_call(functools.partial(shares_kernel, reorder), grid=(wide // c...  16 us
    ppermute x3, starting transfers between devices, swap_far(): return lax.ppermute(value, 'row', [(0, 2), (1, 3), (2, 0), (3, 1)])  14.6 us
    pallas_call x1, Pallas kernels, pack_grads(): pl.pallas_call(functools.partial(pack_kernel, factor, brows, bcols, 4), o...  14.5 us
    pallas_call x1, Pallas kernels, mask_weights(): pl.pallas_call(functools.partial(mask_kernel, bcols), grid=(feat // BLOCK...  13.4 us
  transfers between devices with their start and end apart: 18, of which 13 were waited for; matrix products, arithmetic and copies ran while one was open for 6% of the time, Pallas kernels for 21%

profile of v7, /device:TPU:2, one launch (start us, length us, event | category | flops | bytes accessed | tf_op | source)
XLA Modules:
  0.0 300.9 jit_solution(12682311362083255575)
XLA Ops:
  3.6 9.1 %all-to-all-start.1 = ((bf16[32,16,3072]{2,1,0:T(8,128)(2,1)}), bf16[32,16,3072]{2,1,0:T(8,128)(2,1)S(1)}, u32[]{:S(2)}, u32[]{:S(2)}) async-start(bf16[32,16,3072]{2,1,0:T(8,128)(2,1)} %broadcast_in_dim.5), calls=%async_computation.1 | async-start | bytes 6291456 | tf_op jit(solution)/shard_map/all_to_all | solution.py:422
  24.4 13.4 %shard_map.94 = (bf16[3072,1536]{1,0:T(8,128)(2,1)}, bf16[768,3072]{1,0:T(8,128)(2,1)}) custom-call(s32[432]{0:T(512)S(1)} %reshape.93.kept_ref, bf16[3072,768]{1,0:T(8,128)(2,1)S(1)} %copy-done, bf16[3072,768]{1,0:T(8,128)(2,1)S(1)} %copy-done.1, bf16[768,3072]{1,0:T(8,128)(2,1)S(1)} %copy-done.2), custom_call_target="tpu_custom_call" | custom-call | tf_op jit(solution)/shard_map/pallas_call | solution.py:91
  37.7 11.6 %collective-permute-done.10 = bf16[16,3200]{1,0:T(8,128)(2,1)S(1)} collective-permute-done((bf16[16,3200]{1,0:T(8,128)(2,1)S(1)}, bf16[16,3200]{1,0:T(8,128)(2,1)S(1)}, u32[]{:S(2)}, u32[]{:S(2)}) %collective-permute-start.10) | collective-permute-done | bytes 102432 | tf_op jit(solution)/shard_map/ppermute | solution.py:33
  49.4 4.1 %all-to-all-done.1 = bf16[32,16,3072]{2,1,0:T(8,128)(2,1)S(1)} async-done(((bf16[32,16,3072]{2,1,0:T(8,128)(2,1)}), bf16[32,16,3072]{2,1,0:T(8,128)(2,1)S(1)}, u32[]{:S(2)}, u32[]{:S(2)}) %all-to-all-start.1) | async-done | bytes 3145760 | tf_op jit(solution)/shard_map/all_to_all | solution.py:422
  56.2 4.8 %all-to-all-start.2 = ((bf16[16,32,3200]{2,1,0:T(8,128)(2,1)}), bf16[16,32,3200]{2,1,0:T(8,128)(2,1)S(1)}, u32[]{:S(2)}, u32[]{:S(2)}) async-start(bf16[16,32,3200]{2,1,0:T(8,128)(2,1)} %broadcast_in_dim.7), calls=%async_computation.2 | async-start | bytes 6553600 | tf_op jit(solution)/shard_map/all_to_all | solution.py:41
  61.8 45.9 %conditional.4 = (f32[256,1536]{1,0:T(8,128)}, bf16[256,1536]{1,0:T(8,128)(2,1)}, bf16[512,768]{1,0:T(8,128)(2,1)}, bf16[512,3072]{1,0:T(8,128)(2,1)}) conditional(s32[]{:T(128)} %convert_element_type.57, () %tuple.49, (s32[2]{0:T(128)S(1)}, bf16[512,3072]{1,0:T(8,128)(2,1)}, bf16[3072,1536]{1,0:T(8,128)(2,1)}, bf16[768,3072]{1,0:T(8,128)(2,1)}) %tuple.79), branch_computations={%region_4.5_spmd, %region_5.6_spmd} | conditional | flops 2752512 | bytes 36569288 | solution.py:25
  61.8 9.8 %branch_1_fun.8 = (f32[256,1536]{1,0:T(8,128)S(1)}, f32[256,1536]{1,0:T(8,128)S(1)}) custom-call(s32[2]{0:T(128)S(1)} %get-tuple-element.68.core_ref, bf16[512,3072]{1,0:T(8,128)(2,1)} %get-tuple-element.69.rows_ref, bf16[3072,1536]{1,0:T(8,128)(2,1)} %get-tuple-element.70.weight_ref), custom_call_target="tpu_custom_call" | custom-call | tf_op jit(solution)/shard_map/cond/branch_1_fun/pallas_call | solution.py:142
  76.6 3.6 %collective-permute-start.4 = (bf16[256,1536]{1,0:T(8,128)(2,1)S(1)}, bf16[256,1536]{1,0:T(8,128)(2,1)}, u32[]{:S(2)}, u32[]{:S(2)}) collective-permute-start(bf16[256,1536]{1,0:T(8,128)(2,1)S(1)} %get-tuple-element.189), channel_id=1, source_target_pairs={{0,64},{32,96},{64,0},{96,32},{1,65},{33,97},{65,1},{97,33},{2,66}... | collective-permute-start | bytes 2359304 | tf_op jit(solution)/shard_map/cond/branch_1_fun/ppermute | solution.py:60
  80.1 17.9 %collective-permute-done.4 = bf16[256,1536]{1,0:T(8,128)(2,1)} collective-permute-done((bf16[256,1536]{1,0:T(8,128)(2,1)S(1)}, bf16[256,1536]{1,0:T(8,128)(2,1)}, u32[]{:S(2)}, u32[]{:S(2)}) %collective-permute-start.4) | collective-permute-done | bytes 786464 | tf_op jit(solution)/shard_map/cond/branch_1_fun/ppermute | solution.py:60
  101.9 5.7 %branch_1_fun.9 = (bf16[512,768]{1,0:T(8,128)(2,1)}, bf16[512,3072]{1,0:T(8,128)(2,1)}) custom-call(s32[2]{0:T(128)S(1)} %get-tuple-element.68.core_ref, bf16[256,768]{1,0:T(8,128)(2,1)S(1)} %fusion.mine_ref, bf16[256,768]{1,0:T(8,128)(2,1)S(1)} %collective-permute-done.5.other_ref, bf16[768,3072]{1,0:T(8,128)(2,1)S(1)} %bitcast.39), custom_call_target="tpu_custom_call" | custom-call | tf_op jit(solution)/shard_map/cond/branch_1_fun/pallas_call | solution.py:169
  107.6 7.2 %all-to-all-start.3 = ((bf16[16,32,3072]{2,1,0:T(8,128)(2,1)}), bf16[16,32,3072]{2,1,0:T(8,128)(2,1)}, u32[]{:S(2)}, u32[]{:S(2)}) async-start(bf16[16,32,3072]{2,1,0:T(8,128)(2,1)} %bitcast.18), calls=%async_computation.3 | async-start | bytes 6291456 | tf_op jit(solution)/shard_map/all_to_all | solution.py:41
  114.9 34.6 %conditional.5 = (bf16[512,1536]{1,0:T(8,128)(2,1)}, bf16[512,3072]{1,0:T(8,128)(2,1)}, s32[8,256]{1,0:T(8,128)S(1)}, s32[1,128]{1,0:T(1,128)}, s32[1,128]{1,0:T...) conditional(s32[]{:T(128)} %convert_element_type.57, () %tuple.52, ...), branch_computations={%region_6.7_spmd, %region_7.8_spmd} | conditional | flops 1572864 | bytes 35913980 | solution.py:25
  114.9 6.2 %branch_1_fun.10 = (f32[256,768]{1,0:T(8,128)S(1)}, f32[256,768]{1,0:T(8,128)S(1)}) custom-call(s32[2]{0:T(128)S(1)} %get-tuple-element.76.core_ref, bf16[512,3200]{1,0:T(8,128)(2,1)S(1)} %get-tuple-element.79.rows_ref, bf16[768,3072]{1,0:T(8,128)(2,1)} %get-tuple-element.80.weight_ref), custom_call_target="tpu_custom_call" | custom-call | tf_op jit(solution)/shard_map/cond/branch_1_fun/pallas_call | solution.py:142
  127.0 9.3 %collective-permute-done.8 = bf16[256,768]{1,0:T(8,128)(2,1)S(1)} collective-permute-done((bf16[256,768]{1,0:T(8,128)(2,1)S(1)}, bf16[256,768]{1,0:T(8,128)(2,1)S(1)}, u32[]{:S(2)}, u32[]{:S(2)}) %collective-permute-start.8) | collective-permute-done | bytes 393248 | tf_op jit(solution)/shard_map/cond/branch_1_fun/ppermute | solution.py:60
  138.8 10.2 %branch_1_fun.11 = (bf16[512,1536]{1,0:T(8,128)(2,1)}, bf16[512,3072]{1,0:T(8,128)(2,1)}) custom-call(s32[2]{0:T(128)S(1)} %get-tuple-element.76.core_ref, f32[256,1536]{1,0:T(8,128)S(1)} %convert_add_fusion.1.mine_ref, f32[256,1536]{1,0:T(8,128)} %collective-permute-done.6.other_ref, f32[256,768]{1,0:T(8,128)S(1)} %convert_add_fusion.2.back_ref, ...), custom_call_target="tpu_custom_call" | custom-call | tf_op jit(solution)/shard_map/cond/branch_1_fun/pallas_call | solution.py:203
  149.5 7.3 %all-to-all-done.3 = bf16[16,32,3072]{2,1,0:T(8,128)(2,1)} async-done(((bf16[16,32,3072]{2,1,0:T(8,128)(2,1)}), bf16[16,32,3072]{2,1,0:T(8,128)(2,1)}, u32[]{:S(2)}, u32[]{:S(2)}) %all-to-all-start.3) | async-done | bytes 3145760 | tf_op jit(solution)/shard_map/all_to_all | solution.py:41
  156.8 11.2 %all-to-all-start.4 = ((bf16[16,32,3072]{2,1,0:T(8,128)(2,1)}), bf16[16,32,3072]{2,1,0:T(8,128)(2,1)}, u32[]{:S(2)}, u32[]{:S(2)}) async-start(bf16[16,32,3072]{2,1,0:T(8,128)(2,1)} %bitcast.20), calls=%async_computation.4 | async-start | bytes 6291456 | tf_op jit(solution)/shard_map/all_to_all | solution.py:41
  172.5 31.9 %conditional.6 = (bf16[192,128,128]{2,1,0:T(8,128)(2,1)}, bf16[96,128,128]{2,1,0:T(8,128)(2,1)}, s32[]{:T(128)}) conditional(s32[]{:T(128)} %convert_element_type.57, () %tuple.55, (bf16[512,3072]{1,0:T(8,128)(2,1)S(1)}, s32[2]{0:T(128)}, s32[8,256]{1,0:T(8,128)S(1)}, s32[1,128]{1,0:T(1,128)}, bf16[512,3200]{1,0:T(8,128)(2,1)S(1)}, ...), branch_computations={%region_8.9_spmd, %region_9.10_spmd} | conditional | flops 2 | bytes 9437220 | solution.py:25
  172.5 14.5 %branch_1_fun.13 = (bf16[192,128,128]{2,1,0:T(8,128)(2,1)}, bf16[96,128,128]{2,1,0:T(8,128)(2,1)}, bf16[16,128,128]{2,1,0:T(8,128)(2,1)S(1)}) custom-call(s32[2]{0:T(128)} %get-tuple-element.95.core_ref, s32[8,256]{1,0:T(8,128)S(1)} %get-tuple-element.96.where_ref, s32[1,128]{1,0:T(1,128)} %get-tuple-element.97.hand_at_ref, ...), custom_call_target="tpu_custom_call" | custom-call | tf_op jit(solution)/shard_map/cond/branch_1_fun/pallas_call | solution.py:258
  189.8 7.7 %collective-permute-start.2 = (s32[1]{0:T(128)}, s32[1]{0:T(128)}, u32[]{:S(2)}, u32[]{:S(2)}) collective-permute-start(s32[1]{0:T(128)} %max.4), channel_id=1, source_target_pairs={{0,64},{32,96},{64,0},{96,32},{1,65},{33,97},{65,1},{97,33},{2,66}... | collective-permute-start | bytes 20 | tf_op jit(solution)/shard_map/cond/branch_1_fun/ppermute | solution.py:60
  197.5 3.7 %collective-permute-done.2 = s32[1]{0:T(128)} collective-permute-done((s32[1]{0:T(128)}, s32[1]{0:T(128)}, u32[]{:S(2)}, u32[]{:S(2)}) %collective-permute-start.2) | collective-permute-done | bytes 36 | tf_op jit(solution)/shard_map/cond/branch_1_fun/ppermute | solution.py:60
  206.5 8.3 %all-to-all-start.5 = ((bf16[192,128,128]{2,1,0:T(8,128)(2,1)}), bf16[192,128,128]{2,1,0:T(8,128)(2,1)}, u32[]{:S(2)}, u32[]{:S(2)}) async-start(bf16[192,128,128]{2,1,0:T(8,128)(2,1)} %get-tuple-element.177), calls=%async_computation.5 | async-start | bytes 12582912 | tf_op jit(solution)/shard_map/all_to_all | solution.py:465
  218.9 55.8 %collective-permute-done.12 = f32[16,3072]{1,0:T(8,128)S(1)} collective-permute-done((f32[16,3072]{1,0:T(8,128)S(1)}, f32[16,3072]{1,0:T(8,128)S(1)}, u32[]{:S(2)}, u32[]{:S(2)}) %collective-permute-start.12) | collective-permute-done | bytes 196640 | tf_op jit(solution)/shard_map/ppermute | solution.py:33
  275.4 21.2 %all-to-all-done.5 = bf16[192,128,128]{2,1,0:T(8,128)(2,1)} async-done(((bf16[192,128,128]{2,1,0:T(8,128)(2,1)}), bf16[192,128,128]{2,1,0:T(8,128)(2,1)}, u32[]{:S(2)}, u32[]{:S(2)}) %all-to-all-start.5) | async-done | bytes 6291488 | tf_op jit(solution)/shard_map/all_to_all | solution.py:465
  (96 shorter events, 57.5 us)
Async XLA Ops:
  3.6 9.1 %copy-start.14 = (s32[3,24,6]{1,2,0:T(8,128)S(1)}, s32[3,24,6]{1,2,0:T(8,128)}, u32[]{:S(2)}) copy-start(s32[3,24,6]{1,2,0:T(8,128)} %param.23) | copy-start | bytes 5188
  3.6 9.8 %copy-start.10 = (bf16[16,3072]{1,0:T(8,128)(2,1)S(1)}, bf16[16,3072]{1,0:T(8,128)(2,1)}, u32[]{:S(2)}) copy-start(bf16[16,3072]{1,0:T(8,128)(2,1)} %param.18) | copy-start | bytes 294916
  3.6 49.9 %all-to-all-start.1 = ((bf16[32,16,3072]{2,1,0:T(8,128)(2,1)}), bf16[32,16,3072]{2,1,0:T(8,128)(2,1)S(1)}, u32[]{:S(2)}, u32[]{:S(2)}) async-start(bf16[32,16,3072]{2,1,0:T(8,128)(2,1)} %broadcast_in_dim.5), calls=%async_computation.1 | async-start | bytes 6291456 | tf_op jit(solution)/shard_map/all_to_all | solution.py:422
  13.4 35.9 %collective-permute-start.10 = (bf16[16,3200]{1,0:T(8,128)(2,1)S(1)}, bf16[16,3200]{1,0:T(8,128)(2,1)S(1)}, u32[]{:S(2)}, u32[]{:S(2)}) collective-permute-start(bf16[16,3200]{1,0:T(8,128)(2,1)S(1)} %pad_maximum_fusion.2), channel_id=1, source_target_pairs={{0,16},{1,17},{2,18},{3,19},{4,20},{5,21},{6,22},{7,23},{8,24},{9,... | collective-permute-start | bytes 307208 | tf_op jit(solution)/shard_map/ppermute | solution.py:33
  56.2 51.4 %all-to-all-start.2 = ((bf16[16,32,3200]{2,1,0:T(8,128)(2,1)}), bf16[16,32,3200]{2,1,0:T(8,128)(2,1)S(1)}, u32[]{:S(2)}, u32[]{:S(2)}) async-start(bf16[16,32,3200]{2,1,0:T(8,128)(2,1)} %broadcast_in_dim.7), calls=%async_computation.2 | async-start | bytes 6553600 | tf_op jit(solution)/shard_map/all_to_all | solution.py:41
  61.8 53.1 %copy-start.13 = (s32[2]{0:T(128)}, s32[2]{0:T(128)S(1)}, u32[]{:S(2)}) copy-start(s32[2]{0:T(128)S(1)} %pad_add_fusion) | copy-start | bytes 28
  61.8 40.2 %slice-start = ((s8[4718592]{0:T(1024)(128)(4,1)}), s8[4194304]{0:T(1024)(128)(4,1)S(1)}, s32[]{:S(2)}) async-start(s8[4718592]{0:T(1024)(128)(4,1)} %bitcast.38), calls=%async_computation.6 | async-start | bytes 8388608 | tf_op jit(solution)/shard_map/cond
  61.8 40.2 %slice-start.1 = ((s8[4718592]{0:T(1024)(128)(4,1)}), s8[524288]{0:T(1024)(128)(4,1)S(1)}, s32[]{:S(2)}) async-start(s8[4718592]{0:T(1024)(128)(4,1)} %bitcast.38), calls=%async_computation.7 | async-start | bytes 1048576 | tf_op jit(solution)/shard_map/cond
  71.6 3.5 %collective-permute-start.3 = (f32[256,1536]{1,0:T(8,128)S(1)}, f32[256,1536]{1,0:T(8,128)S(1)}, u32[]{:S(2)}, u32[]{:S(2)}) collective-permute-start(f32[256,1536]{1,0:T(8,128)S(1)} %get-tuple-element.72), channel_id=1, source_target_pairs={{0,32},{32,0},{64,96},{96,64},{1,33},{33,1},{65,97},{97,65},{2,34}... | collective-permute-start | bytes 4718600 | tf_op jit(solution)/shard_map/cond/branch_1_fun/ppermute | solution.py:56
  76.6 21.5 %collective-permute-start.4 = (bf16[256,1536]{1,0:T(8,128)(2,1)S(1)}, bf16[256,1536]{1,0:T(8,128)(2,1)}, u32[]{:S(2)}, u32[]{:S(2)}) collective-permute-start(bf16[256,1536]{1,0:T(8,128)(2,1)S(1)} %get-tuple-element.189), channel_id=1, source_target_pairs={{0,64},{32,96},{64,0},{96,32},{1,65},{33,97},{65,1},{97,33},{2,66}... | collective-permute-start | bytes 2359304 | tf_op jit(solution)/shard_map/cond/branch_1_fun/ppermute | solution.py:60
  100.1 1.8 collective-permute-start.5
  107.6 49.2 %all-to-all-start.3 = ((bf16[16,32,3072]{2,1,0:T(8,128)(2,1)}), bf16[16,32,3072]{2,1,0:T(8,128)(2,1)}, u32[]{:S(2)}, u32[]{:S(2)}) async-start(bf16[16,32,3072]{2,1,0:T(8,128)(2,1)} %bitcast.18), calls=%async_computation.3 | async-start | bytes 6291456 | tf_op jit(solution)/shard_map/all_to_all | solution.py:41
  121.1 2.5 collective-permute-start.7
  123.0 15.3 %collective-permute-start.6 = (f32[256,1536]{1,0:T(8,128)S(1)}, f32[256,1536]{1,0:T(8,128)}, u32[]{:S(2)}, u32[]{:S(2)}) collective-permute-start(f32[256,1536]{1,0:T(8,128)S(1)} %convert_add_fusion.1.mine_ref), channel_id=1, source_target_pairs={{0,32},{32,0},{64,96},{96,64},{1,33},{33,1},{65,97},{97,65},{2,34}... | collective-permute-start | bytes 4718600 | tf_op jit(solution)/shard_map/cond/branch_1_fun/ppermute | solution.py:56
  123.7 12.6 %collective-permute-start.8 = (bf16[256,768]{1,0:T(8,128)(2,1)S(1)}, bf16[256,768]{1,0:T(8,128)(2,1)S(1)}, u32[]{:S(2)}, u32[]{:S(2)}) collective-permute-start(bf16[256,768]{1,0:T(8,128)(2,1)S(1)} %get-tuple-element.191), channel_id=1, source_target_pairs={{0,64},{32,96},{64,0},{96,32},{1,65},{33,97},{65,1},{97,33},{2,66}... | collective-permute-start | bytes 1179656 | tf_op jit(solution)/shard_map/cond/branch_1_fun/ppermute | solution.py:60
  136.4 2.4 collective-permute-start.9
  156.8 15.7 %copy-start.7 = (bf16[32,16,3072]{2,1,0:T(8,128)(2,1)S(1)}, bf16[32,16,3072]{2,1,0:T(8,128)(2,1)}, u32[]{:S(2)}) copy-start(bf16[32,16,3072]{2,1,0:T(8,128)(2,1)} %copy-done.6) | copy-start | bytes 9437188
  156.8 49.7 %all-to-all-start.4 = ((bf16[16,32,3072]{2,1,0:T(8,128)(2,1)}), bf16[16,32,3072]{2,1,0:T(8,128)(2,1)}, u32[]{:S(2)}, u32[]{:S(2)}) async-start(bf16[16,32,3072]{2,1,0:T(8,128)(2,1)} %bitcast.20), calls=%async_computation.4 | async-start | bytes 6291456 | tf_op jit(solution)/shard_map/all_to_all | solution.py:41
  171.3 33.0 %collective-permute-start.11 = (f32[16,3072]{1,0:T(8,128)}, f32[16,3072]{1,0:T(8,128)}, u32[]{:S(2)}, u32[]{:S(2)}) collective-permute-start(f32[16,3072]{1,0:T(8,128)} %slice.55), channel_id=1, source_target_pairs={{0,16},{1,17},{2,18},{3,19},{4,20},{5,21},{6,22},{7,23},{8,24},{9,... | collective-permute-start | bytes 589832 | tf_op jit(solution)/shard_map/ppermute | solution.py:33
  187.0 14.8 %collective-permute-start = (bf16[16,128,128]{2,1,0:T(8,128)(2,1)S(1)}, bf16[16,128,128]{2,1,0:T(8,128)(2,1)S(1)}, u32[]{:S(2)}, u32[]{:S(2)}) collective-permute-start(bf16[16,128,128]{2,1,0:T(8,128)(2,1)S(1)} %get-tuple-element.102), channel_id=1, source_target_pairs={{0,16},{1,17},{2,18},{3,19},{4,20},{5,21},{6,22},{7,23},{8,24},{9,... | collective-permute-start | bytes 1572872 | tf_op jit(solution)/shard_map/cond/branch_1_fun/ppermute | solution.py:33
  188.0 1.3 collective-permute-start.1
  189.8 11.4 %collective-permute-start.2 = (s32[1]{0:T(128)}, s32[1]{0:T(128)}, u32[]{:S(2)}, u32[]{:S(2)}) collective-permute-start(s32[1]{0:T(128)} %max.4), channel_id=1, source_target_pairs={{0,64},{32,96},{64,0},{96,32},{1,65},{33,97},{65,1},{97,33},{2,66}... | collective-permute-start | bytes 20 | tf_op jit(solution)/shard_map/cond/branch_1_fun/ppermute | solution.py:60
  206.5 90.0 %all-to-all-start.5 = ((bf16[192,128,128]{2,1,0:T(8,128)(2,1)}), bf16[192,128,128]{2,1,0:T(8,128)(2,1)}, u32[]{:S(2)}, u32[]{:S(2)}) async-start(bf16[192,128,128]{2,1,0:T(8,128)(2,1)} %get-tuple-element.177), calls=%async_computation.5 | async-start | bytes 12582912 | tf_op jit(solution)/shard_map/all_to_all | solution.py:465
  217.3 57.4 %collective-permute-start.12 = (f32[16,3072]{1,0:T(8,128)S(1)}, f32[16,3072]{1,0:T(8,128)S(1)}, u32[]{:S(2)}, u32[]{:S(2)}) collective-permute-start(f32[16,3072]{1,0:T(8,128)S(1)} %slice.57), channel_id=1, source_target_pairs={{0,16},{1,17},{2,18},{3,19},{4,20},{5,21},{6,22},{7,23},{8,24},{9,... | collective-permute-start | bytes 589832 | tf_op jit(solution)/shard_map/ppermute | solution.py:33
  (11 other events, 46.6 us)
